TPU v7x, 32 devices: a whole 2x2x4 slice. The times are simulated.
32 devices in a mesh: parts: 2 (over x), clus: 16 (over z, y, core).
Axes of the slice: x: 2, y: 2, z: 4, core: 2. Of those that a mesh axis runs over, the one named last changes fastest.
Arguments:
- embeddings: float32 [65536, 768], P(('parts', 'clus')), parts along dimension 0, may hold values from -6 to 6
- coverage: bfloat16 [65536], P(('parts', 'clus')), parts along dimension 0, may hold values from 0.0019989014 to 0.059814453
- cluster_ids: int32 [65536, 1], P(('parts', 'clus')), parts along dimension 0, may hold values from 0 to 63, as said below
Outputs:
- gains: float32 [65536], P(('parts', 'clus')), parts along dimension 0
There are 2 independent parts, one for each index of `parts`. A program takes and returns all parts, laid end to end along the dimension named above; each array names one. Nothing has to cross between parts.
Inputs may be any that keep to these rules, and one draw needn't show every extreme that they name: `cluster_ids`: cluster k belongs to owner k // 4. Among the 2048 documents of one device (aligned blocks of 2048 rows) no cluster appears more than 64 times and some cluster exactly 64 times; half of the owners receive exactly 192 of these documents and the other half exactly one third of 192.
All inputs are finite; a program needn't handle non-finite values.
Results may differ from a plain program's by a relative error of at most 0.00045.
Values may be sent and summed in bfloat16 or wider, within the bound.
No kernel may reach another device: no remote copies, remote signals or barrier semaphores. Data moves between devices by JAX's collectives and lax.ppermute only.
A program may use at most 128 MiB of HBM per device.

v0:
```python
import jax
import jax.numpy as jnp
from jax import lax
from jax.sharding import PartitionSpec as P

CL_DEV = 4


def unit_rows(raw):
    sums = jnp.sum(raw * raw, axis=-1, keepdims=True)
    return (raw * lax.rsqrt(sums + 1e-06)).astype(jnp.bfloat16)


def similar_tile(left, right):
    return lax.dot_general(
        left, right, (((1,), (1,)), ((), ())), preferred_element_type=jnp.float32
    )


def padded_gains(members, cover):
    similar = similar_tile(members, members)
    return jnp.sum(jnp.maximum(similar - cover[:, None], 0.0), axis=0)


def body(embeddings, coverage, cluster_ids):
    devices = lax.axis_size("clus")
    rows_here = embeddings.shape[0]
    width = embeddings.shape[1]
    clusters = CL_DEV * devices
    cap = 2 * rows_here // clusters
    slots = clusters * cap
    cluster = cluster_ids[:, 0]
    onehot = (cluster[:, None] == jnp.arange(clusters, dtype=jnp.int32)[None, :]).astype(jnp.int32)
    rank = jnp.sum(jnp.cumsum(onehot, axis=0) * onehot, axis=1) - 1
    slot_index = (cluster % CL_DEV * devices + cluster // CL_DEV) * cap + rank
    buffer = (
        jnp.zeros((slots, width), jnp.float32)
        .at[slot_index]
        .set(embeddings)
        .reshape(CL_DEV, devices, cap, width)
    )
    cover_buffer = (
        jnp.zeros((slots,), jnp.float32)
        .at[slot_index]
        .set(coverage.astype(jnp.float32))
        .reshape(CL_DEV, devices, cap)
    )
    members = unit_rows(lax.all_to_all(buffer, "clus", split_axis=1, concat_axis=1, tiled=True))
    items = members.shape[0]
    flat_rows = members.reshape(items, -1, width)
    flat_cover = lax.all_to_all(
        cover_buffer, "clus", split_axis=1, concat_axis=1, tiled=True
    ).reshape(items, -1)
    result = lax.map(lambda both: padded_gains(both[0], both[1]), (flat_rows, flat_cover))
    gains = result.reshape(items, members.shape[1], members.shape[2])
    returned = lax.all_to_all(gains, "clus", split_axis=1, concat_axis=1, tiled=True)
    return returned.reshape(-1)[slot_index]


def solution(mesh):
    placed = (P(("parts", "clus"), None), P(("parts", "clus")), P(("parts", "clus"), None))
    return jax.shard_map(
        body, mesh=mesh, in_specs=placed, out_specs=P(("parts", "clus")), check_vma=False
    )
```

profile of v0, /device:TPU:0, one launch (start us, length us, event | category | flops | bytes accessed | tf_op | source)
XLA Modules:
  0.0 405.1 jit_solution(6079742635799782421)
XLA Ops:
  0.0 0.7 fusion.8
  0.7 18.1 %reduce-window.6 = s32[64,16,128]{2,1,0:T(8,128)S(1)} reduce-window(s32[64,16,128]{2,1,0:T(8,128)S(1)} %fusion.8, s32[]{:T(128)} %constant.52.clone.1), window={size=1x1x128 pad=0_0x0_0x127_0}, to_apply=%region_0.0 | reduce-window | flops 16646144 | bytes 1048580 | tf_op jit(solution)/shard_map/reduce-window
  18.9 0.2 slice.10
  19.1 0.4 copy.35
  19.5 0.2 reduce-window.9
  19.7 0.2 broadcast_add_fusion
  19.9 0.9 fusion.7
  20.8 0.8 compare_select_fusion
  21.6 0.7 convert_element_type.13
  22.3 8.1 %scatter_custom_fusion.1 = f32[4096]{0:T(1024)S(1)} fusion(s32[2048]{0:T(1024)S(1)} %bitcast.54, f32[2048]{0:T(1024)S(1)} %convert_element_type.13, f32[]{:T(128)} %constant.53.clone.1), kind=kCustom, calls=%fused_computation.30 | custom fusion | bytes 16388 | tf_op jit(solution)/shard_map/scatter | solution.py:45
  30.4 0.1 reshape.54
  30.5 0.7 reshape.86
  31.1 7.4 %all-to-all-start.1 = ((f32[16,1,256]{2,1,0:T(1,128)}), f32[16,1,256]{2,1,0:T(1,128)S(1)}, u32[]{:S(2)}, u32[]{:S(2)}) async-start(f32[16,1,256]{2,1,0:T(1,128)} %reshape.86), calls=%async_computation.1 | async-start | bytes 32768 | tf_op jit(solution)/shard_map/all_to_all | solution.py:51
  38.5 15.1 %scatter_custom_fusion = f32[4096,768]{1,0:T(8,128)} fusion(s32[2048]{0:T(1024)S(1)} %bitcast.55, f32[2048,768]{1,0:T(8,128)} %param.5, f32[]{:T(128)} %constant.53.clone.1), kind=kCustom, calls=%fused_computation.11 | custom fusion | bytes 12583424 | tf_op jit(solution)/shard_map/scatter | solution.py:39
  53.6 10.6 %copy.28 = f32[4,16,64,768]{3,2,0,1:T(8,128)} copy(f32[4,16,64,768]{3,2,1,0:T(8,128)} %bitcast.41) | data formatting | bytes 25165824 | tf_op jit(solution)/shard_map/reshape | solution.py:40
  64.2 0.0 all-to-all-done.1
  64.2 6.1 %all-to-all-start = ((f32[4,16,64,768]{3,2,0,1:T(8,128)}), f32[4,16,64,768]{3,2,0,1:T(8,128)}, u32[]{:S(2)}, u32[]{:S(2)}) async-start(f32[4,16,64,768]{3,2,0,1:T(8,128)} %copy.28), calls=%async_computation | async-start | bytes 25165824 | tf_op jit(solution)/shard_map/all_to_all | solution.py:48
  70.3 0.5 broadcast.83
  70.8 0.7 reduce
  71.5 0.1 reshape.87
  71.6 0.1 reshape.55
  71.7 222.4 %all-to-all-done = f32[4,16,64,768]{3,2,0,1:T(8,128)} async-done(((f32[4,16,64,768]{3,2,0,1:T(8,128)}), f32[4,16,64,768]{3,2,0,1:T(8,128)}, u32[]{:S(2)}, u32[]{:S(2)}) %all-to-all-start) | async-done | bytes 12582944 | tf_op jit(solution)/shard_map/all_to_all | solution.py:48
  294.0 5.5 %multiply_reduce_fusion = f32[4,16,64]{2,0,1:T(4,128)S(1)} fusion(f32[4,16,64,768]{3,2,0,1:T(8,128)} %all-to-all-done), kind=kLoop, calls=%fused_computation.10 | loop fusion | flops 6287360 | bytes 12599296 | tf_op jit(solution)/shard_map/reduce_sum | solution.py:10
  299.5 8.1 %fusion.3 = bf16[4,16,64,768]{3,2,1,0:T(8,128)(2,1)} fusion(f32[4,16,64,768]{3,2,0,1:T(8,128)} %all-to-all-done, f32[4,16,64]{2,1,0:T(8,128)S(1)} %fusion.9), kind=kLoop, calls=%fused_computation.9 | loop fusion | flops 6291456 | bytes 18890752 | tf_op jit(solution)/shard_map/convert_element_type | solution.py:11
  307.6 15.5 %while.10 = (s32[]{:T(128)}, f32[4,1024]{1,0:T(4,128)S(1)}, bf16[4,1024,768]{2,1,0:T(8,128)(2,1)}, f32[4,1024]{1,0:T(4,128)S(1)}, s32[]{:T(128)}, /*index=5*/s32[]{:T(128)}) while((s32[]{:T(128)}, f32[4,1024]{1,0:T(4,128)S(1)}, bf16[4,1024,768]{2,1,0:T(8,128)(2,1)}, f32[4,1024]{1,0:T(4,128)S(1)}, s32[]{:T(128)}, /*index=5*/s32[]{:T(128)}) %tuple.21), condition=%wide.region_8.9_spmd, body=%wide.region_6.8_spmd.sunk | while | flops 1613757440 | bytes 1598029 | solution.py:54
  307.7 3.7 maximum_reduce_fusion.2
  311.4 0.1 dynamic_update_slice.5
  311.5 3.7 maximum_reduce_fusion.2
  315.3 0.1 dynamic_update_slice.5
  315.4 3.7 maximum_reduce_fusion.2
  319.1 0.1 dynamic_update_slice.5
  319.2 3.8 maximum_reduce_fusion.2
  323.0 0.1 dynamic_update_slice.5
  323.1 0.1 reshape.56
  323.2 0.7 reshape.88
  323.9 53.3 %all-to-all-start.2 = ((f32[16,1,256]{2,1,0:T(1,128)}), f32[16,1,256]{2,1,0:T(1,128)S(1)}, u32[]{:S(2)}, u32[]{:S(2)}) async-start(f32[16,1,256]{2,1,0:T(1,128)} %reshape.88), calls=%async_computation.2 | async-start | bytes 32768 | tf_op jit(solution)/shard_map/all_to_all | solution.py:56
  377.3 6.5 %all-to-all-done.2 = f32[16,1,256]{2,1,0:T(1,128)S(1)} async-done(((f32[16,1,256]{2,1,0:T(1,128)}), f32[16,1,256]{2,1,0:T(1,128)S(1)}, u32[]{:S(2)}, u32[]{:S(2)}) %all-to-all-start.2) | async-done | bytes 16416 | tf_op jit(solution)/shard_map/all_to_all | solution.py:56
  383.7 0.7 reduce.1
  384.4 0.1 reshape.89
  384.5 0.1 reshape.57
  384.6 20.5 %gather_fusion = f32[2048]{0:T(1024)} fusion(f32[4096]{0:T(1024)S(1)} %reshape.57, s32[2048]{0:T(1024)S(1)} %broadcast_clamp_fusion), kind=kCustom, calls=%fused_computation | custom fusion | bytes 24576 | tf_op jit(solution)/shard_map/gather | solution.py:57
  (12 shorter events, 0.1 us)
Async XLA Ops:
  31.1 33.1 %all-to-all-start.1 = ((f32[16,1,256]{2,1,0:T(1,128)}), f32[16,1,256]{2,1,0:T(1,128)S(1)}, u32[]{:S(2)}, u32[]{:S(2)}) async-start(f32[16,1,256]{2,1,0:T(1,128)} %reshape.86), calls=%async_computation.1 | async-start | bytes 32768 | tf_op jit(solution)/shard_map/all_to_all | solution.py:51
  64.2 229.8 %all-to-all-start = ((f32[4,16,64,768]{3,2,0,1:T(8,128)}), f32[4,16,64,768]{3,2,0,1:T(8,128)}, u32[]{:S(2)}, u32[]{:S(2)}) async-start(f32[4,16,64,768]{3,2,0,1:T(8,128)} %copy.28), calls=%async_computation | async-start | bytes 25165824 | tf_op jit(solution)/shard_map/all_to_all | solution.py:48
  323.9 59.8 %all-to-all-start.2 = ((f32[16,1,256]{2,1,0:T(1,128)}), f32[16,1,256]{2,1,0:T(1,128)S(1)}, u32[]{:S(2)}, u32[]{:S(2)}) async-start(f32[16,1,256]{2,1,0:T(1,128)} %reshape.88), calls=%async_computation.2 | async-start | bytes 32768 | tf_op jit(solution)/shard_map/all_to_all | solution.py:56
where the time goes:
time: 406 us; the launch traced here: 405 us
  waiting for transfers between devices  229 us (56%)
  starting transfers between devices  66.8 us (16%)
  local copies, waits for them, and re-layouts  57.7 us (14%)
  other arithmetic  36.6 us (9%)
  matrix products  15 us (4%)
    all_to_all x1, waiting for transfers between devices, body(): lax.all_to_all(buffer, 'clus', split_axis=1, concat_axis=1, tiled=True)  222 us
    all_to_all x1, starting transfers between devices, body(): lax.all_to_all(gains, 'clus', split_axis=1, concat_axis=1, tiled=True)  53.3 us
    gather x1, local copies, waits for them, and re-layouts, body(): return returned.reshape(-1)[slot_index]  20.5 us
    another operation x3, other arithmetic  18.5 us
    scatter x1, local copies, waits for them, and re-layouts, body(): buffer = jnp.zeros((slots, width), jnp.float32).at[slot_index].set(embedd...  15.1 us
    dot_general x4, matrix products, similar_tile(): lax.dot_general(left, right, (((1,), (1,)), ((), ())), preferred_element_...  15 us
    reshape x1, local copies, waits for them, and re-layouts, body(): buffer = jnp.zeros((slots, width), jnp.float32).at[slot_index].set(embedd...  10.6 us
  transfers between devices with their start and end apart: 3, of which 2 were waited for; matrix products, arithmetic and copies ran while one was open for 7% of the time, Pallas kernels for 0%

commit v1 on v0

v1 whole, which is shorter than its diff:
```python
import jax
import jax.numpy as jnp
from jax import lax
from jax.experimental import pallas as pl
from jax.experimental.pallas import tpu as pltpu
from jax.sharding import PartitionSpec as P

CL_DEV = 4
PARTS = 3
VMEM = 56 * 1024 * 1024

NN = (((1,), (0,)), ((), ()))
NT = (((1,), (1,)), ((), ()))


def dot(left, right, dims, precision=None):
    return lax.dot_general(
        left, right, dims, precision=precision, preferred_element_type=jnp.float32
    )


def lanes(n):
    return -(-n // 128) * 128


def hot(values, count, first=0):
    index = lax.broadcasted_iota(jnp.int32, (count, values.shape[1]), 0) + first
    return jnp.where(index == values, 1.0, 0.0).astype(jnp.bfloat16)


def place(ids, devices, cap):
    rows = ids.shape[1]
    clusters = CL_DEV * devices
    step = 256
    onehot = hot(ids, clusters)
    before = (
        lax.broadcasted_iota(jnp.int32, (step, step), 0)
        < lax.broadcasted_iota(jnp.int32, (step, step), 1)
    )
    before = jnp.where(before, 1.0, 0.0).astype(jnp.bfloat16)
    count = jnp.zeros((clusters, 1), jnp.float32)
    ranks = []
    for start in range(0, rows, step):
        piece = onehot[:, start : start + step]
        wide = piece.astype(jnp.float32)
        ahead = dot(piece, before, NN) + count
        ranks.append(ahead)
        count = count + jnp.sum(wide, axis=1, keepdims=True)
    k = lax.broadcasted_iota(jnp.int32, (clusters, clusters), 0)
    m = lax.broadcasted_iota(jnp.int32, (clusters, clusters), 1)
    j = k % CL_DEV
    plus = (j == 1) & (m == k - 1)
    minus = ((j == 2) & ((m == k) | (m == k + 1))) | ((j == 3) & (m == k))
    mix = (jnp.where(plus, 1.0, 0.0) - jnp.where(minus, 1.0, 0.0)).astype(jnp.bfloat16)
    wide_count = jnp.broadcast_to(count, (clusters, 128)).astype(jnp.bfloat16)
    base = dot(mix, wide_count, NN)[:, :1]
    jcol = lax.broadcasted_iota(jnp.int32, (clusters, 1), 0) % CL_DEV
    base = base + jnp.where(jcol >= 2, float(PARTS * cap), 0.0)
    position = []
    for i, start in enumerate(range(0, rows, step)):
        wide = onehot[:, start : start + step].astype(jnp.float32)
        position.append(jnp.sum(wide * (ranks[i] + base), axis=0, keepdims=True))
    position = jnp.concatenate(position, axis=1).astype(jnp.int32)
    return ids // CL_DEV, position


def first_kernel(devices, cap, block):
    def kernel(ids_ref, cover_ref, emb_ref, unit_ref, where_ref, meta_ref, out_ref, acc_ref):
        step = pl.program_id(0)
        last = pl.num_programs(0) - 1
        slots = devices * cap
        seg = lanes(PARTS * cap)

        @pl.when(step == 0)
        def _():
            ids = ids_ref[...]
            owner, position = place(ids, devices, cap)
            chunk = position // cap
            slot = chunk * slots + owner * cap + position - chunk * cap
            where_ref[0:1, :] = slot
            where_ref[1:2, :] = owner
            where_ref[2:3, :] = position
            own = hot(owner, devices)
            there = hot(position, seg)
            cover = own * cover_ref[...].astype(jnp.bfloat16)
            which = own * (ids % CL_DEV).astype(jnp.float32).astype(jnp.bfloat16)
            meta_ref[:, 0, :seg] = dot(cover, there, NT)
            meta_ref[:, 0, seg:] = dot(which, there, NT)
            acc_ref[...] = jnp.zeros_like(acc_ref)

        raw = emb_ref[...]
        sums = jnp.sum(raw * raw, axis=-1, keepdims=True)
        unit = (raw * lax.rsqrt(sums + 1e-06)).astype(jnp.bfloat16)
        begin = pl.multiple_of(step * block, block)
        unit_ref[pl.ds(begin, block), :] = unit
        slot = where_ref[0:1, pl.ds(begin, block)]
        acc_ref[...] += dot(hot(slot, slots), unit, NN)

        @pl.when(step == last)
        def _():
            out_ref[...] = acc_ref[...].astype(jnp.bfloat16)

    return kernel


def dispatch_kernel(slots, part, tile):
    def kernel(where_ref, unit_ref, out_ref):
        begin = pl.program_id(0) * tile
        pick = hot(where_ref[0:1, :], tile, part * slots + begin)
        out_ref[...] = dot(pick, unit_ref[...], NN).astype(jnp.bfloat16)

    return kernel


def column(row):
    return jnp.transpose(jnp.broadcast_to(row, (128, row.shape[1])))


def wide(col, n):
    return jnp.concatenate([col] * (n // 128), axis=1)


def pair(left_ref, right_ref, left_meta, right_meta, tile, both):
    rows = left_ref.shape[0]
    cols = right_ref.shape[0]
    cover_left = column(left_meta[0:1, :])
    which_left = column(left_meta[1:2, :])
    right = right_ref[...]
    down = jnp.zeros((8, cols), jnp.float32)
    across = []
    for start in range(0, rows, tile):
        similar = dot(left_ref[start : start + tile, :], right, NT)
        same = wide(which_left[start : start + tile], cols) == right_meta[1:2, :]
        similar = jnp.where(same, similar, -1e30)
        gain = jnp.maximum(similar - wide(cover_left[start : start + tile], cols), 0.0)
        down = down + jnp.sum(gain.reshape(tile // 8, 8, cols), axis=0)
        if both:
            other = jnp.maximum(similar - right_meta[0:1, :], 0.0)
            part = other[:, :128]
            for lane in range(128, cols, 128):
                part = part + other[:, lane : lane + 128]
            across.append(part)
    down = jnp.sum(down, axis=0, keepdims=True)
    if not both:
        return down, None
    across = jnp.concatenate(across, axis=0)
    across = jnp.sum(jnp.transpose(across), axis=0, keepdims=True)
    return down, across


def gram_first(tile):
    def kernel(meta_ref, a_ref, out_ref):
        down, _ = pair(a_ref, a_ref, meta_ref, meta_ref, tile, False)
        out_ref[...] = down

    return kernel


def gram_second(tile):
    def kernel(ma_ref, mb_ref, a_ref, b_ref, ga_ref, outa_ref, outb_ref):
        down, across = pair(a_ref, b_ref, ma_ref, mb_ref, tile, True)
        own, _ = pair(b_ref, b_ref, mb_ref, mb_ref, tile, False)
        outa_ref[...] = ga_ref[...] + across
        outb_ref[...] = down + own

    return kernel


def gram_third(tile, devices, cap):
    def kernel(mb_ref, mc_ref, b_ref, c_ref, ga_ref, gb_ref, out_ref):
        down, across = pair(b_ref, c_ref, mb_ref, mc_ref, tile, True)
        own, _ = pair(c_ref, c_ref, mc_ref, mc_ref, tile, False)
        all_gains = [ga_ref[...], gb_ref[...] + across, down + own]
        fill = jnp.zeros((1, out_ref.shape[2] - PARTS * cap), jnp.float32)
        for o in range(devices):
            parts = [g[:, o * cap : (o + 1) * cap] for g in all_gains]
            if fill.shape[1]:
                parts.append(fill)
            out_ref[o] = jnp.concatenate(parts, axis=1)

    return kernel


def last_kernel(devices):
    def kernel(where_ref, gains_ref, out_ref):
        gains = gains_ref[:, 0, :]
        high = gains.astype(jnp.bfloat16)
        rest = gains - high.astype(jnp.float32)
        mid = rest.astype(jnp.bfloat16)
        low = (rest - mid.astype(jnp.float32)).astype(jnp.bfloat16)
        there = hot(where_ref[2:3, :], gains.shape[1])
        found = dot(high, there, NN) + dot(mid, there, NN) + dot(low, there, NN)
        index = lax.broadcasted_iota(jnp.int32, found.shape, 0)
        mine = jnp.where(index == where_ref[1:2, :], found, 0.0)
        out_ref[...] = jnp.sum(mine, axis=0, keepdims=True)

    return kernel


def call(kernel, outs, cost, name, **extra):
    return pl.pallas_call(
        kernel,
        out_shape=outs,
        compiler_params=pltpu.CompilerParams(vmem_limit_bytes=VMEM),
        cost_estimate=pl.CostEstimate(flops=cost[0], bytes_accessed=cost[1], transcendentals=0),
        name=name,
        **extra,
    )


def body(embeddings, coverage, cluster_ids):
    devices = lax.axis_size("clus")
    rows, width = embeddings.shape
    clusters = CL_DEV * devices
    cap = 2 * rows // clusters
    slots = devices * cap
    seg = lanes(PARTS * cap)
    f32, bf16 = jnp.float32, jnp.bfloat16
    S = jax.ShapeDtypeStruct
    ids = cluster_ids.reshape(1, rows)
    cover = coverage.astype(f32).reshape(1, rows)
    block = rows // 4

    unit, where, meta, chunk_a = call(
        first_kernel(devices, cap, block),
        [S((rows, width), bf16), S((3, rows), jnp.int32), S((devices, 1, 2 * seg), f32), S((slots, width), bf16)],
        (2 * slots * rows * width, 4 * rows * width),
        "first",
        grid=(rows // block,),
        in_specs=[
            pl.BlockSpec((1, rows), lambda i: (0, 0)),
            pl.BlockSpec((1, rows), lambda i: (0, 0)),
            pl.BlockSpec((block, width), lambda i: (i, 0)),
        ],
        out_specs=[
            pl.BlockSpec((rows, width), lambda i: (0, 0)),
            pl.BlockSpec((3, rows), lambda i: (0, 0)),
            pl.BlockSpec((devices, 1, 2 * seg), lambda i: (0, 0, 0)),
            pl.BlockSpec((slots, width), lambda i: (0, 0)),
        ],
        scratch_shapes=[pltpu.VMEM((slots, width), f32)],
    )(ids, cover, embeddings)

    def swap(chunk):
        return lax.all_to_all(
            chunk.reshape(devices, cap, width), "clus", 0, 0, tiled=True
        ).reshape(slots, width)

    def dispatch(part):
        tile = slots // 2
        return call(
            dispatch_kernel(slots, part, tile),
            S((slots, width), bf16),
            (2 * slots * rows * width, 2 * rows * width),
            "dispatch",
            grid=(slots // tile,),
            in_specs=[
                pl.BlockSpec((3, rows), lambda i: (0, 0)),
                pl.BlockSpec((rows, width), lambda i: (0, 0)),
            ],
            out_specs=pl.BlockSpec((tile, width), lambda i: (i, 0)),
        )(where, unit)

    got_a = swap(chunk_a)
    met = lax.all_to_all(meta, "clus", 0, 0, tiled=True)
    got_b = swap(dispatch(1))
    got_c = swap(dispatch(2))

    met = met.reshape(devices, 2, seg)[:, :, : PARTS * cap].reshape(devices, 2, PARTS, cap)
    met = met.transpose(2, 1, 0, 3).reshape(PARTS, 2, slots)
    ma, mb, mc = met[0], met[1], met[2]

    square = 2 * slots * slots * width
    tile = slots // 4
    gain_a = call(gram_first(tile), S((1, slots), f32), (square, 2 * slots * width), "gram_a")(ma, got_a)
    gain_a, gain_b = call(
        gram_second(tile), [S((1, slots), f32)] * 2, (2 * square, 4 * slots * width), "gram_b"
    )(ma, mb, got_a, got_b, gain_a)
    gains = call(
        gram_third(tile, devices, cap), S((devices, 1, seg), f32), (2 * square, 4 * slots * width), "gram_c"
    )(mb, mc, got_b, got_c, gain_a, gain_b)
    back = lax.all_to_all(gains, "clus", 0, 0, tiled=True)
    out = call(last_kernel(devices), S((1, rows), f32), (2 * rows * seg * 48, 8 * rows), "last")(where, back)
    return out.reshape(rows)


def solution(mesh):
    placed = (P(("parts", "clus"), None), P(("parts", "clus")), P(("parts", "clus"), None))
    return jax.shard_map(
        body, mesh=mesh, in_specs=placed, out_specs=P(("parts", "clus")), check_vma=False
    )
```

time: 406 us -> 171 us (0.42)
  waiting for transfers between devices: 229 us -> 70.5 us
  local copies, waits for them, and re-layouts: 57.7 us -> 5.75 us
  starting transfers between devices: 66.8 us -> 21.9 us
  Pallas kernels: 0 us -> 41.3 us
  other arithmetic: 36.6 us -> 1.36 us
  blocking collectives: 0 us -> 29.7 us
  matrix products: 15 us -> 0 us
    all_to_all x3, waiting for transfers between devices: 229 us -> 70.5 us  [swap(): lax.all_to_all(chunk.reshape(devices, cap, width), 'clus', 0, 0, tiled=True)]
    all_to_all x3, starting transfers between devices: 66.8 us -> 21.9 us  [swap(): lax.all_to_all(chunk.reshape(devices, cap, width), 'clus', 0, 0, tiled=True)]
    pallas_call x0 -> x7, Pallas kernels: none -> 41.3 us  [the longest x2 12.8 us: dispatch(): call(dispatch_kernel(slots, part, tile), S((slots, width), bf16), (2 * sl...]
    all_to_all x0 -> x2, blocking collectives: none -> 29.7 us  [the longest x1 15.7 us: body(): back = lax.all_to_all(gains, 'clus', 0, 0, tiled=True)]
    scatter x2 -> x0, local copies, waits for them, and re-layouts: 23.1 us -> none  [the longest x1 15.1 us: body(): buffer = jnp.zeros((slots, width), jnp.float32).at[slot_index].set(embedd...]
    gather x1 -> x0, local copies, waits for them, and re-layouts: 20.5 us -> none  [body(): return returned.reshape(-1)[slot_index]]
    another operation x3 -> x0, other arithmetic: 18.5 us -> none
    dot_general x4 -> x0, matrix products: 15 us -> none  [similar_tile(): lax.dot_general(left, right, (((1,), (1,)), ((), ())), preferred_element_...]
  transfers between devices with their start and end apart: 3 -> 3, of which waited for: 2 -> 3; matrix products, arithmetic and copies ran while one was open for 7% -> 1% of each run, Pallas kernels for 0% -> 13%
where the time goes in v1:
time: 171 us
  waiting for transfers between devices  70.5 us (41%)
  Pallas kernels  41.3 us (24%)
  blocking collectives  29.7 us (17%)
  starting transfers between devices  21.9 us (13%)
  local copies, waits for them, and re-layouts  5.75 us (3%)
    all_to_all x3, waiting for transfers between devices, swap(): lax.all_to_all(chunk.reshape(devices, cap, width), 'clus', 0, 0, tiled=True)  70.5 us
    all_to_all x3, starting transfers between devices, swap(): lax.all_to_all(chunk.reshape(devices, cap, width), 'clus', 0, 0, tiled=True)  21.9 us
    all_to_all x1, blocking collectives, body(): back = lax.all_to_all(gains, 'clus', 0, 0, tiled=True)  15.7 us
    all_to_all x1, blocking collectives, body(): met = lax.all_to_all(meta, 'clus', 0, 0, tiled=True)  14 us
    pallas_call x2, Pallas kernels, dispatch(): call(dispatch_kernel(slots, part, tile), S((slots, width), bf16), (2 * sl...  12.8 us
    pallas_call x1, Pallas kernels, body(): call(first_kernel(devices, cap, block), [S((rows, width), bf16), S((3, ro...  10.1 us
    pallas_call x1, Pallas kernels, body(): call(gram_third(tile, devices, cap), S((devices, 1, seg), f32), (2 * squa...  6.27 us
    pallas_call x1, Pallas kernels, body(): call(gram_second(tile), [S((1, slots), f32)] * 2, (2 * square, 4 * slots...  6.19 us
  transfers between devices with their start and end apart: 3, of which 3 were waited for; matrix products, arithmetic and copies ran while one was open for 1% of the time, Pallas kernels for 13%

profile of v1, /device:TPU:0, one launch (start us, length us, event | category | flops | bytes accessed | tf_op | source)
XLA Modules:
  0.0 170.6 jit_solution(13257849224408078285)
XLA Ops:
  0.0 1.3 reshape.54
  1.3 10.1 %first.1 = (bf16[2048,768]{1,0:T(8,128)(2,1)}, s32[3,2048]{1,0:T(4,128)}, f32[16,1,512]{2,1,0:T(1,128)}, bf16[1024,768]{1,0:T(8,128)(2,1)}) custom-call(s32[1,2048]{1,0:T(1,128)} %bitcast.24, f32[1,2048]{1,0:T(1,128)} %bitcast.23, f32[2048,768]{1,0:T(8,128)} %emb_ref.1), custom_call_target="tpu_custom_call" | custom-call | flops 3221225472 | bytes 6291456 | tf_op jit(solution)/shard_map/first/pallas_call | solution.py:224
  11.4 14.0 %all_to_all.25 = f32[16,1,512]{2,1,0:T(1,128)S(1)} all-to-all(f32[16,1,512]{2,1,0:T(1,128)} %get-tuple-element.12), channel_id=1, replica_groups=mesh['parts'=2,'clus'=16] {'clus'}, dimensions={0} | all-to-all | bytes 65536 | tf_op jit(solution)/shard_map/all_to_all | solution.py:265
  25.4 3.7 %all-to-all-start.3 = ((bf16[16,64,768]{2,1,0:T(8,128)(2,1)}), bf16[16,64,768]{2,1,0:T(8,128)(2,1)S(1)}, u32[]{:S(2)}, u32[]{:S(2)}) async-start(bf16[16,64,768]{2,1,0:T(8,128)(2,1)} %bitcast.19), calls=%async_computation.3 | async-start | bytes 3145728 | tf_op jit(solution)/shard_map/all_to_all | solution.py:245
  29.1 6.4 %dispatch.2 = bf16[1024,768]{1,0:T(8,128)(2,1)} custom-call(s32[3,2048]{1,0:T(4,128)} %get-tuple-element.11.where_ref, bf16[2048,768]{1,0:T(8,128)(2,1)} %get-tuple-element.13.unit_ref), custom_call_target="tpu_custom_call" | custom-call | flops 3221225472 | bytes 3145728 | tf_op jit(solution)/shard_map/dispatch/pallas_call | solution.py:251
  35.5 25.5 %all-to-all-done.3 = bf16[16,64,768]{2,1,0:T(8,128)(2,1)S(1)} async-done(((bf16[16,64,768]{2,1,0:T(8,128)(2,1)}), bf16[16,64,768]{2,1,0:T(8,128)(2,1)S(1)}, u32[]{:S(2)}, u32[]{:S(2)}) %all-to-all-start.3) | async-done | bytes 1572896 | tf_op jit(solution)/shard_map/all_to_all | solution.py:245
  61.0 0.0 copy-start
  61.0 1.2 copy-done
  62.2 9.1 %all-to-all-start.1 = ((bf16[16,64,768]{2,1,0:T(8,128)(2,1)}), bf16[16,64,768]{2,1,0:T(8,128)(2,1)S(1)}, u32[]{:S(2)}, u32[]{:S(2)}) async-start(bf16[16,64,768]{2,1,0:T(8,128)(2,1)} %bitcast.20), calls=%async_computation.1 | async-start | bytes 3145728 | tf_op jit(solution)/shard_map/all_to_all | solution.py:245
  71.3 6.4 %dispatch.3 = bf16[1024,768]{1,0:T(8,128)(2,1)} custom-call(s32[3,2048]{1,0:T(4,128)} %get-tuple-element.11.where_ref, bf16[2048,768]{1,0:T(8,128)(2,1)} %get-tuple-element.13.unit_ref), custom_call_target="tpu_custom_call" | custom-call | flops 3221225472 | bytes 3145728 | tf_op jit(solution)/shard_map/dispatch/pallas_call | solution.py:251
  77.7 25.5 %all-to-all-done.1 = bf16[16,64,768]{2,1,0:T(8,128)(2,1)S(1)} async-done(((bf16[16,64,768]{2,1,0:T(8,128)(2,1)}), bf16[16,64,768]{2,1,0:T(8,128)(2,1)S(1)}, u32[]{:S(2)}, u32[]{:S(2)}) %all-to-all-start.1) | async-done | bytes 1572896 | tf_op jit(solution)/shard_map/all_to_all | solution.py:245
  103.2 0.0 copy-start.1
  103.2 1.2 copy-done.1
  104.4 9.1 %all-to-all-start.2 = ((bf16[16,64,768]{2,1,0:T(8,128)(2,1)}), bf16[16,64,768]{2,1,0:T(8,128)(2,1)S(1)}, u32[]{:S(2)}, u32[]{:S(2)}) async-start(bf16[16,64,768]{2,1,0:T(8,128)(2,1)} %bitcast.18), calls=%async_computation.2 | async-start | bytes 3145728 | tf_op jit(solution)/shard_map/all_to_all | solution.py:245
  113.5 0.1 reduce
  113.6 0.1 reshape.46
  113.7 0.1 slice_reduce_fusion
  113.9 0.7 squeeze.11.meta_ref.ma_ref
  114.6 0.7 squeeze.9.mb_ref
  115.2 0.7 squeeze.10.mc_ref
  115.9 3.9 %gram_a.1.ga_ref = f32[1,1024]{1,0:T(1,128)} custom-call(f32[2,1024]{1,0:T(2,128)} %squeeze.11.meta_ref.ma_ref, bf16[1024,768]{1,0:T(8,128)(2,1)} %bitcast.13), custom_call_target="tpu_custom_call" | custom-call | flops 1610612736 | bytes 1572864 | tf_op jit(solution)/shard_map/gram_a/pallas_call | solution.py:275
  119.8 6.2 %gram_b.1 = (f32[1,1024]{1,0:T(1,128)}, f32[1,1024]{1,0:T(1,128)}) custom-call(f32[2,1024]{1,0:T(2,128)} %squeeze.11.meta_ref.ma_ref, f32[2,1024]{1,0:T(2,128)} %squeeze.9.mb_ref, bf16[1024,768]{1,0:T(8,128)(2,1)} %bitcast.14, bf16[1024,768]{1,0:T(8,128)(2,1)} %bitcast.15, f32[1,1024]{1,0:T(1,128)} %gram_a.1.ga_ref), custom_call_target="tpu_custom_call" | custom-call | flops 3221225472 | bytes 3145728 | tf_op jit(solution)/shard_map/gram_b/pallas_call | solution.py:276
  126.0 19.4 %all-to-all-done.2 = bf16[16,64,768]{2,1,0:T(8,128)(2,1)S(1)} async-done(((bf16[16,64,768]{2,1,0:T(8,128)(2,1)}), bf16[16,64,768]{2,1,0:T(8,128)(2,1)S(1)}, u32[]{:S(2)}, u32[]{:S(2)}) %all-to-all-start.2) | async-done | bytes 1572896 | tf_op jit(solution)/shard_map/all_to_all | solution.py:245
  145.5 0.0 copy-start.2
  145.5 1.2 copy-done.2
  146.6 6.3 %gram_c.1 = f32[16,1,256]{2,1,0:T(1,128)} custom-call(f32[2,1024]{1,0:T(2,128)} %squeeze.9.mb_ref, f32[2,1024]{1,0:T(2,128)} %squeeze.10.mc_ref, bf16[1024,768]{1,0:T(8,128)(2,1)} %bitcast.16, bf16[1024,768]{1,0:T(8,128)(2,1)} %bitcast.17, f32[1,1024]{1,0:T(1,128)} %get-tuple-element.15.ga_ref, f32[1,1024]{1,0:T(1,128)} %get-tuple-element.16.gb_ref), custom_call_target="tpu_custom_call" | custom-call | flops 3221225472 | bytes 3145728 | tf_op jit(solution)/shard_map/gram_c/pallas_call | solution.py:279
  152.9 15.7 %all_to_all.26.gains_ref = f32[16,1,256]{2,1,0:T(1,128)} all-to-all(f32[16,1,256]{2,1,0:T(1,128)} %gram_c.1), channel_id=1, replica_groups=mesh['parts'=2,'clus'=16] {'clus'}, dimensions={0} | all-to-all | bytes 32768 | tf_op jit(solution)/shard_map/all_to_all | solution.py:282
  168.6 2.0 %last.1 = f32[1,2048]{1,0:T(1,128)} custom-call(s32[3,2048]{1,0:T(4,128)} %get-tuple-element.11.where_ref, f32[16,1,256]{2,1,0:T(1,128)} %all_to_all.26.gains_ref), custom_call_target="tpu_custom_call" | custom-call | flops 50331648 | bytes 16384 | tf_op jit(solution)/shard_map/last/pallas_call | solution.py:283
  (2 shorter events, 0.0 us)
Async XLA Ops:
  25.4 35.6 %all-to-all-start.3 = ((bf16[16,64,768]{2,1,0:T(8,128)(2,1)}), bf16[16,64,768]{2,1,0:T(8,128)(2,1)S(1)}, u32[]{:S(2)}, u32[]{:S(2)}) async-start(bf16[16,64,768]{2,1,0:T(8,128)(2,1)} %bitcast.19), calls=%async_computation.3 | async-start | bytes 3145728 | tf_op jit(solution)/shard_map/all_to_all | solution.py:245
  61.0 1.2 copy-start
  62.2 41.1 %all-to-all-start.1 = ((bf16[16,64,768]{2,1,0:T(8,128)(2,1)}), bf16[16,64,768]{2,1,0:T(8,128)(2,1)S(1)}, u32[]{:S(2)}, u32[]{:S(2)}) async-start(bf16[16,64,768]{2,1,0:T(8,128)(2,1)} %bitcast.20), calls=%async_computation.1 | async-start | bytes 3145728 | tf_op jit(solution)/shard_map/all_to_all | solution.py:245
  103.2 1.2 copy-start.1
  104.4 41.1 %all-to-all-start.2 = ((bf16[16,64,768]{2,1,0:T(8,128)(2,1)}), bf16[16,64,768]{2,1,0:T(8,128)(2,1)S(1)}, u32[]{:S(2)}, u32[]{:S(2)}) async-start(bf16[16,64,768]{2,1,0:T(8,128)(2,1)} %bitcast.18), calls=%async_computation.2 | async-start | bytes 3145728 | tf_op jit(solution)/shard_map/all_to_all | solution.py:245
  145.5 1.2 copy-start.2

commit v2 on v0

v2 whole, which is shorter than its diff:
```python
import jax
import jax.numpy as jnp
from jax import lax
from jax.experimental import pallas as pl
from jax.experimental.pallas import tpu as pltpu
from jax.sharding import PartitionSpec as P

CL_DEV = 4
PARTS = 3
EARLY = 3
MIB = 1024 * 1024

NN = (((1,), (0,)), ((), ()))
NT = (((1,), (1,)), ((), ()))


def dot(left, right, dims):
    return lax.dot_general(left, right, dims, preferred_element_type=jnp.float32)


def lanes(n):
    return -(-n // 128) * 128


def hot(values, count, first=0):
    index = lax.broadcasted_iota(jnp.int32, (count, values.shape[1]), 0) + first
    return jnp.where(index == values, 1.0, 0.0).astype(jnp.bfloat16)


def place(ids, devices, cap):
    rows = ids.shape[1]
    clusters = CL_DEV * devices
    step = 256
    onehot = hot(ids, clusters)
    before = lax.broadcasted_iota(jnp.int32, (step, step), 0) < lax.broadcasted_iota(
        jnp.int32, (step, step), 1
    )
    before = jnp.where(before, 1.0, 0.0).astype(jnp.bfloat16)
    count = jnp.zeros((clusters, 1), jnp.float32)
    ranks = []
    for start in range(0, rows, step):
        piece = onehot[:, start : start + step]
        ranks.append(dot(piece, before, NN) + count)
        count = count + jnp.sum(piece.astype(jnp.float32), axis=1, keepdims=True)
    k = lax.broadcasted_iota(jnp.int32, (clusters, clusters), 0)
    m = lax.broadcasted_iota(jnp.int32, (clusters, clusters), 1)
    j = k % CL_DEV
    plus = (j == 1) & (m == k - 1)
    minus = ((j == 2) & ((m == k) | (m == k + 1))) | ((j == 3) & (m == k))
    mix = (jnp.where(plus, 1.0, 0.0) - jnp.where(minus, 1.0, 0.0)).astype(jnp.bfloat16)
    spread = jnp.broadcast_to(count, (clusters, 128)).astype(jnp.bfloat16)
    base = dot(mix, spread, NN)[:, :1]
    jcol = lax.broadcasted_iota(jnp.int32, (clusters, 1), 0) % CL_DEV
    base = base + jnp.where(jcol >= 2, float(PARTS * cap), 0.0)
    position = []
    for i, start in enumerate(range(0, rows, step)):
        piece = onehot[:, start : start + step].astype(jnp.float32)
        position.append(jnp.sum(piece * (ranks[i] + base), axis=0, keepdims=True))
    return jnp.concatenate(position, axis=1).astype(jnp.int32)


def first_kernel(devices, cap, block, offsets):
    seg = PARTS * cap

    def kernel(ids_ref, emb_ref, unit_ref, where_ref, *rest):
        outs, acc_ref = rest[:-1], rest[-1]
        step = pl.program_id(0)
        last = pl.num_programs(0) - 1
        me = lax.axis_index("clus")

        @pl.when(step == 0)
        def _():
            ids = ids_ref[...]
            owner = ids // CL_DEV
            position = place(ids, devices, cap)
            where_ref[0:1, :] = owner * seg + position
            where_ref[1:2, :] = owner
            where_ref[2:3, :] = position
            where_ref[3:4, :] = ids - owner * CL_DEV
            acc_ref[...] = jnp.zeros_like(acc_ref)

        raw = emb_ref[...]
        sums = jnp.sum(raw * raw, axis=-1, keepdims=True)
        unit = (raw * lax.rsqrt(sums + 1e-06)).astype(jnp.bfloat16)
        begin = pl.multiple_of(step * block, block)
        unit_ref[pl.ds(begin, block), :] = unit
        code = where_ref[0:1, pl.ds(begin, block)]
        pick = jnp.concatenate([hot(code, seg, (me ^ k) * seg) for k in offsets], axis=0)
        acc_ref[...] += dot(pick, unit, NN)

        @pl.when(step == last)
        def _():
            for i, out_ref in enumerate(outs):
                out_ref[...] = acc_ref[i * seg : (i + 1) * seg, :].astype(jnp.bfloat16)

    return kernel


def rest_kernel(devices, cap, offsets):
    seg = PARTS * cap
    wide = lanes(seg)
    half = devices // 2

    def kernel(where_ref, cover_ref, unit_ref, meta_ref, near_ref, *outs):
        me = lax.axis_index("clus")
        own = hot(where_ref[1:2, :], devices)
        there = hot(where_ref[2:3, :], wide)
        cover = own * cover_ref[...].astype(jnp.bfloat16)
        which = own * where_ref[3:4, :].astype(jnp.float32).astype(jnp.bfloat16)
        meta_ref[:, 0, :wide] = dot(cover, there, NT)
        meta_ref[:, 0, wide:] = dot(which, there, NT)
        unit = unit_ref[...]
        code = where_ref[0:1, :]
        for k, out_ref in zip(offsets, outs):
            out_ref[...] = dot(hot(code, seg, (me ^ k) * seg), unit, NN).astype(jnp.bfloat16)
        first = (me // half) * half * seg
        size = half * seg
        tile = size // 4
        for start in range(0, size, tile):
            pick = hot(code, tile, first + start)
            near_ref[start : start + tile, :] = dot(pick, unit, NN).astype(jnp.bfloat16)

    return kernel


def column(row):
    return jnp.transpose(jnp.broadcast_to(row, (128, row.shape[1])))


def source(piece, me, half, offsets):
    if piece < half:
        return (me // half) * half + piece
    return me ^ offsets[piece - half]


def meta_kernel(devices, cap, offsets):
    seg = PARTS * cap
    wide = lanes(seg)
    half = devices // 2

    def kernel(met_ref, rows_ref, cover_ref, which_ref, zero_ref):
        me = lax.axis_index("clus")
        for p in range(devices):
            row = met_ref[source(p, me, half, offsets)]
            rows_ref[p] = row
            cover_ref[p * seg : (p + 1) * seg, :] = column(row[:, :wide])[:seg]
            which_ref[p * seg : (p + 1) * seg, :] = column(row[:, wide:])[:seg]
        zero_ref[...] = jnp.zeros_like(zero_ref)

    return kernel


def pad_rows(piece, count):
    if piece.shape[0] == count:
        return piece
    fill = jnp.zeros((count - piece.shape[0], piece.shape[1]), piece.dtype)
    return jnp.concatenate([piece, fill], axis=0)


def repeat(col, n):
    return jnp.concatenate([col] * (n // 128), axis=1)


def near_gram_kernel(devices, cap, tile):
    seg = PARTS * cap
    wide = lanes(seg)
    half = devices // 2
    group = max(1, 512 // wide)

    def kernel(rows_ref, cover_ref, which_ref, near_ref, gains_ref, out_ref):
        out_ref[...] = gains_ref[...]
        for p in range(0, half, group):
            members = range(p, p + group)
            right = jnp.concatenate(
                [pad_rows(near_ref[q * seg : (q + 1) * seg, :], wide) for q in members], axis=0
            )
            right_which = jnp.concatenate([rows_ref[q][:, wide:] for q in members], axis=1)
            down = jnp.zeros((8, group * wide), jnp.float32)
            for start in range(0, half * seg, tile):
                similar = dot(near_ref[start : start + tile, :], right, NT)
                n = group * wide
                same = repeat(which_ref[start : start + tile, :], n) == right_which
                gain = similar - repeat(cover_ref[start : start + tile, :], n)
                gain = jnp.where(same, jnp.maximum(gain, 0.0), 0.0)
                down = down + jnp.sum(gain.reshape(tile // 8, 8, n), axis=0)
            down = jnp.sum(down, axis=0, keepdims=True)
            for i, q in enumerate(members):
                out_ref[q] = out_ref[q] + down[:, i * wide : (i + 1) * wide]

    return kernel


def far_gram_kernel(devices, cap, offsets, done, new, final):
    seg = PARTS * cap
    wide = lanes(seg)
    half = devices // 2
    per_tile = max(1, 768 // seg)
    xs = list(range(half + done, half + new))

    def kernel(rows_ref, cover_ref, which_ref, near_ref, *rest):
        piece_refs, gains_ref, out_ref = rest[:-2], rest[-2], rest[-1]
        n = len(xs) * wide

        def rows_of(p):
            if p < half:
                return near_ref[p * seg : (p + 1) * seg, :]
            return piece_refs[p - half][...]

        right = jnp.concatenate([pad_rows(rows_of(p), wide) for p in xs], axis=0)
        right_cover = jnp.concatenate([rows_ref[p][:, :wide] for p in xs], axis=1)
        right_which = jnp.concatenate([rows_ref[p][:, wide:] for p in xs], axis=1)
        lane = lax.broadcasted_iota(jnp.int32, (1, wide), 1)
        inside = jnp.concatenate([lane < seg] * len(xs), axis=1)
        right_which = jnp.where(inside, right_which, -1.0)
        down = jnp.zeros((8, n), jnp.float32)
        total = {}
        order = list(range(half + done)) + xs
        for start in range(0, len(order), per_tile):
            members = order[start : start + per_tile]
            left = jnp.concatenate([rows_of(p) for p in members], axis=0)
            similar = dot(left, right, NT)
            low, high = members[0] * seg, (members[-1] + 1) * seg
            same = repeat(which_ref[low:high, :], n) == right_which
            similar = jnp.where(same, similar, -1e30)
            gain = jnp.maximum(similar - repeat(cover_ref[low:high, :], n), 0.0)
            down = down + jnp.sum(gain.reshape((high - low) // 8, 8, n), axis=0)
            old = [p for p in members if p < half + done]
            if not old:
                continue
            count = len(old) * seg
            other = jnp.maximum(similar[:count] - right_cover, 0.0)
            part = other[:, :128]
            for lane0 in range(128, n, 128):
                part = part + other[:, lane0 : lane0 + 128]
            for i, p in enumerate(old):
                mine = pad_rows(part[i * seg : (i + 1) * seg], wide)
                total[p] = jnp.sum(jnp.transpose(mine), axis=0, keepdims=True)
        down = jnp.sum(down, axis=0, keepdims=True)
        for i, p in enumerate(xs):
            total[p] = down[:, i * wide : (i + 1) * wide]
        me = lax.axis_index("clus")
        for p in range(devices):
            value = gains_ref[p]
            if p in total:
                value = value + total[p]
            if final:
                out_ref[source(p, me, half, offsets)] = value
            else:
                out_ref[p] = value

    return kernel


def last_kernel(kernel_devices):
    def kernel(where_ref, gains_ref, out_ref):
        gains = gains_ref[:, 0, :]
        high = gains.astype(jnp.bfloat16)
        rest = gains - high.astype(jnp.float32)
        mid = rest.astype(jnp.bfloat16)
        low = (rest - mid.astype(jnp.float32)).astype(jnp.bfloat16)
        there = hot(where_ref[2:3, :], gains.shape[1])
        found = dot(high, there, NN) + dot(mid, there, NN) + dot(low, there, NN)
        index = lax.broadcasted_iota(jnp.int32, found.shape, 0)
        mine = jnp.where(index == where_ref[1:2, :], found, 0.0)
        out_ref[...] = jnp.sum(mine, axis=0, keepdims=True)

    return kernel


def call(kernel, outs, cost, name, vmem=24, **extra):
    return pl.pallas_call(
        kernel,
        out_shape=outs,
        compiler_params=pltpu.CompilerParams(vmem_limit_bytes=vmem * MIB),
        cost_estimate=pl.CostEstimate(flops=cost[0], bytes_accessed=cost[1], transcendentals=0),
        name=name,
        **extra,
    )


def body(embeddings, coverage, cluster_ids):
    devices = lax.axis_size("clus")
    rows, width = embeddings.shape
    cap = 2 * rows // (CL_DEV * devices)
    seg = PARTS * cap
    wide = lanes(seg)
    half = devices // 2
    quarter = max(1, half // 2)
    offsets = []
    for i in range(quarter):
        offsets += [half + i, half + quarter + i]
    f32, bf16 = jnp.float32, jnp.bfloat16
    S = jax.ShapeDtypeStruct
    ids = cluster_ids.reshape(1, rows)
    cover = coverage.astype(f32).reshape(1, rows)
    block = rows // 4
    unitg = half // 8
    early = EARLY * unitg
    piece = S((seg, width), bf16)

    unit, where, *sent = call(
        first_kernel(devices, cap, block, offsets[:early]),
        [S((rows, width), bf16), S((4, rows), jnp.int32)] + [piece] * early,
        (2 * early * seg * rows * width, 4 * rows * width),
        "first",
        grid=(rows // block,),
        in_specs=[
            pl.BlockSpec((1, rows), lambda i: (0, 0)),
            pl.BlockSpec((block, width), lambda i: (i, 0)),
        ],
        out_specs=[
            pl.BlockSpec((rows, width), lambda i: (0, 0)),
            pl.BlockSpec((4, rows), lambda i: (0, 0)),
        ]
        + [pl.BlockSpec((seg, width), lambda i: (0, 0))] * early,
        scratch_shapes=[pltpu.VMEM((early * seg, width), f32)],
        vmem=56,
    )(ids, embeddings)
    meta, near, *others = call(
        rest_kernel(devices, cap, offsets[early:]),
        [S((devices, 1, 2 * wide), f32), S((half * seg, width), bf16)] + [piece] * (half - early),
        (0, 0),
        "rest",
    )(where, cover, unit)
    sent = sent + others

    far = []
    for i, x in enumerate(sent):
        if i >= early:
            x, far[i - early] = lax.optimization_barrier((x, far[i - early]))
        far.append(lax.ppermute(x, "clus", [(d, d ^ offsets[i]) for d in range(devices)]))
    meta, far[1] = lax.optimization_barrier((meta, far[1]))
    near, far[2] = lax.optimization_barrier((near, far[2]))
    met = lax.all_to_all(meta, "clus", 0, 0, tiled=True)
    groups = [[d for d in range(half)], [d for d in range(half, devices)]]
    near = lax.all_to_all(
        near.reshape(half, seg, width), "clus", 0, 0, tiled=True, axis_index_groups=groups
    ).reshape(half * seg, width)

    cols = S((devices * seg, 128), f32)
    gain_shape = S((devices, 1, wide), f32)
    row_meta, cover_col, which_col, gains = call(
        meta_kernel(devices, cap, offsets),
        [S((devices, 1, 2 * wide), f32), cols, cols, gain_shape],
        (0, 2 * devices * seg * 512),
        "meta",
    )(met)
    size = half * seg
    gains = call(
        near_gram_kernel(devices, cap, size // 2),
        gain_shape,
        (2 * size * size * width, 2 * size * width),
        "near_gram",
    )(row_meta, cover_col, which_col, near, gains)
    done = 0
    for new in [2 * unitg, 4 * unitg, 6 * unitg, 7 * unitg, 8 * unitg]:
        gains = call(
            far_gram_kernel(devices, cap, offsets, done, new, new == half),
            gain_shape,
            (2 * (half + new) * seg * (new - done) * seg * width, 2 * (half + new) * seg * width),
            "far_gram",
        )(row_meta, cover_col, which_col, near, *far[:new], gains)
        done = new
    back = lax.all_to_all(gains, "clus", 0, 0, tiled=True)
    out = call(last_kernel(devices), S((1, rows), f32), (2 * rows * wide * 48, 8 * rows), "last")(where, back)
    return out.reshape(rows)


def solution(mesh):
    placed = (P(("parts", "clus"), None), P(("parts", "clus")), P(("parts", "clus"), None))
    return jax.shard_map(
        body, mesh=mesh, in_specs=placed, out_specs=P(("parts", "clus")), check_vma=False
    )
```

time: 406 us -> 163 us (0.40)
  waiting for transfers between devices: 229 us -> 51.6 us
  local copies, waits for them, and re-layouts: 57.7 us -> 16.3 us
  Pallas kernels: 0 us -> 38 us
  other arithmetic: 36.6 us -> 0.01 us
  starting transfers between devices: 66.8 us -> 44.6 us
  matrix products: 15 us -> 0 us
  blocking collectives: 0 us -> 11.9 us
    all_to_all x3 -> x2, waiting for transfers between devices: 229 us -> 6.37 us  [the longest x1 6.37 us: body(): met = lax.all_to_all(meta, 'clus', 0, 0, tiled=True)]
    all_to_all x3 -> x2, starting transfers between devices: 66.8 us -> 11.7 us  [the longest x1 7.78 us: body(): met = lax.all_to_all(meta, 'clus', 0, 0, tiled=True)]
    ppermute x0 -> x8, waiting for transfers between devices: none -> 45.2 us  [body(): lax.ppermute(x, 'clus', [(d, d ^ offsets[i]) for d in range(devices)])]
    pallas_call x0 -> x10, Pallas kernels: none -> 38 us  [the longest x5 13.7 us: body(): call(far_gram_kernel(devices, cap, offsets, done, new, new == half), gain...]
    ppermute x0 -> x8, starting transfers between devices: none -> 32.9 us  [body(): lax.ppermute(x, 'clus', [(d, d ^ offsets[i]) for d in range(devices)])]
    scatter x2 -> x0, local copies, waits for them, and re-layouts: 23.1 us -> none  [the longest x1 15.1 us: body(): buffer = jnp.zeros((slots, width), jnp.float32).at[slot_index].set(embedd...]
    gather x1 -> x0, local copies, waits for them, and re-layouts: 20.5 us -> none  [body(): return returned.reshape(-1)[slot_index]]
    another operation x3 -> x0, other arithmetic: 18.5 us -> none
  transfers between devices with their start and end apart: 3 -> 10, of which waited for: 2 -> 5; matrix products, arithmetic and copies ran while one was open for 7% -> 0% of each run, Pallas kernels for 0% -> 16%
where the time goes in v2:
time: 163 us; the launch traced here: 162 us
  waiting for transfers between devices  51.6 us (32%)
  starting transfers between devices  44.6 us (27%)
  Pallas kernels  38 us (23%)
  local copies, waits for them, and re-layouts  16.3 us (10%)
  blocking collectives  11.9 us (7%)
    ppermute x8, waiting for transfers between devices, body(): lax.ppermute(x, 'clus', [(d, d ^ offsets[i]) for d in range(devices)])  45.2 us
    ppermute x8, starting transfers between devices, body(): lax.ppermute(x, 'clus', [(d, d ^ offsets[i]) for d in range(devices)])  32.9 us
    unnamed x44, local copies, waits for them, and re-layouts  16.3 us
    pallas_call x5, Pallas kernels, body(): call(far_gram_kernel(devices, cap, offsets, done, new, new == half), gain...  13.7 us
    all_to_all x1, blocking collectives, body(): back = lax.all_to_all(gains, 'clus', 0, 0, tiled=True)  11.9 us
    pallas_call x1, Pallas kernels, body(): call(rest_kernel(devices, cap, offsets[early:]), [S((devices, 1, 2 * wide...  8.64 us
    pallas_call x1, Pallas kernels, body(): call(first_kernel(devices, cap, block, offsets[:early]), [S((rows, width)...  8 us
    all_to_all x1, starting transfers between devices, body(): met = lax.all_to_all(meta, 'clus', 0, 0, tiled=True)  7.78 us
  transfers between devices with their start and end apart: 10, of which 5 were waited for; matrix products, arithmetic and copies ran while one was open for 0% of the time, Pallas kernels for 16%

profile of v2, /device:TPU:0, one launch (start us, length us, event | category | flops | bytes accessed | tf_op | source)
XLA Modules:
  0.0 162.5 jit_solution(3374851737761711649)
XLA Ops:
  0.0 0.0 copy-start.20
  0.0 8.0 %first.1 = (bf16[2048,768]{1,0:T(8,128)(2,1)}, s32[4,2048]{1,0:T(4,128)}, bf16[192,768]{1,0:T(8,128)(2,1)}, bf16[192,768]{1,0:T(8,128)(2,1)}, bf16[192,768]{1,0:T(8,128)(2,1)}) custom-call(s32[1,2048]{1,0:T(1,128)} %bitcast.13, f32[2048,768]{1,0:T(8,128)} %emb_ref.1), custom_call_target="tpu_custom_call" | custom-call | flops 1811939328 | bytes 6291456 | tf_op jit(solution)/shard_map/first/pallas_call | solution.py:301
  8.0 5.0 %collective-permute-start = (bf16[192,768]{1,0:T(8,128)(2,1)}, bf16[192,768]{1,0:T(8,128)(2,1)S(1)}, u32[]{:S(2)}, u32[]{:S(2)}) collective-permute-start(bf16[192,768]{1,0:T(8,128)(2,1)} %get-tuple-element.39), channel_id=1, source_target_pairs={{0,12},{1,13},{2,14},{3,15},{4,8},{5,9},{6,10},{7,11},{8,4},{9,5},... | collective-permute-start | bytes 884744 | tf_op jit(solution)/shard_map/ppermute | solution.py:331
  13.0 0.0 collective-permute-start.1
  13.0 0.0 copy-done.20
  13.1 0.0 copy-start.4
  13.1 1.9 %copy-done.4 = bf16[2048,768]{1,0:T(8,128)(2,1)S(1)} copy-done((bf16[2048,768]{1,0:T(8,128)(2,1)S(1)}, bf16[2048,768]{1,0:T(8,128)(2,1)}, u32[]{:S(2)}) %copy-start.4) | copy-done | bytes 3145752
  14.9 0.0 copy-start.13
  14.9 0.8 copy-done.13
  15.7 8.6 %rest.1 = (f32[16,1,512]{2,1,0:T(1,128)}, bf16[1536,768]{1,0:T(8,128)(2,1)S(1)}, bf16[192,768]{1,0:T(8,128)(2,1)S(1)}, bf16[192,768]{1,0:T(8,128)(2,1)S(1)}, bf1...) custom-call(s32[4,2048]{1,0:T(4,128)S(1)} %copy-done.13, ...), custom_call_target="tpu_custom_call" | custom-call | tf_op jit(solution)/shard_map/rest/pallas_call | solution.py:319
  24.4 0.0 copy-start.7
  24.4 1.4 copy-done.7
  25.8 0.0 copy-start.15
  25.8 0.7 copy-done.15
  26.5 0.0 copy-start.16
  26.5 0.7 copy-done.16
  27.2 0.0 copy-start.17
  27.2 0.7 copy-done.17
  27.9 0.7 copy-done.18
  28.6 0.7 copy-done.19
  29.3 0.0 collective-permute-done.rest_1_
  29.3 7.8 %all-to-all-start = ((f32[16,1,512]{2,1,0:T(1,128)}), f32[16,1,512]{2,1,0:T(1,128)S(1)}, u32[]{:S(2)}, u32[]{:S(2)}) async-start(f32[16,1,512]{2,1,0:T(1,128)} %get-tuple-element.41), calls=%async_computation | async-start | bytes 65536 | tf_op jit(solution)/shard_map/all_to_all | solution.py:334
  37.1 0.3 collective-permute-done.1.rest_2_
  37.4 6.4 %all-to-all-done.met_ref = f32[16,1,512]{2,1,0:T(1,128)S(1)} async-done(((f32[16,1,512]{2,1,0:T(1,128)}), f32[16,1,512]{2,1,0:T(1,128)S(1)}, u32[]{:S(2)}, u32[]{:S(2)}) %all-to-all-start) | async-done | bytes 32800 | tf_op jit(solution)/shard_map/all_to_all | solution.py:334
  43.8 0.6 copy-done.11
  44.4 3.9 %all-to-all-start.1 = ((bf16[8,192,768]{2,1,0:T(8,128)(2,1)}), bf16[8,192,768]{2,1,0:T(8,128)(2,1)S(1)}, u32[]{:S(2)}, u32[]{:S(2)}) async-start(bf16[8,192,768]{2,1,0:T(8,128)(2,1)} %bitcast.11), calls=%async_computation.1 | async-start | bytes 4718592 | tf_op jit(solution)/shard_map/all_to_all | solution.py:336
  48.3 0.0 copy-done.21
  48.3 0.5 collective-permute-start.2
  48.8 32.0 %collective-permute-done.2.rest_0_ = bf16[192,768]{1,0:T(8,128)(2,1)S(1)} collective-permute-done((bf16[192,768]{1,0:T(8,128)(2,1)S(1)}, bf16[192,768]{1,0:T(8,128)(2,1)S(1)}, u32[]{:S(2)}, u32[]{:S(2)}) %collective-permute-start.2) | collective-permute-done | bytes 294944 | tf_op jit(solution)/shard_map/ppermute | solution.py:331
  80.8 0.7 collective-permute-start.3
  81.5 3.7 %collective-permute-start.4 = (bf16[192,768]{1,0:T(8,128)(2,1)}, bf16[192,768]{1,0:T(8,128)(2,1)S(1)}, u32[]{:S(2)}, u32[]{:S(2)}) collective-permute-start(bf16[192,768]{1,0:T(8,128)(2,1)} %copy-done.18), channel_id=1, source_target_pairs={{0,10},{1,11},{2,8},{3,9},{4,14},{5,15},{6,12},{7,13},{8,2},{9,3},... | collective-permute-start | bytes 884744 | tf_op jit(solution)/shard_map/ppermute | solution.py:331
  85.2 2.2 %collective-permute-start.5 = (bf16[192,768]{1,0:T(8,128)(2,1)}, bf16[192,768]{1,0:T(8,128)(2,1)}, u32[]{:S(2)}, u32[]{:S(2)}) collective-permute-start(bf16[192,768]{1,0:T(8,128)(2,1)} %copy-done.17), channel_id=1, source_target_pairs={{0,14},{1,15},{2,12},{3,13},{4,10},{5,11},{6,8},{7,9},{8,6},{9,7},... | collective-permute-start | bytes 884744 | tf_op jit(solution)/shard_map/ppermute | solution.py:331
  87.5 0.8 copy-done.12
  88.2 1.1 meta.1
  89.4 0.0 copy-start
  89.4 1.2 copy-done
  90.5 1.2 copy-done.2
  91.7 0.6 copy-done.8
  92.3 0.0 collective-permute-done.3.rest_3_
  92.4 19.7 %collective-permute-start.6 = (bf16[192,768]{1,0:T(8,128)(2,1)}, bf16[192,768]{1,0:T(8,128)(2,1)}, u32[]{:S(2)}, u32[]{:S(2)}) collective-permute-start(bf16[192,768]{1,0:T(8,128)(2,1)} %copy-done.16), channel_id=1, source_target_pairs={{0,11},{1,10},{2,9},{3,8},{4,15},{5,14},{6,13},{7,12},{8,3},{9,2},... | collective-permute-start | bytes 884744 | tf_op jit(solution)/shard_map/ppermute | solution.py:331
  112.1 12.5 %collective-permute-done.4.rest_4_ = bf16[192,768]{1,0:T(8,128)(2,1)S(1)} collective-permute-done((bf16[192,768]{1,0:T(8,128)(2,1)}, bf16[192,768]{1,0:T(8,128)(2,1)S(1)}, u32[]{:S(2)}, u32[]{:S(2)}) %collective-permute-start.4) | collective-permute-done | bytes 294944 | tf_op jit(solution)/shard_map/ppermute | solution.py:331
  124.6 0.7 copy-done.5
  125.3 1.0 collective-permute-start.7
  126.3 0.0 all-to-all-done.1
  126.3 1.4 copy-done.1
  127.7 1.4 copy-done.3
  129.1 0.8 copy-done.9
  129.9 5.2 %near_gram.1.rest_2_ = f32[16,1,256]{2,1,0:T(1,128)S(1)} custom-call(f32[16,1,512]{2,1,0:T(1,128)S(1)} %copy-done.9, f32[3072,128]{1,0:T(8,128)S(1)} %copy-done.1, f32[3072,128]{1,0:T(8,128)S(1)} %copy-done.3, bf16[1536,768]{1,0:T(8,128)(2,1)S(1)} %bitcast.5, f32[16,1,256]{2,1,0:T(1,128)S(1)} %get-tuple-element.64.gains_ref), custom_call_target="tpu_custom_call" | custom-call | flops 3623878656 | bytes 2359296 | tf_op jit(solution)/shard_map/near_gram/pallas_call | solution.py:349
  135.1 0.0 copy-start.10
  135.1 1.9 %far_gram.5.rest_4_ = f32[16,1,256]{2,1,0:T(1,128)S(1)} custom-call(f32[16,1,512]{2,1,0:T(1,128)S(1)} %copy-done.9, f32[3072,128]{1,0:T(8,128)S(1)} %copy-done.1, f32[3072,128]{1,0:T(8,128)S(1)} %copy-done.3, bf16[1536,768]{1,0:T(8,128)(2,1)S(1)} %bitcast.6, bf16[192,768]{1,0:T(8,128)(2,1)S(1)} %collective-permute-done.2.rest_0_, ...), custom_call_target="tpu_custom_call" | custom-call | flops 1132462080 | bytes 2949120 | tf_op jit(solution)/shard_map/far_gram/pallas_call | solution.py:357
  137.1 0.0 copy-done.10
  137.1 0.0 copy-start.6
  137.1 2.5 %far_gram.6.rest_6_ = f32[16,1,256]{2,1,0:T(1,128)S(1)} custom-call(f32[16,1,512]{2,1,0:T(1,128)S(1)} %copy-done.10, f32[3072,128]{1,0:T(8,128)S(1)} %copy-done.1, f32[3072,128]{1,0:T(8,128)S(1)} %copy-done.3, bf16[1536,768]{1,0:T(8,128)(2,1)S(1)} %bitcast.7, bf16[192,768]{1,0:T(8,128)(2,1)S(1)} %collective-permute-done.2.rest_0_, ...), custom_call_target="tpu_custom_call" | custom-call | flops 1358954496 | bytes 3538944 | tf_op jit(solution)/shard_map/far_gram/pallas_call | solution.py:357
  139.5 0.0 collective-permute-done.5.rest_5_
  139.5 0.0 copy-done.6
  139.5 3.7 %far_gram.7.rest_7_ = f32[16,1,256]{2,1,0:T(1,128)S(1)} custom-call(f32[16,1,512]{2,1,0:T(1,128)S(1)} %copy-done.10, f32[3072,128]{1,0:T(8,128)S(1)} %copy-done.1, f32[3072,128]{1,0:T(8,128)S(1)} %copy-done.3, bf16[1536,768]{1,0:T(8,128)(2,1)S(1)} %bitcast.8, bf16[192,768]{1,0:T(8,128)(2,1)S(1)} %collective-permute-done.2.rest_0_, ...), custom_call_target="tpu_custom_call" | custom-call | flops 1585446912 | bytes 4128768 | tf_op jit(solution)/shard_map/far_gram/pallas_call | solution.py:357
  143.2 0.4 collective-permute-done.6.rest_6_
  143.6 2.7 %far_gram.8.rest_8_ = f32[16,1,256]{2,1,0:T(1,128)S(1)} custom-call(f32[16,1,512]{2,1,0:T(1,128)S(1)} %copy-done.10, f32[3072,128]{1,0:T(8,128)S(1)} %copy-done.1, f32[3072,128]{1,0:T(8,128)S(1)} %copy-done.3, bf16[1536,768]{1,0:T(8,128)(2,1)S(1)} %bitcast.9, bf16[192,768]{1,0:T(8,128)(2,1)S(1)} %collective-permute-done.2.rest_0_, ...), custom_call_target="tpu_custom_call" | custom-call | flops 849346560 | bytes 4423680 | tf_op jit(solution)/shard_map/far_gram/pallas_call | solution.py:357
  146.3 0.0 copy-start.14
  146.3 0.0 collective-permute-done.7.rest_7_
  146.3 3.0 %far_gram.9 = f32[16,1,256]{2,1,0:T(1,128)S(1)} custom-call(f32[16,1,512]{2,1,0:T(1,128)S(1)} %copy-done.10, f32[3072,128]{1,0:T(8,128)S(1)} %copy-done.1, f32[3072,128]{1,0:T(8,128)S(1)} %copy-done.3, bf16[1536,768]{1,0:T(8,128)(2,1)S(1)} %bitcast.10, bf16[192,768]{1,0:T(8,128)(2,1)S(1)} %collective-permute-done.2.rest_0_, ...), custom_call_target="tpu_custom_call" | custom-call | flops 905969664 | bytes 4718592 | tf_op jit(solution)/shard_map/far_gram/pallas_call | solution.py:357
  149.3 11.9 %all_to_all.15.gains_ref = f32[16,1,256]{2,1,0:T(1,128)S(1)} all-to-all(f32[16,1,256]{2,1,0:T(1,128)S(1)} %far_gram.9), channel_id=1, replica_groups=mesh['parts'=2,'clus'=16] {'clus'}, dimensions={0} | all-to-all | bytes 32768 | tf_op jit(solution)/shard_map/all_to_all | solution.py:364
  161.2 0.0 copy-done.14
  161.2 1.3 last.1
  (12 shorter events, 0.0 us)
Async XLA Ops:
  0.0 13.1 %copy-start.20 = (bf16[2048]{0:T(1024)(128)(2,1)S(1)}, bf16[2048]{0:T(1024)(128)(2,1)}, u32[]{:S(2)}) copy-start(bf16[2048]{0:T(1024)(128)(2,1)} %param.4) | copy-start | bytes 12292
  8.0 21.3 %collective-permute-start = (bf16[192,768]{1,0:T(8,128)(2,1)}, bf16[192,768]{1,0:T(8,128)(2,1)S(1)}, u32[]{:S(2)}, u32[]{:S(2)}) collective-permute-start(bf16[192,768]{1,0:T(8,128)(2,1)} %get-tuple-element.39), channel_id=1, source_target_pairs={{0,12},{1,13},{2,14},{3,15},{4,8},{5,9},{6,10},{7,11},{8,4},{9,5},... | collective-permute-start | bytes 884744 | tf_op jit(solution)/shard_map/ppermute | solution.py:331
  13.0 24.4 %collective-permute-start.1 = (bf16[192,768]{1,0:T(8,128)(2,1)}, bf16[192,768]{1,0:T(8,128)(2,1)S(1)}, u32[]{:S(2)}, u32[]{:S(2)}) collective-permute-start(bf16[192,768]{1,0:T(8,128)(2,1)} %get-tuple-element.47), channel_id=1, source_target_pairs={{0,9},{1,8},{2,11},{3,10},{4,13},{5,12},{6,15},{7,14},{8,1},{9,0},... | collective-permute-start | bytes 884744 | tf_op jit(solution)/shard_map/ppermute | solution.py:331
  13.1 1.9 %copy-start.4 = (bf16[2048,768]{1,0:T(8,128)(2,1)S(1)}, bf16[2048,768]{1,0:T(8,128)(2,1)}, u32[]{:S(2)}) copy-start(bf16[2048,768]{1,0:T(8,128)(2,1)} %get-tuple-element.36.unit_ref) | copy-start | bytes 9437188
  14.9 0.8 copy-start.13
  24.4 1.4 copy-start.7
  25.8 0.7 copy-start.15
  26.5 0.7 copy-start.16
  27.2 0.7 copy-start.17
  27.9 0.7 copy-start.18
  28.6 0.7 copy-start.19
  29.3 14.4 %all-to-all-start = ((f32[16,1,512]{2,1,0:T(1,128)}), f32[16,1,512]{2,1,0:T(1,128)S(1)}, u32[]{:S(2)}, u32[]{:S(2)}) async-start(f32[16,1,512]{2,1,0:T(1,128)} %get-tuple-element.41), calls=%async_computation | async-start | bytes 65536 | tf_op jit(solution)/shard_map/all_to_all | solution.py:334
  43.8 0.6 copy-start.11
  44.4 3.9 %copy-start.21 = (bf16[192,768]{1,0:T(8,128)(2,1)S(1)}, bf16[192,768]{1,0:T(8,128)(2,1)}, u32[]{:S(2)}) copy-start(bf16[192,768]{1,0:T(8,128)(2,1)} %get-tuple-element.51) | copy-start | bytes 884740
  44.4 81.9 %all-to-all-start.1 = ((bf16[8,192,768]{2,1,0:T(8,128)(2,1)}), bf16[8,192,768]{2,1,0:T(8,128)(2,1)S(1)}, u32[]{:S(2)}, u32[]{:S(2)}) async-start(bf16[8,192,768]{2,1,0:T(8,128)(2,1)} %bitcast.11), calls=%async_computation.1 | async-start | bytes 4718592 | tf_op jit(solution)/shard_map/all_to_all | solution.py:336
  48.3 32.5 %collective-permute-start.2 = (bf16[192,768]{1,0:T(8,128)(2,1)S(1)}, bf16[192,768]{1,0:T(8,128)(2,1)S(1)}, u32[]{:S(2)}, u32[]{:S(2)}) collective-permute-start(bf16[192,768]{1,0:T(8,128)(2,1)S(1)} %copy-done.21), channel_id=1, source_target_pairs={{0,8},{1,9},{2,10},{3,11},{4,12},{5,13},{6,14},{7,15},{8,0},{9,1},... | collective-permute-start | bytes 884744 | tf_op jit(solution)/shard_map/ppermute | solution.py:331
  80.8 11.6 %collective-permute-start.3 = (bf16[192,768]{1,0:T(8,128)(2,1)}, bf16[192,768]{1,0:T(8,128)(2,1)S(1)}, u32[]{:S(2)}, u32[]{:S(2)}) collective-permute-start(bf16[192,768]{1,0:T(8,128)(2,1)} %copy-done.19), channel_id=1, source_target_pairs={{0,13},{1,12},{2,15},{3,14},{4,9},{5,8},{6,11},{7,10},{8,5},{9,4},... | collective-permute-start | bytes 884744 | tf_op jit(solution)/shard_map/ppermute | solution.py:331
  81.5 43.1 %collective-permute-start.4 = (bf16[192,768]{1,0:T(8,128)(2,1)}, bf16[192,768]{1,0:T(8,128)(2,1)S(1)}, u32[]{:S(2)}, u32[]{:S(2)}) collective-permute-start(bf16[192,768]{1,0:T(8,128)(2,1)} %copy-done.18), channel_id=1, source_target_pairs={{0,10},{1,11},{2,8},{3,9},{4,14},{5,15},{6,12},{7,13},{8,2},{9,3},... | collective-permute-start | bytes 884744 | tf_op jit(solution)/shard_map/ppermute | solution.py:331
  85.2 54.3 %collective-permute-start.5 = (bf16[192,768]{1,0:T(8,128)(2,1)}, bf16[192,768]{1,0:T(8,128)(2,1)}, u32[]{:S(2)}, u32[]{:S(2)}) collective-permute-start(bf16[192,768]{1,0:T(8,128)(2,1)} %copy-done.17), channel_id=1, source_target_pairs={{0,14},{1,15},{2,12},{3,13},{4,10},{5,11},{6,8},{7,9},{8,6},{9,7},... | collective-permute-start | bytes 884744 | tf_op jit(solution)/shard_map/ppermute | solution.py:331
  87.5 0.8 copy-start.12
  89.4 1.2 copy-start
  90.5 1.2 copy-start.2
  91.7 0.6 copy-start.8
  92.4 51.3 %collective-permute-start.6 = (bf16[192,768]{1,0:T(8,128)(2,1)}, bf16[192,768]{1,0:T(8,128)(2,1)}, u32[]{:S(2)}, u32[]{:S(2)}) collective-permute-start(bf16[192,768]{1,0:T(8,128)(2,1)} %copy-done.16), channel_id=1, source_target_pairs={{0,11},{1,10},{2,9},{3,8},{4,15},{5,14},{6,13},{7,12},{8,3},{9,2},... | collective-permute-start | bytes 884744 | tf_op jit(solution)/shard_map/ppermute | solution.py:331
  124.6 0.7 copy-start.5
  125.3 21.0 %collective-permute-start.7 = (bf16[192,768]{1,0:T(8,128)(2,1)}, bf16[192,768]{1,0:T(8,128)(2,1)}, u32[]{:S(2)}, u32[]{:S(2)}) collective-permute-start(bf16[192,768]{1,0:T(8,128)(2,1)} %copy-done.15), channel_id=1, source_target_pairs={{0,15},{1,14},{2,13},{3,12},{4,11},{5,10},{6,9},{7,8},{8,7},{9,6},... | collective-permute-start | bytes 884744 | tf_op jit(solution)/shard_map/ppermute | solution.py:331
  126.3 1.4 copy-start.1
  127.7 1.4 copy-start.3
  129.1 0.8 copy-start.9
  135.1 2.0 %copy-start.10 = (f32[16,1,512]{2,1,0:T(1,128)S(1)}, f32[16,1,512]{2,1,0:T(1,128)}, u32[]{:S(2)}) copy-start(f32[16,1,512]{2,1,0:T(1,128)} %copy-done.8) | copy-start | bytes 98308
  137.1 2.5 %copy-start.6 = (bf16[192,768]{1,0:T(8,128)(2,1)S(1)}, bf16[192,768]{1,0:T(8,128)(2,1)}, u32[]{:S(2)}) copy-start(bf16[192,768]{1,0:T(8,128)(2,1)} %copy-done.5) | copy-start | bytes 884740
  146.3 14.9 %copy-start.14 = (s32[4,2048]{1,0:T(4,128)S(1)}, s32[4,2048]{1,0:T(4,128)}, u32[]{:S(2)}) copy-start(s32[4,2048]{1,0:T(4,128)} %get-tuple-element.35.where_ref) | copy-start | bytes 98308

commit v3 on v2

--- a/solution.py
+++ b/solution.py
@@ -8,6 +8,8 @@
 CL_DEV = 4
 PARTS = 3
 EARLY = 3
+DEPTH = 4
+STOPS = (4, 6, 8, 10, 12, 14, 15, 16)
 MIB = 1024 * 1024
 
 NN = (((1,), (0,)), ((), ()))
@@ -99,9 +101,8 @@
 def rest_kernel(devices, cap, offsets):
     seg = PARTS * cap
     wide = lanes(seg)
-    half = devices // 2
-
-    def kernel(where_ref, cover_ref, unit_ref, meta_ref, near_ref, *outs):
+
+    def kernel(where_ref, cover_ref, unit_ref, meta_ref, *outs):
         me = lax.axis_index("clus")
         own = hot(where_ref[1:2, :], devices)
         there = hot(where_ref[2:3, :], wide)
@@ -113,12 +114,6 @@
         code = where_ref[0:1, :]
         for k, out_ref in zip(offsets, outs):
             out_ref[...] = dot(hot(code, seg, (me ^ k) * seg), unit, NN).astype(jnp.bfloat16)
-        first = (me // half) * half * seg
-        size = half * seg
-        tile = size // 4
-        for start in range(0, size, tile):
-            pick = hot(code, tile, first + start)
-            near_ref[start : start + tile, :] = dot(pick, unit, NN).astype(jnp.bfloat16)
 
     return kernel
 
@@ -127,21 +122,14 @@
     return jnp.transpose(jnp.broadcast_to(row, (128, row.shape[1])))
 
 
-def source(piece, me, half, offsets):
-    if piece < half:
-        return (me // half) * half + piece
-    return me ^ offsets[piece - half]
-
-
 def meta_kernel(devices, cap, offsets):
     seg = PARTS * cap
     wide = lanes(seg)
-    half = devices // 2
 
     def kernel(met_ref, rows_ref, cover_ref, which_ref, zero_ref):
         me = lax.axis_index("clus")
         for p in range(devices):
-            row = met_ref[source(p, me, half, offsets)]
+            row = met_ref[me ^ offsets[p]]
             rows_ref[p] = row
             cover_ref[p * seg : (p + 1) * seg, :] = column(row[:, :wide])[:seg]
             which_ref[p * seg : (p + 1) * seg, :] = column(row[:, wide:])[:seg]
@@ -161,52 +149,16 @@
     return jnp.concatenate([col] * (n // 128), axis=1)
 
 
-def near_gram_kernel(devices, cap, tile):
+def gram_kernel(devices, cap, offsets, done, new):
     seg = PARTS * cap
     wide = lanes(seg)
-    half = devices // 2
-    group = max(1, 512 // wide)
-
-    def kernel(rows_ref, cover_ref, which_ref, near_ref, gains_ref, out_ref):
-        out_ref[...] = gains_ref[...]
-        for p in range(0, half, group):
-            members = range(p, p + group)
-            right = jnp.concatenate(
-                [pad_rows(near_ref[q * seg : (q + 1) * seg, :], wide) for q in members], axis=0
-            )
-            right_which = jnp.concatenate([rows_ref[q][:, wide:] for q in members], axis=1)
-            down = jnp.zeros((8, group * wide), jnp.float32)
-            for start in range(0, half * seg, tile):
-                similar = dot(near_ref[start : start + tile, :], right, NT)
-                n = group * wide
-                same = repeat(which_ref[start : start + tile, :], n) == right_which
-                gain = similar - repeat(cover_ref[start : start + tile, :], n)
-                gain = jnp.where(same, jnp.maximum(gain, 0.0), 0.0)
-                down = down + jnp.sum(gain.reshape(tile // 8, 8, n), axis=0)
-            down = jnp.sum(down, axis=0, keepdims=True)
-            for i, q in enumerate(members):
-                out_ref[q] = out_ref[q] + down[:, i * wide : (i + 1) * wide]
-
-    return kernel
-
-
-def far_gram_kernel(devices, cap, offsets, done, new, final):
-    seg = PARTS * cap
-    wide = lanes(seg)
-    half = devices // 2
     per_tile = max(1, 768 // seg)
-    xs = list(range(half + done, half + new))
-
-    def kernel(rows_ref, cover_ref, which_ref, near_ref, *rest):
-        piece_refs, gains_ref, out_ref = rest[:-2], rest[-2], rest[-1]
-        n = len(xs) * wide
-
-        def rows_of(p):
-            if p < half:
-                return near_ref[p * seg : (p + 1) * seg, :]
-            return piece_refs[p - half][...]
-
-        right = jnp.concatenate([pad_rows(rows_of(p), wide) for p in xs], axis=0)
+    xs = list(range(done, new))
+    n = len(xs) * wide
+
+    def kernel(rows_ref, cover_ref, which_ref, *rest):
+        pieces, gains_ref, out_ref = rest[:-2], rest[-2], rest[-1]
+        right = jnp.concatenate([pad_rows(pieces[p][...], wide) for p in xs], axis=0)
         right_cover = jnp.concatenate([rows_ref[p][:, :wide] for p in xs], axis=1)
         right_which = jnp.concatenate([rows_ref[p][:, wide:] for p in xs], axis=1)
         lane = lax.broadcasted_iota(jnp.int32, (1, wide), 1)
@@ -214,24 +166,23 @@
         right_which = jnp.where(inside, right_which, -1.0)
         down = jnp.zeros((8, n), jnp.float32)
         total = {}
-        order = list(range(half + done)) + xs
-        for start in range(0, len(order), per_tile):
-            members = order[start : start + per_tile]
-            left = jnp.concatenate([rows_of(p) for p in members], axis=0)
+        for start in range(0, new, per_tile):
+            members = range(start, min(start + per_tile, new))
+            left = jnp.concatenate([pieces[p][...] for p in members], axis=0)
             similar = dot(left, right, NT)
             low, high = members[0] * seg, (members[-1] + 1) * seg
             same = repeat(which_ref[low:high, :], n) == right_which
             similar = jnp.where(same, similar, -1e30)
             gain = jnp.maximum(similar - repeat(cover_ref[low:high, :], n), 0.0)
             down = down + jnp.sum(gain.reshape((high - low) // 8, 8, n), axis=0)
-            old = [p for p in members if p < half + done]
+            old = [p for p in members if p < done]
             if not old:
                 continue
             count = len(old) * seg
             other = jnp.maximum(similar[:count] - right_cover, 0.0)
             part = other[:, :128]
-            for lane0 in range(128, n, 128):
-                part = part + other[:, lane0 : lane0 + 128]
+            for begin in range(128, n, 128):
+                part = part + other[:, begin : begin + 128]
             for i, p in enumerate(old):
                 mine = pad_rows(part[i * seg : (i + 1) * seg], wide)
                 total[p] = jnp.sum(jnp.transpose(mine), axis=0, keepdims=True)
@@ -243,8 +194,8 @@
             value = gains_ref[p]
             if p in total:
                 value = value + total[p]
-            if final:
-                out_ref[source(p, me, half, offsets)] = value
+            if new == devices:
+                out_ref[me ^ offsets[p]] = value
             else:
                 out_ref[p] = value
 
@@ -278,28 +229,39 @@
     )
 
 
+def sequence(devices):
+    half = devices // 2
+    quarter = max(1, half // 2)
+    far = []
+    for i in range(quarter):
+        far += [half + i, half + quarter + i]
+    near = sorted(range(1, half), key=lambda k: (-k.bit_length(), k))
+    order = [0, far[0]]
+    for i in range(half - 2):
+        order += [far[i + 1], near[i]]
+    return order + [near[-1], far[-1]]
+
+
 def body(embeddings, coverage, cluster_ids):
     devices = lax.axis_size("clus")
     rows, width = embeddings.shape
     cap = 2 * rows // (CL_DEV * devices)
     seg = PARTS * cap
     wide = lanes(seg)
-    half = devices // 2
-    quarter = max(1, half // 2)
-    offsets = []
-    for i in range(quarter):
-        offsets += [half + i, half + quarter + i]
+    offsets = sequence(devices)
     f32, bf16 = jnp.float32, jnp.bfloat16
     S = jax.ShapeDtypeStruct
     ids = cluster_ids.reshape(1, rows)
     cover = coverage.astype(f32).reshape(1, rows)
     block = rows // 4
-    unitg = half // 8
+    unitg = devices // 16
     early = EARLY * unitg
+    depth = DEPTH * unitg
     piece = S((seg, width), bf16)
+    later = [0] + offsets[1 + early :]
 
     unit, where, *sent = call(
-        first_kernel(devices, cap, block, offsets[:early]),
+        first_kernel(devices, cap, block, offsets[1 : 1 + early]),
         [S((rows, width), bf16), S((4, rows), jnp.int32)] + [piece] * early,
         (2 * early * seg * rows * width, 4 * rows * width),
         "first",
@@ -316,26 +278,23 @@
         scratch_shapes=[pltpu.VMEM((early * seg, width), f32)],
         vmem=56,
     )(ids, embeddings)
-    meta, near, *others = call(
-        rest_kernel(devices, cap, offsets[early:]),
-        [S((devices, 1, 2 * wide), f32), S((half * seg, width), bf16)] + [piece] * (half - early),
+    meta, own, *others = call(
+        rest_kernel(devices, cap, later),
+        [S((devices, 1, 2 * wide), f32)] + [piece] * len(later),
         (0, 0),
         "rest",
+        vmem=56,
     )(where, cover, unit)
     sent = sent + others
 
-    far = []
+    got = []
     for i, x in enumerate(sent):
-        if i >= early:
-            x, far[i - early] = lax.optimization_barrier((x, far[i - early]))
-        far.append(lax.ppermute(x, "clus", [(d, d ^ offsets[i]) for d in range(devices)]))
-    meta, far[1] = lax.optimization_barrier((meta, far[1]))
-    near, far[2] = lax.optimization_barrier((near, far[2]))
+        if i >= depth:
+            x, got[i - depth] = lax.optimization_barrier((x, got[i - depth]))
+        got.append(lax.ppermute(x, "clus", [(d, d ^ offsets[1 + i]) for d in range(devices)]))
+    meta, got[1] = lax.optimization_barrier((meta, got[1]))
     met = lax.all_to_all(meta, "clus", 0, 0, tiled=True)
-    groups = [[d for d in range(half)], [d for d in range(half, devices)]]
-    near = lax.all_to_all(
-        near.reshape(half, seg, width), "clus", 0, 0, tiled=True, axis_index_groups=groups
-    ).reshape(half * seg, width)
+    pieces = [own] + got
 
     cols = S((devices * seg, 128), f32)
     gain_shape = S((devices, 1, wide), f32)
@@ -345,21 +304,16 @@
         (0, 2 * devices * seg * 512),
         "meta",
     )(met)
-    size = half * seg
-    gains = call(
-        near_gram_kernel(devices, cap, size // 2),
-        gain_shape,
-        (2 * size * size * width, 2 * size * width),
-        "near_gram",
-    )(row_meta, cover_col, which_col, near, gains)
     done = 0
-    for new in [2 * unitg, 4 * unitg, 6 * unitg, 7 * unitg, 8 * unitg]:
+    for new in STOPS:
+        new = new * unitg
         gains = call(
-            far_gram_kernel(devices, cap, offsets, done, new, new == half),
+            gram_kernel(devices, cap, offsets, done, new),
             gain_shape,
-            (2 * (half + new) * seg * (new - done) * seg * width, 2 * (half + new) * seg * width),
-            "far_gram",
-        )(row_meta, cover_col, which_col, near, *far[:new], gains)
+            (2 * new * seg * (new - done) * seg * width, 2 * new * seg * width),
+            "gram",
+            vmem=16,
+        )(row_meta, cover_col, which_col, *pieces[:new], gains)
         done = new
     back = lax.all_to_all(gains, "clus", 0, 0, tiled=True)
     out = call(last_kernel(devices), S((1, rows), f32), (2 * rows * wide * 48, 8 * rows), "last")(where, back)

time: 163 us -> 131 us (0.80)
  local copies, waits for them, and re-layouts: 16.3 us -> 0.98 us
  waiting for transfers between devices: 51.6 us -> 43.7 us
  starting transfers between devices: 44.6 us -> 38 us
    unnamed x44 -> x14, local copies, waits for them, and re-layouts: 16.3 us -> 0.98 us
    ppermute x8 -> x15, waiting for transfers between devices: 45.2 us -> 33.3 us  [body(): lax.ppermute(x, 'clus', [(d, d ^ offsets[1 + i]) for d in range(devices)])]
    ppermute x8 -> x15, starting transfers between devices: 32.9 us -> 24.9 us  [body(): lax.ppermute(x, 'clus', [(d, d ^ offsets[1 + i]) for d in range(devices)])]
    all_to_all x1, starting transfers between devices: 7.78 us -> 13 us  [body(): met = lax.all_to_all(meta, 'clus', 0, 0, tiled=True)]
    all_to_all x1, waiting for transfers between devices: 6.37 us -> 10.4 us  [body(): met = lax.all_to_all(meta, 'clus', 0, 0, tiled=True)]
    all_to_all x1 -> x0, starting transfers between devices: 3.93 us -> none  [body(): lax.all_to_all(near.reshape(half, seg, width), 'clus', 0, 0, tiled=True,...]
    pallas_call x8 -> x10, Pallas kernels: 35.6 us -> 34.1 us  [the longest x8 14.9 us: body(): call(gram_kernel(devices, cap, offsets, done, new), gain_shape, (2 * new...]
  transfers between devices with their start and end apart: 10 -> 16, of which waited for: 5 -> 5; matrix products, arithmetic and copies ran while one was open for 0% -> 0% of each run, Pallas kernels for 16% -> 19%
where the time goes in v3:
time: 131 us
  waiting for transfers between devices  43.7 us (33%)
  starting transfers between devices  38 us (29%)
  Pallas kernels  36.5 us (28%)
  blocking collectives  11.1 us (8%)
    ppermute x15, waiting for transfers between devices, body(): lax.ppermute(x, 'clus', [(d, d ^ offsets[1 + i]) for d in range(devices)])  33.3 us
    ppermute x15, starting transfers between devices, body(): lax.ppermute(x, 'clus', [(d, d ^ offsets[1 + i]) for d in range(devices)])  24.9 us
    pallas_call x8, Pallas kernels, body(): call(gram_kernel(devices, cap, offsets, done, new), gain_shape, (2 * new...  14.9 us
    all_to_all x1, starting transfers between devices, body(): met = lax.all_to_all(meta, 'clus', 0, 0, tiled=True)  13 us
    pallas_call x1, Pallas kernels, body(): call(rest_kernel(devices, cap, later), [S((devices, 1, 2 * wide), f32)] +...  11.2 us
    all_to_all x1, blocking collectives, body(): back = lax.all_to_all(gains, 'clus', 0, 0, tiled=True)  11.1 us
    all_to_all x1, waiting for transfers between devices, body(): met = lax.all_to_all(meta, 'clus', 0, 0, tiled=True)  10.4 us
    pallas_call x1, Pallas kernels, body(): call(first_kernel(devices, cap, block, offsets[1:1 + early]), [S((rows, w...  8.01 us
  transfers between devices with their start and end apart: 16, of which 5 were waited for; matrix products, arithmetic and copies ran while one was open for 0% of the time, Pallas kernels for 19%

profile of v3, /device:TPU:0, one launch (start us, length us, event | category | flops | bytes accessed | tf_op | source)
XLA Modules:
  0.0 131.1 jit_solution(8410205226506640956)
XLA Ops:
  0.0 0.0 copy-start.2
  0.0 8.0 %first.1 = (bf16[2048,768]{1,0:T(8,128)(2,1)}, s32[4,2048]{1,0:T(4,128)}, bf16[192,768]{1,0:T(8,128)(2,1)}, bf16[192,768]{1,0:T(8,128)(2,1)}, bf16[192,768]{1,0:T(8,128)(2,1)}) custom-call(s32[1,2048]{1,0:T(1,128)} %bitcast.4, f32[2048,768]{1,0:T(8,128)} %emb_ref.1), custom_call_target="tpu_custom_call" | custom-call | flops 1811939328 | bytes 6291456 | tf_op jit(solution)/shard_map/first/pallas_call | solution.py:263
  8.0 4.0 %collective-permute-start.1 = (bf16[192,768]{1,0:T(8,128)(2,1)}, bf16[192,768]{1,0:T(8,128)(2,1)S(1)}, u32[]{:S(2)}, u32[]{:S(2)}) collective-permute-start(bf16[192,768]{1,0:T(8,128)(2,1)} %get-tuple-element.64), channel_id=1, source_target_pairs={{0,8},{1,9},{2,10},{3,11},{4,12},{5,13},{6,14},{7,15},{8,0},{9,1},... | collective-permute-start | bytes 884744 | tf_op jit(solution)/shard_map/ppermute | solution.py:294
  12.0 1.6 %collective-permute-start.2 = (bf16[192,768]{1,0:T(8,128)(2,1)}, bf16[192,768]{1,0:T(8,128)(2,1)S(1)}, u32[]{:S(2)}, u32[]{:S(2)}) collective-permute-start(bf16[192,768]{1,0:T(8,128)(2,1)} %get-tuple-element.68), channel_id=1, source_target_pairs={{0,4},{1,5},{2,6},{3,7},{4,0},{5,1},{6,2},{7,3},{8,12},{9,13},{10,... | collective-permute-start | bytes 884744 | tf_op jit(solution)/shard_map/ppermute | solution.py:294
  13.6 0.0 collective-permute-start
  13.6 0.0 copy-done.2
  13.6 0.6 reshape.15
  14.2 11.2 %rest.1 = (f32[16,1,512]{2,1,0:T(1,128)}, bf16[192,768]{1,0:T(8,128)(2,1)}, bf16[192,768]{1,0:T(8,128)(2,1)}, bf16[192,768]{1,0:T(8,128)(2,1)}, bf16[192,768]{1,...) custom-call(s32[4,2048]{1,0:T(4,128)} %get-tuple-element.52.where_re, ...), custom_call_target="tpu_custom_call" | custom-call | tf_op jit(solution)/shard_map/rest/pallas_call | solution.py:281
  25.5 0.5 collective-permute-start.3
  26.0 1.4 %collective-permute-done.1.rest_1_ = bf16[192,768]{1,0:T(8,128)(2,1)S(1)} collective-permute-done((bf16[192,768]{1,0:T(8,128)(2,1)}, bf16[192,768]{1,0:T(8,128)(2,1)S(1)}, u32[]{:S(2)}, u32[]{:S(2)}) %collective-permute-start.1) | collective-permute-done | bytes 294944 | tf_op jit(solution)/shard_map/ppermute | solution.py:294
  27.3 2.2 %collective-permute-start.4 = (bf16[192,768]{1,0:T(8,128)(2,1)}, bf16[192,768]{1,0:T(8,128)(2,1)S(1)}, u32[]{:S(2)}, u32[]{:S(2)}) collective-permute-start(bf16[192,768]{1,0:T(8,128)(2,1)} %get-tuple-element.74), channel_id=1, source_target_pairs={{0,5},{1,4},{2,7},{3,6},{4,1},{5,0},{6,3},{7,2},{8,13},{9,12},{10,... | collective-permute-start | bytes 884744 | tf_op jit(solution)/shard_map/ppermute | solution.py:294
  29.6 0.0 collective-permute-done.2.rest_3_
  29.6 0.5 collective-permute-start.6
  30.1 4.1 %collective-permute-done.rest_2_ = bf16[192,768]{1,0:T(8,128)(2,1)S(1)} collective-permute-done((bf16[192,768]{1,0:T(8,128)(2,1)}, bf16[192,768]{1,0:T(8,128)(2,1)S(1)}, u32[]{:S(2)}, u32[]{:S(2)}) %collective-permute-start) | collective-permute-done | bytes 294944 | tf_op jit(solution)/shard_map/ppermute | solution.py:294
  34.2 0.0 collective-permute-start.5
  34.2 15.9 %collective-permute-done.3.rest_4_ = bf16[192,768]{1,0:T(8,128)(2,1)S(1)} collective-permute-done((bf16[192,768]{1,0:T(8,128)(2,1)}, bf16[192,768]{1,0:T(8,128)(2,1)S(1)}, u32[]{:S(2)}, u32[]{:S(2)}) %collective-permute-start.3) | collective-permute-done | bytes 294944 | tf_op jit(solution)/shard_map/ppermute | solution.py:294
  50.2 3.3 %collective-permute-start.7 = (bf16[192,768]{1,0:T(8,128)(2,1)}, bf16[192,768]{1,0:T(8,128)(2,1)S(1)}, u32[]{:S(2)}, u32[]{:S(2)}) collective-permute-start(bf16[192,768]{1,0:T(8,128)(2,1)} %get-tuple-element.83), channel_id=1, source_target_pairs={{0,10},{1,11},{2,8},{3,9},{4,14},{5,15},{6,12},{7,13},{8,2},{9,3},... | collective-permute-start | bytes 884744 | tf_op jit(solution)/shard_map/ppermute | solution.py:294
  53.5 0.0 collective-permute-done.4.rest_5_
  53.5 3.2 %collective-permute-start.8 = (bf16[192,768]{1,0:T(8,128)(2,1)}, bf16[192,768]{1,0:T(8,128)(2,1)S(1)}, u32[]{:S(2)}, u32[]{:S(2)}) collective-permute-start(bf16[192,768]{1,0:T(8,128)(2,1)} %get-tuple-element.86), channel_id=1, source_target_pairs={{0,7},{1,6},{2,5},{3,4},{4,3},{5,2},{6,1},{7,0},{8,15},{9,14},{10,... | collective-permute-start | bytes 884744 | tf_op jit(solution)/shard_map/ppermute | solution.py:294
  56.6 13.0 %all-to-all-start = ((f32[16,1,512]{2,1,0:T(1,128)}), f32[16,1,512]{2,1,0:T(1,128)S(1)}, u32[]{:S(2)}, u32[]{:S(2)}) async-start(f32[16,1,512]{2,1,0:T(1,128)} %get-tuple-element.58), calls=%async_computation | async-start | bytes 65536 | tf_op jit(solution)/shard_map/all_to_all | solution.py:296
  69.7 0.0 collective-permute-done.6.rest_7_
  69.7 1.8 %collective-permute-start.10 = (bf16[192,768]{1,0:T(8,128)(2,1)}, bf16[192,768]{1,0:T(8,128)(2,1)S(1)}, u32[]{:S(2)}, u32[]{:S(2)}) collective-permute-start(bf16[192,768]{1,0:T(8,128)(2,1)} %get-tuple-element.92), channel_id=1, source_target_pairs={{0,2},{1,3},{2,0},{3,1},{4,6},{5,7},{6,4},{7,5},{8,10},{9,11},{10,... | collective-permute-start | bytes 884744 | tf_op jit(solution)/shard_map/ppermute | solution.py:294
  71.5 0.0 collective-permute-done.5.rest_6_
  71.5 3.3 %collective-permute-start.9 = (bf16[192,768]{1,0:T(8,128)(2,1)}, bf16[192,768]{1,0:T(8,128)(2,1)S(1)}, u32[]{:S(2)}, u32[]{:S(2)}) collective-permute-start(bf16[192,768]{1,0:T(8,128)(2,1)} %get-tuple-element.89), channel_id=1, source_target_pairs={{0,14},{1,15},{2,12},{3,13},{4,10},{5,11},{6,8},{7,9},{8,6},{9,7},... | collective-permute-start | bytes 884744 | tf_op jit(solution)/shard_map/ppermute | solution.py:294
  74.8 10.4 %all-to-all-done.met_ref = f32[16,1,512]{2,1,0:T(1,128)S(1)} async-done(((f32[16,1,512]{2,1,0:T(1,128)}), f32[16,1,512]{2,1,0:T(1,128)S(1)}, u32[]{:S(2)}, u32[]{:S(2)}) %all-to-all-start) | async-done | bytes 32800 | tf_op jit(solution)/shard_map/all_to_all | solution.py:296
  85.1 1.1 meta.1
  86.3 0.0 copy-start
  86.3 1.0 copy-done
  87.2 0.0 copy-start.6
  87.2 1.5 %gram.8.rest_6_ = f32[16,1,256]{2,1,0:T(1,128)S(1)} custom-call(f32[16,1,512]{2,1,0:T(1,128)S(1)} %get-tuple-element.59.rows_ref, f32[3072,128]{1,0:T(8,128)S(1)} %get-tuple-element.60.cover_ref, f32[3072,128]{1,0:T(8,128)S(1)} %get-tuple-element.61.which_ref, bf16[192,768]{1,0:T(8,128)(2,1)S(1)} %copy-done, ...), custom_call_target="tpu_custom_call" | custom-call | flops 905969664 | bytes 1179648 | tf_op jit(solution)/shard_map/gram/pallas_call | solution.py:310
  88.7 0.0 copy-start.5
  88.7 0.0 collective-permute-done.7.rest_8_
  88.8 0.0 copy-done.6
  88.8 1.2 collective-permute-start.11
  90.0 1.2 gram.9.rest_8_
  91.2 0.0 copy-start.3
  91.2 0.0 copy-start.4
  91.2 0.0 collective-permute-done.8.rest_9_
  91.2 0.0 copy-done.5
  91.2 1.8 %collective-permute-start.12 = (bf16[192,768]{1,0:T(8,128)(2,1)S(1)}, bf16[192,768]{1,0:T(8,128)(2,1)S(1)}, u32[]{:S(2)}, u32[]{:S(2)}) collective-permute-start(bf16[192,768]{1,0:T(8,128)(2,1)S(1)} %copy-done.5), channel_id=1, source_target_pairs={{0,3},{1,2},{2,1},{3,0},{4,7},{5,6},{6,5},{7,4},{8,11},{9,10},{10,... | collective-permute-start | bytes 884744 | tf_op jit(solution)/shard_map/ppermute | solution.py:294
  93.0 1.7 %gram.10.rest_10_ = f32[16,1,256]{2,1,0:T(1,128)S(1)} custom-call(f32[16,1,512]{2,1,0:T(1,128)S(1)} %get-tuple-element.59.rows_ref, f32[3072,128]{1,0:T(8,128)S(1)} %get-tuple-element.60.cover_ref, f32[3072,128]{1,0:T(8,128)S(1)} %get-tuple-element.61.which_ref, bf16[192,768]{1,0:T(8,128)(2,1)S(1)} %copy-done, ...), custom_call_target="tpu_custom_call" | custom-call | flops 905969664 | bytes 2359296 | tf_op jit(solution)/shard_map/gram/pallas_call | solution.py:310
  94.7 0.0 collective-permute-done.10.rest_11_
  94.7 0.0 copy-done.3
  94.7 1.2 collective-permute-start.14
  96.0 0.0 collective-permute-done.9.rest_10_
  96.0 0.0 copy-done.4
  96.0 0.2 collective-permute-start.13
  96.2 1.9 %gram.11.rest_12_ = f32[16,1,256]{2,1,0:T(1,128)S(1)} custom-call(f32[16,1,512]{2,1,0:T(1,128)S(1)} %get-tuple-element.59.rows_ref, f32[3072,128]{1,0:T(8,128)S(1)} %get-tuple-element.60.cover_ref, f32[3072,128]{1,0:T(8,128)S(1)} %get-tuple-element.61.which_ref, bf16[192,768]{1,0:T(8,128)(2,1)S(1)} %copy-done, ...), custom_call_target="tpu_custom_call" | custom-call | flops 1132462080 | bytes 2949120 | tf_op jit(solution)/shard_map/gram/pallas_call | solution.py:310
  98.2 2.5 %gram.12.rest_14_ = f32[16,1,256]{2,1,0:T(1,128)S(1)} custom-call(f32[16,1,512]{2,1,0:T(1,128)S(1)} %get-tuple-element.59.rows_ref, f32[3072,128]{1,0:T(8,128)S(1)} %get-tuple-element.60.cover_ref, f32[3072,128]{1,0:T(8,128)S(1)} %get-tuple-element.61.which_ref, bf16[192,768]{1,0:T(8,128)(2,1)S(1)} %copy-done, ...), custom_call_target="tpu_custom_call" | custom-call | flops 1358954496 | bytes 3538944 | tf_op jit(solution)/shard_map/gram/pallas_call | solution.py:310
  100.6 11.9 %collective-permute-done.11.rest_12_ = bf16[192,768]{1,0:T(8,128)(2,1)S(1)} collective-permute-done((bf16[192,768]{1,0:T(8,128)(2,1)S(1)}, bf16[192,768]{1,0:T(8,128)(2,1)S(1)}, u32[]{:S(2)}, u32[]{:S(2)}) %collective-permute-start.11) | collective-permute-done | bytes 294944 | tf_op jit(solution)/shard_map/ppermute | solution.py:294
  112.5 0.0 collective-permute-done.12.rest_13_
  112.5 2.7 %gram.13.rest_15_ = f32[16,1,256]{2,1,0:T(1,128)S(1)} custom-call(f32[16,1,512]{2,1,0:T(1,128)S(1)} %get-tuple-element.59.rows_ref, f32[3072,128]{1,0:T(8,128)S(1)} %get-tuple-element.60.cover_ref, f32[3072,128]{1,0:T(8,128)S(1)} %get-tuple-element.61.which_ref, bf16[192,768]{1,0:T(8,128)(2,1)S(1)} %copy-done, ...), custom_call_target="tpu_custom_call" | custom-call | flops 1585446912 | bytes 4128768 | tf_op jit(solution)/shard_map/gram/pallas_call | solution.py:310
  115.2 0.0 collective-permute-done.13.rest_14_
  115.2 1.6 %gram.14.rest_16_ = f32[16,1,256]{2,1,0:T(1,128)S(1)} custom-call(f32[16,1,512]{2,1,0:T(1,128)S(1)} %get-tuple-element.59.rows_ref, f32[3072,128]{1,0:T(8,128)S(1)} %get-tuple-element.60.cover_ref, f32[3072,128]{1,0:T(8,128)S(1)} %get-tuple-element.61.which_ref, bf16[192,768]{1,0:T(8,128)(2,1)S(1)} %copy-done, ...), custom_call_target="tpu_custom_call" | custom-call | flops 849346560 | bytes 4423680 | tf_op jit(solution)/shard_map/gram/pallas_call | solution.py:310
  116.8 0.0 copy-start.1
  116.8 0.0 collective-permute-done.14.rest_15_
  116.8 1.9 %gram.15 = f32[16,1,256]{2,1,0:T(1,128)S(1)} custom-call(f32[16,1,512]{2,1,0:T(1,128)S(1)} %get-tuple-element.59.rows_ref, f32[3072,128]{1,0:T(8,128)S(1)} %get-tuple-element.60.cover_ref, f32[3072,128]{1,0:T(8,128)S(1)} %get-tuple-element.61.which_ref, bf16[192,768]{1,0:T(8,128)(2,1)S(1)} %copy-done, bf16[192,768]{1,0:T(8,128)(2,1)S(1)} %collective-permute-done.1.rest_1_, ...), custom_call_target="tpu_custom_call" | custom-call | flops 905969664 | bytes 4718592 | tf_op jit(solution)/shard_map/gram/pallas_call | solution.py:310
  118.7 11.1 %all_to_all.10.gains_ref = f32[16,1,256]{2,1,0:T(1,128)S(1)} all-to-all(f32[16,1,256]{2,1,0:T(1,128)S(1)} %gram.15), channel_id=1, replica_groups=mesh['parts'=2,'clus'=16] {'clus'}, dimensions={0} | all-to-all | bytes 32768 | tf_op jit(solution)/shard_map/all_to_all | solution.py:318
  129.9 0.0 copy-done.1
  129.9 1.3 last.1
Async XLA Ops:
  0.0 13.6 %copy-start.2 = (bf16[2048]{0:T(1024)(128)(2,1)S(1)}, bf16[2048]{0:T(1024)(128)(2,1)}, u32[]{:S(2)}) copy-start(bf16[2048]{0:T(1024)(128)(2,1)} %param.4) | copy-start | bytes 12292
  8.0 19.3 %collective-permute-start.1 = (bf16[192,768]{1,0:T(8,128)(2,1)}, bf16[192,768]{1,0:T(8,128)(2,1)S(1)}, u32[]{:S(2)}, u32[]{:S(2)}) collective-permute-start(bf16[192,768]{1,0:T(8,128)(2,1)} %get-tuple-element.64), channel_id=1, source_target_pairs={{0,8},{1,9},{2,10},{3,11},{4,12},{5,13},{6,14},{7,15},{8,0},{9,1},... | collective-permute-start | bytes 884744 | tf_op jit(solution)/shard_map/ppermute | solution.py:294
  12.0 17.5 %collective-permute-start.2 = (bf16[192,768]{1,0:T(8,128)(2,1)}, bf16[192,768]{1,0:T(8,128)(2,1)S(1)}, u32[]{:S(2)}, u32[]{:S(2)}) collective-permute-start(bf16[192,768]{1,0:T(8,128)(2,1)} %get-tuple-element.68), channel_id=1, source_target_pairs={{0,4},{1,5},{2,6},{3,7},{4,0},{5,1},{6,2},{7,3},{8,12},{9,13},{10,... | collective-permute-start | bytes 884744 | tf_op jit(solution)/shard_map/ppermute | solution.py:294
  13.6 20.6 %collective-permute-start = (bf16[192,768]{1,0:T(8,128)(2,1)}, bf16[192,768]{1,0:T(8,128)(2,1)S(1)}, u32[]{:S(2)}, u32[]{:S(2)}) collective-permute-start(bf16[192,768]{1,0:T(8,128)(2,1)} %get-tuple-element.56), channel_id=1, source_target_pairs={{0,12},{1,13},{2,14},{3,15},{4,8},{5,9},{6,10},{7,11},{8,4},{9,5},... | collective-permute-start | bytes 884744 | tf_op jit(solution)/shard_map/ppermute | solution.py:294
  25.5 24.7 %collective-permute-start.3 = (bf16[192,768]{1,0:T(8,128)(2,1)}, bf16[192,768]{1,0:T(8,128)(2,1)S(1)}, u32[]{:S(2)}, u32[]{:S(2)}) collective-permute-start(bf16[192,768]{1,0:T(8,128)(2,1)} %get-tuple-element.71), channel_id=1, source_target_pairs={{0,9},{1,8},{2,11},{3,10},{4,13},{5,12},{6,15},{7,14},{8,1},{9,0},... | collective-permute-start | bytes 884744 | tf_op jit(solution)/shard_map/ppermute | solution.py:294
  27.3 26.1 %collective-permute-start.4 = (bf16[192,768]{1,0:T(8,128)(2,1)}, bf16[192,768]{1,0:T(8,128)(2,1)S(1)}, u32[]{:S(2)}, u32[]{:S(2)}) collective-permute-start(bf16[192,768]{1,0:T(8,128)(2,1)} %get-tuple-element.74), channel_id=1, source_target_pairs={{0,5},{1,4},{2,7},{3,6},{4,1},{5,0},{6,3},{7,2},{8,13},{9,12},{10,... | collective-permute-start | bytes 884744 | tf_op jit(solution)/shard_map/ppermute | solution.py:294
  29.6 40.1 %collective-permute-start.6 = (bf16[192,768]{1,0:T(8,128)(2,1)}, bf16[192,768]{1,0:T(8,128)(2,1)S(1)}, u32[]{:S(2)}, u32[]{:S(2)}) collective-permute-start(bf16[192,768]{1,0:T(8,128)(2,1)} %get-tuple-element.80), channel_id=1, source_target_pairs={{0,6},{1,7},{2,4},{3,5},{4,2},{5,3},{6,0},{7,1},{8,14},{9,15},{10,... | collective-permute-start | bytes 884744 | tf_op jit(solution)/shard_map/ppermute | solution.py:294
  34.2 37.3 %collective-permute-start.5 = (bf16[192,768]{1,0:T(8,128)(2,1)}, bf16[192,768]{1,0:T(8,128)(2,1)S(1)}, u32[]{:S(2)}, u32[]{:S(2)}) collective-permute-start(bf16[192,768]{1,0:T(8,128)(2,1)} %get-tuple-element.77), channel_id=1, source_target_pairs={{0,13},{1,12},{2,15},{3,14},{4,9},{5,8},{6,11},{7,10},{8,5},{9,4},... | collective-permute-start | bytes 884744 | tf_op jit(solution)/shard_map/ppermute | solution.py:294
  50.2 38.6 %collective-permute-start.7 = (bf16[192,768]{1,0:T(8,128)(2,1)}, bf16[192,768]{1,0:T(8,128)(2,1)S(1)}, u32[]{:S(2)}, u32[]{:S(2)}) collective-permute-start(bf16[192,768]{1,0:T(8,128)(2,1)} %get-tuple-element.83), channel_id=1, source_target_pairs={{0,10},{1,11},{2,8},{3,9},{4,14},{5,15},{6,12},{7,13},{8,2},{9,3},... | collective-permute-start | bytes 884744 | tf_op jit(solution)/shard_map/ppermute | solution.py:294
  53.5 37.7 %collective-permute-start.8 = (bf16[192,768]{1,0:T(8,128)(2,1)}, bf16[192,768]{1,0:T(8,128)(2,1)S(1)}, u32[]{:S(2)}, u32[]{:S(2)}) collective-permute-start(bf16[192,768]{1,0:T(8,128)(2,1)} %get-tuple-element.86), channel_id=1, source_target_pairs={{0,7},{1,6},{2,5},{3,4},{4,3},{5,2},{6,1},{7,0},{8,15},{9,14},{10,... | collective-permute-start | bytes 884744 | tf_op jit(solution)/shard_map/ppermute | solution.py:294
  56.6 28.5 %all-to-all-start = ((f32[16,1,512]{2,1,0:T(1,128)}), f32[16,1,512]{2,1,0:T(1,128)S(1)}, u32[]{:S(2)}, u32[]{:S(2)}) async-start(f32[16,1,512]{2,1,0:T(1,128)} %get-tuple-element.58), calls=%async_computation | async-start | bytes 65536 | tf_op jit(solution)/shard_map/all_to_all | solution.py:296
  69.7 25.1 %collective-permute-start.10 = (bf16[192,768]{1,0:T(8,128)(2,1)}, bf16[192,768]{1,0:T(8,128)(2,1)S(1)}, u32[]{:S(2)}, u32[]{:S(2)}) collective-permute-start(bf16[192,768]{1,0:T(8,128)(2,1)} %get-tuple-element.92), channel_id=1, source_target_pairs={{0,2},{1,3},{2,0},{3,1},{4,6},{5,7},{6,4},{7,5},{8,10},{9,11},{10,... | collective-permute-start | bytes 884744 | tf_op jit(solution)/shard_map/ppermute | solution.py:294
  71.5 24.5 %collective-permute-start.9 = (bf16[192,768]{1,0:T(8,128)(2,1)}, bf16[192,768]{1,0:T(8,128)(2,1)S(1)}, u32[]{:S(2)}, u32[]{:S(2)}) collective-permute-start(bf16[192,768]{1,0:T(8,128)(2,1)} %get-tuple-element.89), channel_id=1, source_target_pairs={{0,14},{1,15},{2,12},{3,13},{4,10},{5,11},{6,8},{7,9},{8,6},{9,7},... | collective-permute-start | bytes 884744 | tf_op jit(solution)/shard_map/ppermute | solution.py:294
  86.3 1.0 copy-start
  87.2 1.5 %copy-start.6 = (bf16[192,768]{1,0:T(8,128)(2,1)S(1)}, bf16[192,768]{1,0:T(8,128)(2,1)}, u32[]{:S(2)}) copy-start(bf16[192,768]{1,0:T(8,128)(2,1)} %get-tuple-element.94) | copy-start | bytes 884740
  88.7 2.5 %copy-start.5 = (bf16[192,768]{1,0:T(8,128)(2,1)S(1)}, bf16[192,768]{1,0:T(8,128)(2,1)}, u32[]{:S(2)}) copy-start(bf16[192,768]{1,0:T(8,128)(2,1)} %get-tuple-element.95) | copy-start | bytes 884740
  88.8 23.7 %collective-permute-start.11 = (bf16[192,768]{1,0:T(8,128)(2,1)S(1)}, bf16[192,768]{1,0:T(8,128)(2,1)S(1)}, u32[]{:S(2)}, u32[]{:S(2)}) collective-permute-start(bf16[192,768]{1,0:T(8,128)(2,1)S(1)} %copy-done.6), channel_id=1, source_target_pairs={{0,11},{1,10},{2,9},{3,8},{4,15},{5,14},{6,13},{7,12},{8,3},{9,2},... | collective-permute-start | bytes 884744 | tf_op jit(solution)/shard_map/ppermute | solution.py:294
  91.2 3.6 %copy-start.3 = (bf16[192,768]{1,0:T(8,128)(2,1)S(1)}, bf16[192,768]{1,0:T(8,128)(2,1)}, u32[]{:S(2)}) copy-start(bf16[192,768]{1,0:T(8,128)(2,1)} %get-tuple-element.97) | copy-start | bytes 884740
  91.2 4.8 %copy-start.4 = (bf16[192,768]{1,0:T(8,128)(2,1)S(1)}, bf16[192,768]{1,0:T(8,128)(2,1)}, u32[]{:S(2)}) copy-start(bf16[192,768]{1,0:T(8,128)(2,1)} %get-tuple-element.96) | copy-start | bytes 884740
  91.2 21.3 %collective-permute-start.12 = (bf16[192,768]{1,0:T(8,128)(2,1)S(1)}, bf16[192,768]{1,0:T(8,128)(2,1)S(1)}, u32[]{:S(2)}, u32[]{:S(2)}) collective-permute-start(bf16[192,768]{1,0:T(8,128)(2,1)S(1)} %copy-done.5), channel_id=1, source_target_pairs={{0,3},{1,2},{2,1},{3,0},{4,7},{5,6},{6,5},{7,4},{8,11},{9,10},{10,... | collective-permute-start | bytes 884744 | tf_op jit(solution)/shard_map/ppermute | solution.py:294
  94.7 22.1 %collective-permute-start.14 = (bf16[192,768]{1,0:T(8,128)(2,1)S(1)}, bf16[192,768]{1,0:T(8,128)(2,1)S(1)}, u32[]{:S(2)}, u32[]{:S(2)}) collective-permute-start(bf16[192,768]{1,0:T(8,128)(2,1)S(1)} %copy-done.3), channel_id=1, source_target_pairs={{0,15},{1,14},{2,13},{3,12},{4,11},{5,10},{6,9},{7,8},{8,7},{9,6},... | collective-permute-start | bytes 884744 | tf_op jit(solution)/shard_map/ppermute | solution.py:294
  96.0 19.2 %collective-permute-start.13 = (bf16[192,768]{1,0:T(8,128)(2,1)S(1)}, bf16[192,768]{1,0:T(8,128)(2,1)S(1)}, u32[]{:S(2)}, u32[]{:S(2)}) collective-permute-start(bf16[192,768]{1,0:T(8,128)(2,1)S(1)} %copy-done.4), channel_id=1, source_target_pairs={{0,1},{1,0},{2,3},{3,2},{4,5},{5,4},{6,7},{7,6},{8,9},{9,8},{10,11... | collective-permute-start | bytes 884744 | tf_op jit(solution)/shard_map/ppermute | solution.py:294
  116.8 13.0 %copy-start.1 = (s32[4,2048]{1,0:T(4,128)S(1)}, s32[4,2048]{1,0:T(4,128)}, u32[]{:S(2)}) copy-start(s32[4,2048]{1,0:T(4,128)} %get-tuple-element.52.where_ref) | copy-start | bytes 98308

commit v4 on v3

--- a/solution.py
+++ b/solution.py
@@ -7,7 +7,7 @@
 
 CL_DEV = 4
 PARTS = 3
-EARLY = 3
+EARLY = 1
 DEPTH = 4
 STOPS = (4, 6, 8, 10, 12, 14, 15, 16)
 MIB = 1024 * 1024
@@ -61,48 +61,65 @@
     return jnp.concatenate(position, axis=1).astype(jnp.int32)
 
 
-def first_kernel(devices, cap, block, offsets):
+def first_kernel(devices, cap, steps, offsets):
     seg = PARTS * cap
 
     def kernel(ids_ref, emb_ref, unit_ref, where_ref, *rest):
-        outs, acc_ref = rest[:-1], rest[-1]
-        step = pl.program_id(0)
-        last = pl.num_programs(0) - 1
-        me = lax.axis_index("clus")
-
-        @pl.when(step == 0)
-        def _():
-            ids = ids_ref[...]
-            owner = ids // CL_DEV
-            position = place(ids, devices, cap)
-            where_ref[0:1, :] = owner * seg + position
-            where_ref[1:2, :] = owner
-            where_ref[2:3, :] = position
-            where_ref[3:4, :] = ids - owner * CL_DEV
-            acc_ref[...] = jnp.zeros_like(acc_ref)
-
-        raw = emb_ref[...]
-        sums = jnp.sum(raw * raw, axis=-1, keepdims=True)
-        unit = (raw * lax.rsqrt(sums + 1e-06)).astype(jnp.bfloat16)
-        begin = pl.multiple_of(step * block, block)
-        unit_ref[pl.ds(begin, block), :] = unit
-        code = where_ref[0:1, pl.ds(begin, block)]
-        pick = jnp.concatenate([hot(code, seg, (me ^ k) * seg) for k in offsets], axis=0)
-        acc_ref[...] += dot(pick, unit, NN)
-
-        @pl.when(step == last)
-        def _():
-            for i, out_ref in enumerate(outs):
-                out_ref[...] = acc_ref[i * seg : (i + 1) * seg, :].astype(jnp.bfloat16)
-
-    return kernel
-
-
-def rest_kernel(devices, cap, offsets):
+        count = len(offsets)
+        outs, scratch = rest[:count], rest[count:]
+        raw_ref, rows_ref, piece_ref, in_sems, rows_sems, out_sems = scratch
+        me = lax.axis_index("clus")
+        block = raw_ref.shape[0] // steps
+
+        def load(i):
+            part = pl.ds(i * block, block)
+            return pltpu.make_async_copy(emb_ref.at[part], raw_ref.at[part], in_sems.at[i])
+
+        def store(i):
+            part = pl.ds(i * block, block)
+            return pltpu.make_async_copy(rows_ref.at[part], unit_ref.at[part], rows_sems.at[i])
+
+        for i in range(steps):
+            load(i).start()
+        ids = ids_ref[...]
+        owner = ids // CL_DEV
+        position = place(ids, devices, cap)
+        code = owner * seg + position
+        where_ref[0:1, :] = code
+        where_ref[1:2, :] = owner
+        where_ref[2:3, :] = position
+        where_ref[3:4, :] = ids - owner * CL_DEV
+        for i in range(steps):
+            load(i).wait()
+            raw = raw_ref[i * block : (i + 1) * block, :]
+            sums = jnp.sum(raw * raw, axis=-1, keepdims=True)
+            unit = (raw * lax.rsqrt(sums + 1e-06)).astype(jnp.bfloat16)
+            rows_ref[i * block : (i + 1) * block, :] = unit
+            store(i).start()
+        send_pieces(code, rows_ref, seg, me, offsets, outs, piece_ref, out_sems)
+        for i in range(steps):
+            store(i).wait()
+
+    return kernel
+
+
+def send_pieces(code, unit_ref, seg, me, offsets, outs, piece_ref, sems):
+    copies = []
+    for i, (k, out_ref) in enumerate(zip(offsets, outs)):
+        pick = hot(code, seg, (me ^ k) * seg)
+        piece_ref[i] = dot(pick, unit_ref[...], NN).astype(jnp.bfloat16)
+        copies.append(pltpu.make_async_copy(piece_ref.at[i], out_ref, sems.at[i]))
+        copies[-1].start()
+    for copy in copies:
+        copy.wait()
+
+
+def second_kernel(devices, cap, offsets):
     seg = PARTS * cap
     wide = lanes(seg)
 
-    def kernel(where_ref, cover_ref, unit_ref, meta_ref, *outs):
+    def kernel(where_ref, cover_ref, unit_ref, meta_ref, *rest):
+        outs, (piece_ref, sems) = rest[: len(offsets)], rest[len(offsets) :]
         me = lax.axis_index("clus")
         own = hot(where_ref[1:2, :], devices)
         there = hot(where_ref[2:3, :], wide)
@@ -110,10 +127,18 @@
         which = own * where_ref[3:4, :].astype(jnp.float32).astype(jnp.bfloat16)
         meta_ref[:, 0, :wide] = dot(cover, there, NT)
         meta_ref[:, 0, wide:] = dot(which, there, NT)
-        unit = unit_ref[...]
-        code = where_ref[0:1, :]
-        for k, out_ref in zip(offsets, outs):
-            out_ref[...] = dot(hot(code, seg, (me ^ k) * seg), unit, NN).astype(jnp.bfloat16)
+        send_pieces(where_ref[0:1, :], unit_ref, seg, me, offsets, outs, piece_ref, sems)
+
+    return kernel
+
+
+def rest_kernel(devices, cap, offsets):
+    seg = PARTS * cap
+
+    def kernel(where_ref, unit_ref, *rest):
+        outs, (piece_ref, sems) = rest[: len(offsets)], rest[len(offsets) :]
+        me = lax.axis_index("clus")
+        send_pieces(where_ref[0:1, :], unit_ref, seg, me, offsets, outs, piece_ref, sems)
 
     return kernel
 
@@ -253,38 +278,56 @@
     S = jax.ShapeDtypeStruct
     ids = cluster_ids.reshape(1, rows)
     cover = coverage.astype(f32).reshape(1, rows)
-    block = rows // 4
     unitg = devices // 16
     early = EARLY * unitg
     depth = DEPTH * unitg
     piece = S((seg, width), bf16)
-    later = [0] + offsets[1 + early :]
-
+
+    def pieces_of(count):
+        return dict(
+            out_specs=[pl.BlockSpec(memory_space=pltpu.HBM)] * count,
+            scratch_shapes=[pltpu.VMEM((count, seg, width), bf16), pltpu.SemaphoreType.DMA((count,))],
+        )
+
+    full = pl.BlockSpec(memory_space=pltpu.VMEM)
+    steps = 8
+    lead = pieces_of(early)
     unit, where, *sent = call(
-        first_kernel(devices, cap, block, offsets[1 : 1 + early]),
+        first_kernel(devices, cap, steps, offsets[1 : 1 + early]),
         [S((rows, width), bf16), S((4, rows), jnp.int32)] + [piece] * early,
         (2 * early * seg * rows * width, 4 * rows * width),
         "first",
-        grid=(rows // block,),
-        in_specs=[
-            pl.BlockSpec((1, rows), lambda i: (0, 0)),
-            pl.BlockSpec((block, width), lambda i: (i, 0)),
-        ],
-        out_specs=[
-            pl.BlockSpec((rows, width), lambda i: (0, 0)),
-            pl.BlockSpec((4, rows), lambda i: (0, 0)),
-        ]
-        + [pl.BlockSpec((seg, width), lambda i: (0, 0))] * early,
-        scratch_shapes=[pltpu.VMEM((early * seg, width), f32)],
+        in_specs=[full, pl.BlockSpec(memory_space=pltpu.HBM)],
+        out_specs=[pl.BlockSpec(memory_space=pltpu.HBM), full] + lead["out_specs"],
+        scratch_shapes=[pltpu.VMEM((rows, width), f32), pltpu.VMEM((rows, width), bf16)]
+        + [lead["scratch_shapes"][0], pltpu.SemaphoreType.DMA((steps,))]
+        + [pltpu.SemaphoreType.DMA((steps,)), lead["scratch_shapes"][1]],
         vmem=56,
     )(ids, embeddings)
-    meta, own, *others = call(
+    middle = pieces_of(depth - early)
+    meta, *others = call(
+        second_kernel(devices, cap, offsets[1 + early : 1 + depth]),
+        [S((devices, 1, 2 * wide), f32)] + [piece] * (depth - early),
+        (0, 0),
+        "second",
+        in_specs=[full] * 3,
+        out_specs=[full] + middle["out_specs"],
+        scratch_shapes=middle["scratch_shapes"],
+        vmem=12,
+    )(where, cover, unit)
+    sent = sent + others
+    met = lax.all_to_all(meta, "clus", 0, 0, tiled=True)
+    after, met = lax.optimization_barrier((where, met))
+    later = [0] + offsets[1 + depth :]
+    own, *others = call(
         rest_kernel(devices, cap, later),
-        [S((devices, 1, 2 * wide), f32)] + [piece] * len(later),
+        [piece] * len(later),
         (0, 0),
         "rest",
-        vmem=56,
-    )(where, cover, unit)
+        in_specs=[full] * 2,
+        vmem=20,
+        **pieces_of(len(later)),
+    )(after, unit)
     sent = sent + others
 
     got = []
@@ -292,8 +335,6 @@
         if i >= depth:
             x, got[i - depth] = lax.optimization_barrier((x, got[i - depth]))
         got.append(lax.ppermute(x, "clus", [(d, d ^ offsets[1 + i]) for d in range(devices)]))
-    meta, got[1] = lax.optimization_barrier((meta, got[1]))
-    met = lax.all_to_all(meta, "clus", 0, 0, tiled=True)
     pieces = [own] + got
 
     cols = S((devices * seg, 128), f32)

time: 131 us -> 150 us (1.15)
  blocking collectives: 11.1 us -> 44.4 us
  starting transfers between devices: 38 us -> 20.2 us
  Pallas kernels: 36.5 us -> 40.1 us
  local copies, waits for them, and re-layouts: 0.98 us -> 2.66 us
    all_to_all x0 -> x1, blocking collectives: none -> 32.1 us  [body(): met = lax.all_to_all(meta, 'clus', 0, 0, tiled=True)]
    all_to_all x1 -> x0, starting transfers between devices: 13 us -> none  [body(): met = lax.all_to_all(meta, 'clus', 0, 0, tiled=True)]
    all_to_all x1 -> x0, waiting for transfers between devices: 10.4 us -> none  [body(): met = lax.all_to_all(meta, 'clus', 0, 0, tiled=True)]
    ppermute x15, waiting for transfers between devices: 33.3 us -> 42.6 us  [body(): lax.ppermute(x, 'clus', [(d, d ^ offsets[1 + i]) for d in range(devices)])]
    ppermute x15, starting transfers between devices: 24.9 us -> 20.2 us  [body(): lax.ppermute(x, 'clus', [(d, d ^ offsets[1 + i]) for d in range(devices)])]
    pallas_call x2 -> x3, Pallas kernels: 19.3 us -> 22.8 us  [the longest x1 12.8 us: body(): call(rest_kernel(devices, cap, later), [piece] * len(later), (0, 0), 'res...]
    unnamed x14 -> x10, local copies, waits for them, and re-layouts: 0.98 us -> 2.66 us
  transfers between devices with their start and end apart: 16 -> 15, of which waited for: 5 -> 5; matrix products, arithmetic and copies ran while one was open for 0% -> 0% of each run, Pallas kernels for 19% -> 20%
where the time goes in v4:
time: 150 us
  blocking collectives  44.4 us (30%)
  waiting for transfers between devices  42.6 us (28%)
  Pallas kernels  40.1 us (27%)
  starting transfers between devices  20.2 us (13%)
  local copies, waits for them, and re-layouts  2.66 us (2%)
    ppermute x15, waiting for transfers between devices, body(): lax.ppermute(x, 'clus', [(d, d ^ offsets[1 + i]) for d in range(devices)])  42.6 us
    all_to_all x1, blocking collectives, body(): met = lax.all_to_all(meta, 'clus', 0, 0, tiled=True)  32.1 us
    ppermute x15, starting transfers between devices, body(): lax.ppermute(x, 'clus', [(d, d ^ offsets[1 + i]) for d in range(devices)])  20.2 us
    pallas_call x8, Pallas kernels, body(): call(gram_kernel(devices, cap, offsets, done, new), gain_shape, (2 * new...  14.9 us
    pallas_call x1, Pallas kernels, body(): call(rest_kernel(devices, cap, later), [piece] * len(later), (0, 0), 'res...  12.8 us
    all_to_all x1, blocking collectives, body(): back = lax.all_to_all(gains, 'clus', 0, 0, tiled=True)  12.3 us
    pallas_call x1, Pallas kernels, body(): call(first_kernel(devices, cap, steps, offsets[1:1 + early]), [S((rows, w...  6.5 us
    pallas_call x1, Pallas kernels, body(): call(second_kernel(devices, cap, offsets[1 + early:1 + depth]), [S((devic...  3.49 us
  transfers between devices with their start and end apart: 15, of which 5 were waited for; matrix products, arithmetic and copies ran while one was open for 0% of the time, Pallas kernels for 20%

profile of v4, /device:TPU:0, one launch (start us, length us, event | category | flops | bytes accessed | tf_op | source)
XLA Modules:
  0.0 150.0 jit_solution(7216152751770665171)
XLA Ops:
  0.0 0.0 copy-start.4
  0.0 6.5 %first.1 = (bf16[2048,768]{1,0:T(8,128)(2,1)}, s32[4,2048]{1,0:T(4,128)}, bf16[192,768]{1,0:T(8,128)(2,1)}) custom-call(s32[1,2048]{1,0:T(1,128)} %bitcast.4, f32[2048,768]{1,0:T(8,128)} %emb_ref.1), custom_call_target="tpu_custom_call" | custom-call | flops 603979776 | bytes 6291456 | tf_op jit(solution)/shard_map/first/pallas_call | solution.py:295
  6.5 4.1 %collective-permute-start = (bf16[192,768]{1,0:T(8,128)(2,1)}, bf16[192,768]{1,0:T(8,128)(2,1)S(1)}, u32[]{:S(2)}, u32[]{:S(2)}) collective-permute-start(bf16[192,768]{1,0:T(8,128)(2,1)} %get-tuple-element.62), channel_id=1, source_target_pairs={{0,8},{1,9},{2,10},{3,11},{4,12},{5,13},{6,14},{7,15},{8,0},{9,1},... | collective-permute-start | bytes 884744 | tf_op jit(solution)/shard_map/ppermute | solution.py:337
  10.6 0.0 copy-done.4
  10.6 0.0 copy-start
  10.6 1.9 %copy-done = bf16[2048,768]{1,0:T(8,128)(2,1)S(1)} copy-done((bf16[2048,768]{1,0:T(8,128)(2,1)S(1)}, bf16[2048,768]{1,0:T(8,128)(2,1)}, u32[]{:S(2)}) %copy-start) | copy-done | bytes 3145752
  12.5 0.0 copy-start.2
  12.5 0.8 copy-done.2
  13.3 0.0 copy-start.1
  13.3 0.0 copy-start.3
  13.3 3.5 %second.1 = (f32[16,1,512]{2,1,0:T(1,128)S(1)}, bf16[192,768]{1,0:T(8,128)(2,1)S(1)}, bf16[192,768]{1,0:T(8,128)(2,1)S(1)}, bf16[192,768]{1,0:T(8,128)(2,1)S(1)}) custom-call(s32[4,2048]{1,0:T(4,128)S(1)} %copy-done.2, f32[1,2048]{1,0:T(1,128)S(1)} %bitcast.3, bf16[2048,768]{1,0:T(8,128)(2,1)S(1)} %copy-done), custom_call_target="tpu_custom_call" | custom-call | tf_op jit(solution)/shard_map/second/pallas_call | solution.py:308
  16.8 1.6 %collective-permute-start.2 = (bf16[192,768]{1,0:T(8,128)(2,1)S(1)}, bf16[192,768]{1,0:T(8,128)(2,1)S(1)}, u32[]{:S(2)}, u32[]{:S(2)}) collective-permute-start(bf16[192,768]{1,0:T(8,128)(2,1)S(1)} %get-tuple-element.68), channel_id=1, source_target_pairs={{0,4},{1,5},{2,6},{3,7},{4,0},{5,1},{6,2},{7,3},{8,12},{9,13},{10,... | collective-permute-start | bytes 884744 | tf_op jit(solution)/shard_map/ppermute | solution.py:337
  18.4 0.0 collective-permute-start.1
  18.4 0.5 collective-permute-start.3
  18.9 32.1 %all_to_all.10.met_ref = f32[16,1,512]{2,1,0:T(1,128)S(1)} all-to-all(f32[16,1,512]{2,1,0:T(1,128)S(1)} %get-tuple-element.54), channel_id=1, replica_groups=mesh['parts'=2,'clus'=16] {'clus'}, dimensions={0} | all-to-all | bytes 65536 | tf_op jit(solution)/shard_map/all_to_all | solution.py:319
  51.0 0.0 copy-done.1
  51.0 0.0 copy-done.3
  51.0 12.8 %rest.1 = (bf16[192,768]{1,0:T(8,128)(2,1)S(1)}, bf16[192,768]{1,0:T(8,128)(2,1)S(1)}, bf16[192,768]{1,0:T(8,128)(2,1)S(1)}, bf16[192,768]{1,0:T(8,128)(2,1)S(1)...) custom-call(s32[4,2048]{1,0:T(4,128)S(1)} %copy-done.3, ...), custom_call_target="tpu_custom_call" | custom-call | tf_op jit(solution)/shard_map/rest/pallas_call | solution.py:322
  63.9 0.0 collective-permute-done.rest_1_
  63.9 0.4 collective-permute-start.4
  64.3 0.0 collective-permute-done.2.rest_3_
  64.3 1.5 collective-permute-start.6
  65.7 0.0 collective-permute-done.1.rest_2_
  65.7 3.2 %collective-permute-start.5 = (bf16[192,768]{1,0:T(8,128)(2,1)S(1)}, bf16[192,768]{1,0:T(8,128)(2,1)S(1)}, u32[]{:S(2)}, u32[]{:S(2)}) collective-permute-start(bf16[192,768]{1,0:T(8,128)(2,1)S(1)} %get-tuple-element.77), channel_id=1, source_target_pairs={{0,13},{1,12},{2,15},{3,14},{4,9},{5,8},{6,11},{7,10},{8,5},{9,4},... | collective-permute-start | bytes 884744 | tf_op jit(solution)/shard_map/ppermute | solution.py:337
  68.9 0.0 collective-permute-done.3.rest_4_
  68.9 0.2 collective-permute-start.7
  69.2 3.8 %collective-permute-done.4.rest_5_ = bf16[192,768]{1,0:T(8,128)(2,1)S(1)} collective-permute-done((bf16[192,768]{1,0:T(8,128)(2,1)S(1)}, bf16[192,768]{1,0:T(8,128)(2,1)S(1)}, u32[]{:S(2)}, u32[]{:S(2)}) %collective-permute-start.4) | collective-permute-done | bytes 294944 | tf_op jit(solution)/shard_map/ppermute | solution.py:337
  72.9 1.0 collective-permute-start.8
  74.0 17.2 %collective-permute-done.6.rest_7_ = bf16[192,768]{1,0:T(8,128)(2,1)S(1)} collective-permute-done((bf16[192,768]{1,0:T(8,128)(2,1)S(1)}, bf16[192,768]{1,0:T(8,128)(2,1)S(1)}, u32[]{:S(2)}, u32[]{:S(2)}) %collective-permute-start.6) | collective-permute-done | bytes 294944 | tf_op jit(solution)/shard_map/ppermute | solution.py:337
  91.2 2.8 %collective-permute-start.10 = (bf16[192,768]{1,0:T(8,128)(2,1)S(1)}, bf16[192,768]{1,0:T(8,128)(2,1)S(1)}, u32[]{:S(2)}, u32[]{:S(2)}) collective-permute-start(bf16[192,768]{1,0:T(8,128)(2,1)S(1)} %get-tuple-element.92), channel_id=1, source_target_pairs={{0,2},{1,3},{2,0},{3,1},{4,6},{5,7},{6,4},{7,5},{8,10},{9,11},{10,... | collective-permute-start | bytes 884744 | tf_op jit(solution)/shard_map/ppermute | solution.py:337
  93.9 0.0 collective-permute-done.5.rest_6_
  93.9 0.2 collective-permute-start.9
  94.2 1.1 meta.1
  95.3 1.5 gram.8.rest_6_
  96.8 0.0 collective-permute-done.7.rest_8_
  96.8 0.1 collective-permute-start.11
  96.9 1.2 gram.9.rest_8_
  98.0 4.3 %collective-permute-done.8.rest_9_ = bf16[192,768]{1,0:T(8,128)(2,1)S(1)} collective-permute-done((bf16[192,768]{1,0:T(8,128)(2,1)S(1)}, bf16[192,768]{1,0:T(8,128)(2,1)S(1)}, u32[]{:S(2)}, u32[]{:S(2)}) %collective-permute-start.8) | collective-permute-done | bytes 294944 | tf_op jit(solution)/shard_map/ppermute | solution.py:337
  102.4 0.0 collective-permute-start.12
  102.4 1.7 %gram.10.rest_10_ = f32[16,1,256]{2,1,0:T(1,128)S(1)} custom-call(f32[16,1,512]{2,1,0:T(1,128)S(1)} %get-tuple-element.56.rows_ref, f32[3072,128]{1,0:T(8,128)S(1)} %get-tuple-element.57.cover_ref, f32[3072,128]{1,0:T(8,128)S(1)} %get-tuple-element.58.which_ref, bf16[192,768]{1,0:T(8,128)(2,1)S(1)} %get-tuple-element.60.rest_0_, ...), custom_call_target="tpu_custom_call" | custom-call | flops 905969664 | bytes 2359296 | tf_op jit(solution)/shard_map/gram/pallas_call | solution.py:351
  104.1 7.2 %collective-permute-done.10.rest_11_ = bf16[192,768]{1,0:T(8,128)(2,1)S(1)} collective-permute-done((bf16[192,768]{1,0:T(8,128)(2,1)S(1)}, bf16[192,768]{1,0:T(8,128)(2,1)S(1)}, u32[]{:S(2)}, u32[]{:S(2)}) %collective-permute-start.10) | collective-permute-done | bytes 294944 | tf_op jit(solution)/shard_map/ppermute | solution.py:337
  111.3 3.9 %collective-permute-start.14 = (bf16[192,768]{1,0:T(8,128)(2,1)S(1)}, bf16[192,768]{1,0:T(8,128)(2,1)S(1)}, u32[]{:S(2)}, u32[]{:S(2)}) collective-permute-start(bf16[192,768]{1,0:T(8,128)(2,1)S(1)} %get-tuple-element.97), channel_id=1, source_target_pairs={{0,15},{1,14},{2,13},{3,12},{4,11},{5,10},{6,9},{7,8},{8,7},{9,6},... | collective-permute-start | bytes 884744 | tf_op jit(solution)/shard_map/ppermute | solution.py:337
  115.2 0.0 collective-permute-done.9.rest_10_
  115.2 0.6 collective-permute-start.13
  115.8 1.9 %gram.11.rest_12_ = f32[16,1,256]{2,1,0:T(1,128)S(1)} custom-call(f32[16,1,512]{2,1,0:T(1,128)S(1)} %get-tuple-element.56.rows_ref, f32[3072,128]{1,0:T(8,128)S(1)} %get-tuple-element.57.cover_ref, f32[3072,128]{1,0:T(8,128)S(1)} %get-tuple-element.58.which_ref, bf16[192,768]{1,0:T(8,128)(2,1)S(1)} %get-tuple-element.60.rest_0_, ...), custom_call_target="tpu_custom_call" | custom-call | flops 1132462080 | bytes 2949120 | tf_op jit(solution)/shard_map/gram/pallas_call | solution.py:351
  117.7 2.5 %gram.12.rest_14_ = f32[16,1,256]{2,1,0:T(1,128)S(1)} custom-call(f32[16,1,512]{2,1,0:T(1,128)S(1)} %get-tuple-element.56.rows_ref, f32[3072,128]{1,0:T(8,128)S(1)} %get-tuple-element.57.cover_ref, f32[3072,128]{1,0:T(8,128)S(1)} %get-tuple-element.58.which_ref, bf16[192,768]{1,0:T(8,128)(2,1)S(1)} %get-tuple-element.60.rest_0_, ...), custom_call_target="tpu_custom_call" | custom-call | flops 1358954496 | bytes 3538944 | tf_op jit(solution)/shard_map/gram/pallas_call | solution.py:351
  120.2 10.1 %collective-permute-done.11.rest_12_ = bf16[192,768]{1,0:T(8,128)(2,1)S(1)} collective-permute-done((bf16[192,768]{1,0:T(8,128)(2,1)S(1)}, bf16[192,768]{1,0:T(8,128)(2,1)S(1)}, u32[]{:S(2)}, u32[]{:S(2)}) %collective-permute-start.11) | collective-permute-done | bytes 294944 | tf_op jit(solution)/shard_map/ppermute | solution.py:337
  130.3 0.0 collective-permute-done.12.rest_13_
  130.3 2.7 %gram.13.rest_15_ = f32[16,1,256]{2,1,0:T(1,128)S(1)} custom-call(f32[16,1,512]{2,1,0:T(1,128)S(1)} %get-tuple-element.56.rows_ref, f32[3072,128]{1,0:T(8,128)S(1)} %get-tuple-element.57.cover_ref, f32[3072,128]{1,0:T(8,128)S(1)} %get-tuple-element.58.which_ref, bf16[192,768]{1,0:T(8,128)(2,1)S(1)} %get-tuple-element.60.rest_0_, ...), custom_call_target="tpu_custom_call" | custom-call | flops 1585446912 | bytes 4128768 | tf_op jit(solution)/shard_map/gram/pallas_call | solution.py:351
  133.0 0.0 collective-permute-done.13.rest_14_
  133.0 1.6 %gram.14.rest_16_ = f32[16,1,256]{2,1,0:T(1,128)S(1)} custom-call(f32[16,1,512]{2,1,0:T(1,128)S(1)} %get-tuple-element.56.rows_ref, f32[3072,128]{1,0:T(8,128)S(1)} %get-tuple-element.57.cover_ref, f32[3072,128]{1,0:T(8,128)S(1)} %get-tuple-element.58.which_ref, bf16[192,768]{1,0:T(8,128)(2,1)S(1)} %get-tuple-element.60.rest_0_, ...), custom_call_target="tpu_custom_call" | custom-call | flops 849346560 | bytes 4423680 | tf_op jit(solution)/shard_map/gram/pallas_call | solution.py:351
  134.6 0.0 collective-permute-done.14.rest_15_
  134.6 1.9 %gram.15 = f32[16,1,256]{2,1,0:T(1,128)S(1)} custom-call(f32[16,1,512]{2,1,0:T(1,128)S(1)} %get-tuple-element.56.rows_ref, f32[3072,128]{1,0:T(8,128)S(1)} %get-tuple-element.57.cover_ref, f32[3072,128]{1,0:T(8,128)S(1)} %get-tuple-element.58.which_ref, bf16[192,768]{1,0:T(8,128)(2,1)S(1)} %get-tuple-element.60.rest_0_, ...), custom_call_target="tpu_custom_call" | custom-call | flops 905969664 | bytes 4718592 | tf_op jit(solution)/shard_map/gram/pallas_call | solution.py:351
  136.5 12.3 %all_to_all.11.gains_ref = f32[16,1,256]{2,1,0:T(1,128)S(1)} all-to-all(f32[16,1,256]{2,1,0:T(1,128)S(1)} %gram.15), channel_id=1, replica_groups=mesh['parts'=2,'clus'=16] {'clus'}, dimensions={0} | all-to-all | bytes 32768 | tf_op jit(solution)/shard_map/all_to_all | solution.py:359
  148.8 1.3 last.1
  (1 shorter events, 0.0 us)
Async XLA Ops:
  0.0 10.6 %copy-start.4 = (bf16[2048]{0:T(1024)(128)(2,1)S(1)}, bf16[2048]{0:T(1024)(128)(2,1)}, u32[]{:S(2)}) copy-start(bf16[2048]{0:T(1024)(128)(2,1)} %param.4) | copy-start | bytes 12292
  6.5 57.4 %collective-permute-start = (bf16[192,768]{1,0:T(8,128)(2,1)}, bf16[192,768]{1,0:T(8,128)(2,1)S(1)}, u32[]{:S(2)}, u32[]{:S(2)}) collective-permute-start(bf16[192,768]{1,0:T(8,128)(2,1)} %get-tuple-element.62), channel_id=1, source_target_pairs={{0,8},{1,9},{2,10},{3,11},{4,12},{5,13},{6,14},{7,15},{8,0},{9,1},... | collective-permute-start | bytes 884744 | tf_op jit(solution)/shard_map/ppermute | solution.py:337
  10.6 1.9 %copy-start = (bf16[2048,768]{1,0:T(8,128)(2,1)S(1)}, bf16[2048,768]{1,0:T(8,128)(2,1)}, u32[]{:S(2)}) copy-start(bf16[2048,768]{1,0:T(8,128)(2,1)} %get-tuple-element.53.unit_ref) | copy-start | bytes 9437188
  12.5 0.8 copy-start.2
  13.3 37.8 %copy-start.1 = (bf16[2048,768]{1,0:T(8,128)(2,1)S(1)}, bf16[2048,768]{1,0:T(8,128)(2,1)}, u32[]{:S(2)}) copy-start(bf16[2048,768]{1,0:T(8,128)(2,1)} %get-tuple-element.53.unit_ref) | copy-start | bytes 9437188
  13.3 37.8 %copy-start.3 = (s32[4,2048]{1,0:T(4,128)S(1)}, s32[4,2048]{1,0:T(4,128)}, u32[]{:S(2)}) copy-start(s32[4,2048]{1,0:T(4,128)} %get-tuple-element.59.where_ref) | copy-start | bytes 98308
  16.8 47.5 %collective-permute-start.2 = (bf16[192,768]{1,0:T(8,128)(2,1)S(1)}, bf16[192,768]{1,0:T(8,128)(2,1)S(1)}, u32[]{:S(2)}, u32[]{:S(2)}) collective-permute-start(bf16[192,768]{1,0:T(8,128)(2,1)S(1)} %get-tuple-element.68), channel_id=1, source_target_pairs={{0,4},{1,5},{2,6},{3,7},{4,0},{5,1},{6,2},{7,3},{8,12},{9,13},{10,... | collective-permute-start | bytes 884744 | tf_op jit(solution)/shard_map/ppermute | solution.py:337
  18.4 47.3 %collective-permute-start.1 = (bf16[192,768]{1,0:T(8,128)(2,1)S(1)}, bf16[192,768]{1,0:T(8,128)(2,1)S(1)}, u32[]{:S(2)}, u32[]{:S(2)}) collective-permute-start(bf16[192,768]{1,0:T(8,128)(2,1)S(1)} %get-tuple-element.65), channel_id=1, source_target_pairs={{0,12},{1,13},{2,14},{3,15},{4,8},{5,9},{6,10},{7,11},{8,4},{9,5},... | collective-permute-start | bytes 884744 | tf_op jit(solution)/shard_map/ppermute | solution.py:337
  18.4 50.5 %collective-permute-start.3 = (bf16[192,768]{1,0:T(8,128)(2,1)S(1)}, bf16[192,768]{1,0:T(8,128)(2,1)S(1)}, u32[]{:S(2)}, u32[]{:S(2)}) collective-permute-start(bf16[192,768]{1,0:T(8,128)(2,1)S(1)} %get-tuple-element.71), channel_id=1, source_target_pairs={{0,9},{1,8},{2,11},{3,10},{4,13},{5,12},{6,15},{7,14},{8,1},{9,0},... | collective-permute-start | bytes 884744 | tf_op jit(solution)/shard_map/ppermute | solution.py:337
  63.9 9.1 %collective-permute-start.4 = (bf16[192,768]{1,0:T(8,128)(2,1)S(1)}, bf16[192,768]{1,0:T(8,128)(2,1)S(1)}, u32[]{:S(2)}, u32[]{:S(2)}) collective-permute-start(bf16[192,768]{1,0:T(8,128)(2,1)S(1)} %get-tuple-element.74), channel_id=1, source_target_pairs={{0,5},{1,4},{2,7},{3,6},{4,1},{5,0},{6,3},{7,2},{8,13},{9,12},{10,... | collective-permute-start | bytes 884744 | tf_op jit(solution)/shard_map/ppermute | solution.py:337
  64.3 26.9 %collective-permute-start.6 = (bf16[192,768]{1,0:T(8,128)(2,1)S(1)}, bf16[192,768]{1,0:T(8,128)(2,1)S(1)}, u32[]{:S(2)}, u32[]{:S(2)}) collective-permute-start(bf16[192,768]{1,0:T(8,128)(2,1)S(1)} %get-tuple-element.80), channel_id=1, source_target_pairs={{0,6},{1,7},{2,4},{3,5},{4,2},{5,3},{6,0},{7,1},{8,14},{9,15},{10,... | collective-permute-start | bytes 884744 | tf_op jit(solution)/shard_map/ppermute | solution.py:337
  65.7 28.2 %collective-permute-start.5 = (bf16[192,768]{1,0:T(8,128)(2,1)S(1)}, bf16[192,768]{1,0:T(8,128)(2,1)S(1)}, u32[]{:S(2)}, u32[]{:S(2)}) collective-permute-start(bf16[192,768]{1,0:T(8,128)(2,1)S(1)} %get-tuple-element.77), channel_id=1, source_target_pairs={{0,13},{1,12},{2,15},{3,14},{4,9},{5,8},{6,11},{7,10},{8,5},{9,4},... | collective-permute-start | bytes 884744 | tf_op jit(solution)/shard_map/ppermute | solution.py:337
  68.9 27.9 %collective-permute-start.7 = (bf16[192,768]{1,0:T(8,128)(2,1)S(1)}, bf16[192,768]{1,0:T(8,128)(2,1)S(1)}, u32[]{:S(2)}, u32[]{:S(2)}) collective-permute-start(bf16[192,768]{1,0:T(8,128)(2,1)S(1)} %get-tuple-element.83), channel_id=1, source_target_pairs={{0,10},{1,11},{2,8},{3,9},{4,14},{5,15},{6,12},{7,13},{8,2},{9,3},... | collective-permute-start | bytes 884744 | tf_op jit(solution)/shard_map/ppermute | solution.py:337
  72.9 29.4 %collective-permute-start.8 = (bf16[192,768]{1,0:T(8,128)(2,1)S(1)}, bf16[192,768]{1,0:T(8,128)(2,1)S(1)}, u32[]{:S(2)}, u32[]{:S(2)}) collective-permute-start(bf16[192,768]{1,0:T(8,128)(2,1)S(1)} %get-tuple-element.86), channel_id=1, source_target_pairs={{0,7},{1,6},{2,5},{3,4},{4,3},{5,2},{6,1},{7,0},{8,15},{9,14},{10,... | collective-permute-start | bytes 884744 | tf_op jit(solution)/shard_map/ppermute | solution.py:337
  91.2 20.1 %collective-permute-start.10 = (bf16[192,768]{1,0:T(8,128)(2,1)S(1)}, bf16[192,768]{1,0:T(8,128)(2,1)S(1)}, u32[]{:S(2)}, u32[]{:S(2)}) collective-permute-start(bf16[192,768]{1,0:T(8,128)(2,1)S(1)} %get-tuple-element.92), channel_id=1, source_target_pairs={{0,2},{1,3},{2,0},{3,1},{4,6},{5,7},{6,4},{7,5},{8,10},{9,11},{10,... | collective-permute-start | bytes 884744 | tf_op jit(solution)/shard_map/ppermute | solution.py:337
  93.9 21.3 %collective-permute-start.9 = (bf16[192,768]{1,0:T(8,128)(2,1)S(1)}, bf16[192,768]{1,0:T(8,128)(2,1)S(1)}, u32[]{:S(2)}, u32[]{:S(2)}) collective-permute-start(bf16[192,768]{1,0:T(8,128)(2,1)S(1)} %get-tuple-element.89), channel_id=1, source_target_pairs={{0,14},{1,15},{2,12},{3,13},{4,10},{5,11},{6,8},{7,9},{8,6},{9,7},... | collective-permute-start | bytes 884744 | tf_op jit(solution)/shard_map/ppermute | solution.py:337
  96.8 33.5 %collective-permute-start.11 = (bf16[192,768]{1,0:T(8,128)(2,1)S(1)}, bf16[192,768]{1,0:T(8,128)(2,1)S(1)}, u32[]{:S(2)}, u32[]{:S(2)}) collective-permute-start(bf16[192,768]{1,0:T(8,128)(2,1)S(1)} %get-tuple-element.94), channel_id=1, source_target_pairs={{0,11},{1,10},{2,9},{3,8},{4,15},{5,14},{6,13},{7,12},{8,3},{9,2},... | collective-permute-start | bytes 884744 | tf_op jit(solution)/shard_map/ppermute | solution.py:337
  102.4 27.9 %collective-permute-start.12 = (bf16[192,768]{1,0:T(8,128)(2,1)S(1)}, bf16[192,768]{1,0:T(8,128)(2,1)S(1)}, u32[]{:S(2)}, u32[]{:S(2)}) collective-permute-start(bf16[192,768]{1,0:T(8,128)(2,1)S(1)} %get-tuple-element.95), channel_id=1, source_target_pairs={{0,3},{1,2},{2,1},{3,0},{4,7},{5,6},{6,5},{7,4},{8,11},{9,10},{10,... | collective-permute-start | bytes 884744 | tf_op jit(solution)/shard_map/ppermute | solution.py:337
  111.3 23.3 %collective-permute-start.14 = (bf16[192,768]{1,0:T(8,128)(2,1)S(1)}, bf16[192,768]{1,0:T(8,128)(2,1)S(1)}, u32[]{:S(2)}, u32[]{:S(2)}) collective-permute-start(bf16[192,768]{1,0:T(8,128)(2,1)S(1)} %get-tuple-element.97), channel_id=1, source_target_pairs={{0,15},{1,14},{2,13},{3,12},{4,11},{5,10},{6,9},{7,8},{8,7},{9,6},... | collective-permute-start | bytes 884744 | tf_op jit(solution)/shard_map/ppermute | solution.py:337
  115.2 17.8 %collective-permute-start.13 = (bf16[192,768]{1,0:T(8,128)(2,1)S(1)}, bf16[192,768]{1,0:T(8,128)(2,1)S(1)}, u32[]{:S(2)}, u32[]{:S(2)}) collective-permute-start(bf16[192,768]{1,0:T(8,128)(2,1)S(1)} %get-tuple-element.96), channel_id=1, source_target_pairs={{0,1},{1,0},{2,3},{3,2},{4,5},{5,4},{6,7},{7,6},{8,9},{9,8},{10,11... | collective-permute-start | bytes 884744 | tf_op jit(solution)/shard_map/ppermute | solution.py:337

commit v5 on v4

v5 whole, which is shorter than its diff:
```python
import jax
import jax.numpy as jnp
from jax import lax
from jax.experimental import pallas as pl
from jax.experimental.pallas import tpu as pltpu
from jax.sharding import PartitionSpec as P

CL_DEV = 4
PARTS = 3
TAIL = 16
EARLY = 1
DEPTH = 4
STOPS = (4, 6, 8, 10, 12, 14, 15, 16)
MIB = 1024 * 1024

NN = (((1,), (0,)), ((), ()))
NT = (((1,), (1,)), ((), ()))


def dot(left, right, dims):
    return lax.dot_general(left, right, dims, preferred_element_type=jnp.float32)


def lanes(n):
    return -(-n // 128) * 128


def hot(values, count, first=0):
    index = lax.broadcasted_iota(jnp.int32, (count, values.shape[1]), 0) + first
    return jnp.where(index == values, 1.0, 0.0).astype(jnp.bfloat16)


def place(ids, devices, cap):
    rows = ids.shape[1]
    clusters = CL_DEV * devices
    step = 256
    onehot = hot(ids, clusters)
    before = lax.broadcasted_iota(jnp.int32, (step, step), 0) < lax.broadcasted_iota(
        jnp.int32, (step, step), 1
    )
    before = jnp.where(before, 1.0, 0.0).astype(jnp.bfloat16)
    count = jnp.zeros((clusters, 1), jnp.float32)
    ranks = []
    for start in range(0, rows, step):
        piece = onehot[:, start : start + step]
        ranks.append(dot(piece, before, NN) + count)
        count = count + jnp.sum(piece.astype(jnp.float32), axis=1, keepdims=True)
    k = lax.broadcasted_iota(jnp.int32, (clusters, clusters), 0)
    m = lax.broadcasted_iota(jnp.int32, (clusters, clusters), 1)
    j = k % CL_DEV
    plus = (j == 1) & (m == k - 1)
    minus = ((j == 2) & ((m == k) | (m == k + 1))) | ((j == 3) & (m == k))
    mix = (jnp.where(plus, 1.0, 0.0) - jnp.where(minus, 1.0, 0.0)).astype(jnp.bfloat16)
    spread = jnp.broadcast_to(count, (clusters, 128)).astype(jnp.bfloat16)
    base = dot(mix, spread, NN)[:, :1]
    jcol = lax.broadcasted_iota(jnp.int32, (clusters, 1), 0) % CL_DEV
    base = base + jnp.where(jcol >= 2, float(PARTS * cap), 0.0)
    position = []
    for i, start in enumerate(range(0, rows, step)):
        piece = onehot[:, start : start + step].astype(jnp.float32)
        position.append(jnp.sum(piece * (ranks[i] + base), axis=0, keepdims=True))
    return jnp.concatenate(position, axis=1).astype(jnp.int32)


def first_kernel(devices, cap, steps, offsets):
    seg = PARTS * cap
    wide = lanes(seg)

    def kernel(ids_ref, cover_ref, emb_ref, unit_ref, where_ref, meta_ref, *rest):
        count = len(offsets)
        outs, scratch = rest[:count], rest[count:]
        raw_ref, rows_ref, piece_ref, in_sems, rows_sems, out_sems = scratch
        me = lax.axis_index("clus")
        block = raw_ref.shape[0] // steps

        def load(i):
            part = pl.ds(i * block, block)
            return pltpu.make_async_copy(emb_ref.at[part], raw_ref.at[part], in_sems.at[i])

        def store(i):
            part = pl.ds(i * block, block)
            return pltpu.make_async_copy(rows_ref.at[part], unit_ref.at[part], rows_sems.at[i])

        for i in range(steps):
            load(i).start()
        ids = ids_ref[...]
        owner = ids // CL_DEV
        position = place(ids, devices, cap)
        code = owner * seg + position
        where_ref[0:1, :] = code
        where_ref[1:2, :] = owner
        where_ref[2:3, :] = position
        own = hot(owner, devices)
        there = hot(position, wide)
        cover = cover_ref[...].astype(jnp.float32)
        cover = jnp.concatenate([cover[i : i + 1] for i in range(cover.shape[0])], axis=1)
        which = (ids - owner * CL_DEV).astype(jnp.float32)
        meta_ref[:, 0, :wide] = dot(own * cover.astype(jnp.bfloat16), there, NT)
        meta_ref[:, 0, wide:] = dot(own * which.astype(jnp.bfloat16), there, NT)
        for i in range(steps):
            load(i).wait()
            raw = raw_ref[i * block : (i + 1) * block, :]
            sums = jnp.sum(raw * raw, axis=-1, keepdims=True)
            unit = (raw * lax.rsqrt(sums + 1e-06)).astype(jnp.bfloat16)
            rows_ref[i * block : (i + 1) * block, :] = unit
            store(i).start()
        send_pieces(code, rows_ref, meta_ref, seg, me, offsets, outs, piece_ref, out_sems)
        for i in range(steps):
            store(i).wait()

    return kernel


def send_pieces(code, unit_ref, meta_ref, seg, me, offsets, outs, piece_ref, sems):
    copies = []
    slabs = unit_ref.shape[1] // 128
    index = lax.broadcasted_iota(jnp.int32, (TAIL, 128), 0)
    for i, (k, out_ref) in enumerate(zip(offsets, outs)):
        pick = hot(code, seg, (me ^ k) * seg)
        found = dot(pick, unit_ref[...], NN).astype(jnp.bfloat16)
        for f in range(slabs):
            piece_ref[i, f * seg : (f + 1) * seg, :] = found[:, f * 128 : (f + 1) * 128]
        row = meta_ref[me ^ k]
        tail = jnp.zeros((TAIL, 128), jnp.float32)
        for j in range(row.shape[1] // 128):
            tail = jnp.where(index == j, row[:, j * 128 : (j + 1) * 128], tail)
        piece_ref[i, slabs * seg :, :] = tail.astype(jnp.bfloat16)
        copies.append(pltpu.make_async_copy(piece_ref.at[i], out_ref, sems.at[i]))
        copies[-1].start()
    for copy in copies:
        copy.wait()


def rest_kernel(devices, cap, offsets):
    seg = PARTS * cap

    def kernel(where_ref, meta_ref, unit_ref, *rest):
        outs, (piece_ref, sems) = rest[: len(offsets)], rest[len(offsets) :]
        me = lax.axis_index("clus")
        send_pieces(where_ref[0:1, :], unit_ref, meta_ref, seg, me, offsets, outs, piece_ref, sems)

    return kernel


def column(row):
    return jnp.transpose(jnp.broadcast_to(row, (128, row.shape[1])))


def pad_rows(piece, count):
    if piece.shape[0] == count:
        return piece
    fill = jnp.zeros((count - piece.shape[0], piece.shape[1]), piece.dtype)
    return jnp.concatenate([piece, fill], axis=0)


def repeat(col, n):
    return jnp.concatenate([col] * (n // 128), axis=1)


def gram_kernel(devices, cap, offsets, stops, which_stop):
    seg = PARTS * cap
    wide = lanes(seg)
    per_tile = max(1, 768 // seg)
    done = stops[which_stop - 1] if which_stop else 0
    new = stops[which_stop]
    xs = list(range(done, new))
    n = len(xs) * wide
    final = new == devices

    def kernel(*refs):
        pieces, refs = refs[:new], refs[new:]
        old_cols, refs = refs[:which_stop], refs[which_stop:]
        if which_stop:
            gains_ref, refs = refs[0], refs[1:]
        out_ref = refs[0]
        slabs = (pieces[0].shape[0] - TAIL) // seg

        def rows_of(p):
            return jnp.concatenate([pieces[p][f * seg : (f + 1) * seg, :] for f in range(slabs)], axis=1)

        def meta_of(p):
            tail = pieces[p][slabs * seg :, :].astype(jnp.float32)
            parts = [tail[j : j + 1] for j in range(2 * wide // 128)]
            half = len(parts) // 2
            return jnp.concatenate(parts[:half], axis=1), jnp.concatenate(parts[half:], axis=1)

        metas = [meta_of(p) for p in xs]
        right = jnp.concatenate([pad_rows(rows_of(p), wide) for p in xs], axis=0)
        right_cover = jnp.concatenate([m[0] for m in metas], axis=1)
        right_which = jnp.concatenate([m[1] for m in metas], axis=1)
        lane = lax.broadcasted_iota(jnp.int32, (1, wide), 1)
        inside = jnp.concatenate([lane < seg] * len(xs), axis=1)
        right_which = jnp.where(inside, right_which, -1.0)
        cover_cols, which_cols = {}, {}
        first = 0
        for g in range(which_stop):
            for p in range(first, stops[g]):
                part = slice((p - first) * seg, (p - first + 1) * seg)
                cover_cols[p] = old_cols[g][part, :128]
                which_cols[p] = old_cols[g][part, 128:]
            first = stops[g]
        for i, p in enumerate(xs):
            cover_cols[p] = column(metas[i][0])[:seg]
            which_cols[p] = column(metas[i][1])[:seg]
            if not final:
                refs[1][i * seg : (i + 1) * seg, :128] = cover_cols[p]
                refs[1][i * seg : (i + 1) * seg, 128:] = which_cols[p]
        down = jnp.zeros((8, n), jnp.float32)
        total = {}
        for start in range(0, new, per_tile):
            members = range(start, min(start + per_tile, new))
            left = jnp.concatenate([rows_of(p) for p in members], axis=0)
            similar = dot(left, right, NT)
            count = len(members) * seg
            which = jnp.concatenate([which_cols[p] for p in members], axis=0)
            cover = jnp.concatenate([cover_cols[p] for p in members], axis=0)
            similar = jnp.where(repeat(which, n) == right_which, similar, -1e30)
            gain = jnp.maximum(similar - repeat(cover, n), 0.0)
            down = down + jnp.sum(gain.reshape(count // 8, 8, n), axis=0)
            old = [p for p in members if p < done]
            if not old:
                continue
            other = jnp.maximum(similar[: len(old) * seg] - right_cover, 0.0)
            part = other[:, :128]
            for begin in range(128, n, 128):
                part = part + other[:, begin : begin + 128]
            for i, p in enumerate(old):
                mine = pad_rows(part[i * seg : (i + 1) * seg], wide)
                total[p] = jnp.sum(jnp.transpose(mine), axis=0, keepdims=True)
        down = jnp.sum(down, axis=0, keepdims=True)
        for i, p in enumerate(xs):
            total[p] = down[:, i * wide : (i + 1) * wide]
        me = lax.axis_index("clus")
        for p in range(new):
            value = total[p]
            if p < done:
                value = value + gains_ref[p]
            if final:
                out_ref[me ^ offsets[p]] = value
            else:
                out_ref[p] = value

    return kernel


def last_kernel(kernel_devices):
    def kernel(where_ref, gains_ref, out_ref):
        gains = gains_ref[:, 0, :]
        high = gains.astype(jnp.bfloat16)
        rest = gains - high.astype(jnp.float32)
        mid = rest.astype(jnp.bfloat16)
        low = (rest - mid.astype(jnp.float32)).astype(jnp.bfloat16)
        there = hot(where_ref[2:3, :], gains.shape[1])
        found = dot(high, there, NN) + dot(mid, there, NN) + dot(low, there, NN)
        index = lax.broadcasted_iota(jnp.int32, found.shape, 0)
        mine = jnp.where(index == where_ref[1:2, :], found, 0.0)
        out_ref[...] = jnp.sum(mine, axis=0, keepdims=True)

    return kernel


def call(kernel, outs, cost, name, vmem=24, **extra):
    return pl.pallas_call(
        kernel,
        out_shape=outs,
        compiler_params=pltpu.CompilerParams(vmem_limit_bytes=vmem * MIB),
        cost_estimate=pl.CostEstimate(flops=cost[0], bytes_accessed=cost[1], transcendentals=0),
        name=name,
        **extra,
    )


def sequence(devices):
    half = devices // 2
    quarter = max(1, half // 2)
    far = []
    for i in range(quarter):
        far += [half + i, half + quarter + i]
    near = sorted(range(1, half), key=lambda k: (-k.bit_length(), k))
    order = [0, far[0]]
    for i in range(half - 2):
        order += [far[i + 1], near[i]]
    return order + [near[-1], far[-1]]


def body(embeddings, coverage, cluster_ids):
    devices = lax.axis_size("clus")
    rows, width = embeddings.shape
    cap = 2 * rows // (CL_DEV * devices)
    seg = PARTS * cap
    wide = lanes(seg)
    offsets = sequence(devices)
    f32, bf16 = jnp.float32, jnp.bfloat16
    S = jax.ShapeDtypeStruct
    ids = cluster_ids.reshape(1, rows)
    cover = coverage.reshape(rows // 128, 128)
    unitg = devices // 16
    early = EARLY * unitg
    depth = DEPTH * unitg
    tall = width // 128 * seg + TAIL
    piece = S((tall, 128), bf16)

    def pieces_of(count):
        return dict(
            out_specs=[pl.BlockSpec(memory_space=pltpu.HBM)] * count,
            scratch_shapes=[pltpu.VMEM((count, tall, 128), bf16), pltpu.SemaphoreType.DMA((count,))],
        )

    full = pl.BlockSpec(memory_space=pltpu.VMEM)
    hbm = pl.BlockSpec(memory_space=pltpu.HBM)
    steps = 8
    lead = pieces_of(early)
    unit, where, meta, *sent = call(
        first_kernel(devices, cap, steps, offsets[1 : 1 + early]),
        [S((rows, width), bf16), S((3, rows), jnp.int32), S((devices, 1, 2 * wide), f32)] + [piece] * early,
        (2 * early * seg * rows * width, 4 * rows * width),
        "first",
        in_specs=[full, full, hbm],
        out_specs=[hbm, full, full] + lead["out_specs"],
        scratch_shapes=[pltpu.VMEM((rows, width), f32), pltpu.VMEM((rows, width), bf16)]
        + [lead["scratch_shapes"][0], pltpu.SemaphoreType.DMA((steps,))]
        + [pltpu.SemaphoreType.DMA((steps,)), lead["scratch_shapes"][1]],
        vmem=56,
    )(ids, cover, embeddings)
    for name, ks in (("second", offsets[1 + early : 1 + depth]), ("rest", offsets[1 + depth :] + [0])):
        sent += call(
            rest_kernel(devices, cap, ks),
            [piece] * len(ks),
            (0, 0),
            name,
            in_specs=[full] * 3,
            vmem=20,
            **pieces_of(len(ks)),
        )(where, meta, unit)
    own = sent.pop()

    got = []
    for i, x in enumerate(sent):
        if i >= depth:
            x, got[i - depth] = lax.optimization_barrier((x, got[i - depth]))
        got.append(lax.ppermute(x, "clus", [(d, d ^ offsets[1 + i]) for d in range(devices)]))
    pieces = [own] + got

    gain_shape = S((devices, 1, wide), f32)
    stops = [stop * unitg for stop in STOPS]
    cols, gains = [], []
    for g, new in enumerate(stops):
        fresh = new - (stops[g - 1] if g else 0)
        gains, *more = call(
            gram_kernel(devices, cap, offsets, stops, g),
            [gain_shape] + [S((fresh * seg, 256), f32)] * (new < devices),
            (2 * new * seg * fresh * seg * width, 2 * new * seg * width),
            "gram",
            vmem=16,
        )(*pieces[:new], *cols, *([gains] if g else []))
        cols += more
    back = lax.all_to_all(gains, "clus", 0, 0, tiled=True)
    out = call(last_kernel(devices), S((1, rows), f32), (2 * rows * wide * 48, 8 * rows), "last")(where, back)
    return out.reshape(rows)


def solution(mesh):
    placed = (P(("parts", "clus"), None), P(("parts", "clus")), P(("parts", "clus"), None))
    return jax.shard_map(
        body, mesh=mesh, in_specs=placed, out_specs=P(("parts", "clus")), check_vma=False
    )
```

time: 150 us -> 129 us (0.86)
  blocking collectives: 44.4 us -> 13.1 us
  starting transfers between devices: 20.2 us -> 25.3 us
  waiting for transfers between devices: 42.6 us -> 47.1 us
    all_to_all x1 -> x0, blocking collectives: 32.1 us -> none  [body(): met = lax.all_to_all(meta, 'clus', 0, 0, tiled=True)]
    ppermute x15, starting transfers between devices: 20.2 us -> 25.3 us  [body(): lax.ppermute(x, 'clus', [(d, d ^ offsets[1 + i]) for d in range(devices)])]
    ppermute x15, waiting for transfers between devices: 42.6 us -> 47.1 us  [body(): lax.ppermute(x, 'clus', [(d, d ^ offsets[1 + i]) for d in range(devices)])]
    unnamed x10 -> x8, local copies, waits for them, and re-layouts: 2.66 us -> 3.41 us
    pallas_call x11 -> x10, Pallas kernels: 32.3 us -> 31.8 us  [the longest x2 16.1 us: body(): call(rest_kernel(devices, cap, ks), [piece] * len(ks), (0, 0), name, in_s...]
  transfers between devices with their start and end apart: 15 -> 15, of which waited for: 5 -> 6; matrix products, arithmetic and copies ran while one was open for 0% -> 0% of each run, Pallas kernels for 20% -> 23%
where the time goes in v5:
time: 129 us
  waiting for transfers between devices  47.1 us (37%)
  Pallas kernels  39.9 us (31%)
  starting transfers between devices  25.3 us (20%)
  blocking collectives  13.1 us (10%)
  local copies, waits for them, and re-layouts  3.41 us (3%)
    ppermute x15, waiting for transfers between devices, body(): lax.ppermute(x, 'clus', [(d, d ^ offsets[1 + i]) for d in range(devices)])  47.1 us
    ppermute x15, starting transfers between devices, body(): lax.ppermute(x, 'clus', [(d, d ^ offsets[1 + i]) for d in range(devices)])  25.3 us
    pallas_call x2, Pallas kernels, body(): call(rest_kernel(devices, cap, ks), [piece] * len(ks), (0, 0), name, in_s...  16.1 us
    pallas_call x8, Pallas kernels, body(): call(gram_kernel(devices, cap, offsets, stops, g), [gain_shape] + [S((fre...  15.7 us
    all_to_all x1, blocking collectives, body(): back = lax.all_to_all(gains, 'clus', 0, 0, tiled=True)  13.1 us
    pallas_call x1, Pallas kernels, body(): call(first_kernel(devices, cap, steps, offsets[1:1 + early]), [S((rows, w...  6.84 us
    unnamed x8, local copies, waits for them, and re-layouts  3.41 us
  transfers between devices with their start and end apart: 15, of which 6 were waited for; matrix products, arithmetic and copies ran while one was open for 0% of the time, Pallas kernels for 23%

profile of v5, /device:TPU:0, one launch (start us, length us, event | category | flops | bytes accessed | tf_op | source)
XLA Modules:
  0.0 128.9 jit_solution(3959191103602916795)
XLA Ops:
  0.0 6.8 %first.1 = (bf16[2048,768]{1,0:T(8,128)(2,1)}, s32[3,2048]{1,0:T(4,128)}, f32[16,1,512]{2,1,0:T(1,128)}, bf16[1168,128]{1,0:T(8,128)(2,1)}) custom-call(s32[1,2048]{1,0:T(1,128)} %bitcast.3, bf16[16,128]{1,0:T(8,128)(2,1)} %bitcast.4, f32[2048,768]{1,0:T(8,128)} %emb_ref.1), custom_call_target="tpu_custom_call" | custom-call | flops 603979776 | bytes 6291456 | tf_op jit(solution)/shard_map/first/pallas_call | solution.py:313
  6.8 4.1 %collective-permute-start = (bf16[1168,128]{1,0:T(8,128)(2,1)}, bf16[1168,128]{1,0:T(8,128)(2,1)S(1)}, u32[]{:S(2)}, u32[]{:S(2)}) collective-permute-start(bf16[1168,128]{1,0:T(8,128)(2,1)} %get-tuple-element.65), channel_id=1, source_target_pairs={{0,8},{1,9},{2,10},{3,11},{4,12},{5,13},{6,14},{7,15},{8,0},{9,1},... | collective-permute-start | bytes 897032 | tf_op jit(solution)/shard_map/ppermute | solution.py:341
  10.9 0.0 copy-start
  10.9 1.9 %copy-done = bf16[2048,768]{1,0:T(8,128)(2,1)S(1)} copy-done((bf16[2048,768]{1,0:T(8,128)(2,1)S(1)}, bf16[2048,768]{1,0:T(8,128)(2,1)}, u32[]{:S(2)}) %copy-start) | copy-done | bytes 3145752
  12.8 0.0 copy-start.1
  12.8 0.8 copy-done.1
  13.6 0.0 copy-start.3
  13.6 0.8 copy-done.3
  14.4 3.2 %second.1 = (bf16[1168,128]{1,0:T(8,128)(2,1)S(1)}, bf16[1168,128]{1,0:T(8,128)(2,1)S(1)}, bf16[1168,128]{1,0:T(8,128)(2,1)S(1)}) custom-call(s32[3,2048]{1,0:T(4,128)S(1)} %copy-done.1, f32[16,1,512]{2,1,0:T(1,128)S(1)} %copy-done.3, bf16[2048,768]{1,0:T(8,128)(2,1)S(1)} %copy-done), custom_call_target="tpu_custom_call" | custom-call | tf_op jit(solution)/shard_map/second/pallas_call | solution.py:326
  17.5 1.6 %collective-permute-start.2 = (bf16[1168,128]{1,0:T(8,128)(2,1)S(1)}, bf16[1168,128]{1,0:T(8,128)(2,1)S(1)}, u32[]{:S(2)}, u32[]{:S(2)}) collective-permute-start(bf16[1168,128]{1,0:T(8,128)(2,1)S(1)} %get-tuple-element.71), channel_id=1, source_target_pairs={{0,4},{1,5},{2,6},{3,7},{4,0},{5,1},{6,2},{7,3},{8,12},{9,13},{10,... | collective-permute-start | bytes 897032 | tf_op jit(solution)/shard_map/ppermute | solution.py:341
  19.2 0.0 collective-permute-start.1
  19.2 0.5 collective-permute-start.3
  19.7 13.0 %rest.1 = (bf16[1168,128]{1,0:T(8,128)(2,1)S(1)}, bf16[1168,128]{1,0:T(8,128)(2,1)S(1)}, bf16[1168,128]{1,0:T(8,128)(2,1)S(1)}, bf16[1168,128]{1,0:T(8,128)(2,1)...) custom-call(s32[3,2048]{1,0:T(4,128)S(1)} %copy-done.1, ...), custom_call_target="tpu_custom_call" | custom-call | tf_op jit(solution)/shard_map/rest/pallas_call | solution.py:326
  32.7 0.0 collective-permute-done.refs_1_
  32.7 3.7 %collective-permute-start.4 = (bf16[1168,128]{1,0:T(8,128)(2,1)S(1)}, bf16[1168,128]{1,0:T(8,128)(2,1)S(1)}, u32[]{:S(2)}, u32[]{:S(2)}) collective-permute-start(bf16[1168,128]{1,0:T(8,128)(2,1)S(1)} %get-tuple-element.77), channel_id=1, source_target_pairs={{0,5},{1,4},{2,7},{3,6},{4,1},{5,0},{6,3},{7,2},{8,13},{9,12},{10,... | collective-permute-start | bytes 897032 | tf_op jit(solution)/shard_map/ppermute | solution.py:341
  36.3 1.2 collective-permute-done.2.refs_3_
  37.5 0.6 collective-permute-start.6
  38.0 0.0 collective-permute-done.1.refs_2_
  38.0 1.2 collective-permute-start.5
  39.2 10.4 %collective-permute-done.3.refs_4_ = bf16[1168,128]{1,0:T(8,128)(2,1)S(1)} collective-permute-done((bf16[1168,128]{1,0:T(8,128)(2,1)S(1)}, bf16[1168,128]{1,0:T(8,128)(2,1)S(1)}, u32[]{:S(2)}, u32[]{:S(2)}) %collective-permute-start.3) | collective-permute-done | bytes 299040 | tf_op jit(solution)/shard_map/ppermute | solution.py:341
  49.6 3.4 %collective-permute-start.7 = (bf16[1168,128]{1,0:T(8,128)(2,1)S(1)}, bf16[1168,128]{1,0:T(8,128)(2,1)S(1)}, u32[]{:S(2)}, u32[]{:S(2)}) collective-permute-start(bf16[1168,128]{1,0:T(8,128)(2,1)S(1)} %get-tuple-element.86), channel_id=1, source_target_pairs={{0,10},{1,11},{2,8},{3,9},{4,14},{5,15},{6,12},{7,13},{8,2},{9,3},... | collective-permute-start | bytes 897032 | tf_op jit(solution)/shard_map/ppermute | solution.py:341
  53.0 0.0 collective-permute-done.4.refs_5_
  53.0 2.2 %collective-permute-start.8 = (bf16[1168,128]{1,0:T(8,128)(2,1)S(1)}, bf16[1168,128]{1,0:T(8,128)(2,1)S(1)}, u32[]{:S(2)}, u32[]{:S(2)}) collective-permute-start(bf16[1168,128]{1,0:T(8,128)(2,1)S(1)} %get-tuple-element.89), channel_id=1, source_target_pairs={{0,7},{1,6},{2,5},{3,4},{4,3},{5,2},{6,1},{7,0},{8,15},{9,14},{10,... | collective-permute-start | bytes 897032 | tf_op jit(solution)/shard_map/ppermute | solution.py:341
  55.2 8.8 %collective-permute-done.6.refs_7_ = bf16[1168,128]{1,0:T(8,128)(2,1)S(1)} collective-permute-done((bf16[1168,128]{1,0:T(8,128)(2,1)S(1)}, bf16[1168,128]{1,0:T(8,128)(2,1)S(1)}, u32[]{:S(2)}, u32[]{:S(2)}) %collective-permute-start.6) | collective-permute-done | bytes 299040 | tf_op jit(solution)/shard_map/ppermute | solution.py:341
  64.0 0.4 collective-permute-start.10
  64.4 0.0 collective-permute-done.5.refs_6_
  64.4 4.8 %collective-permute-start.9 = (bf16[1168,128]{1,0:T(8,128)(2,1)S(1)}, bf16[1168,128]{1,0:T(8,128)(2,1)S(1)}, u32[]{:S(2)}, u32[]{:S(2)}) collective-permute-start(bf16[1168,128]{1,0:T(8,128)(2,1)S(1)} %get-tuple-element.92), channel_id=1, source_target_pairs={{0,14},{1,15},{2,12},{3,13},{4,10},{5,11},{6,8},{7,9},{8,6},{9,7},... | collective-permute-start | bytes 897032 | tf_op jit(solution)/shard_map/ppermute | solution.py:341
  69.2 1.5 %gram.8 = (f32[16,1,256]{2,1,0:T(1,128)S(1)}, f32[768,256]{1,0:T(8,128)S(1)}) custom-call(bf16[1168,128]{1,0:T(8,128)(2,1)S(1)} %get-tuple-element.63.refs_0_, bf16[1168,128]{1,0:T(8,128)(2,1)S(1)} %collective-permute-done.refs_1_, bf16[1168,128]{1,0:T(8,128)(2,1)S(1)} %collective-permute-done.1.refs_2_, bf16[1168,128]{1,0:T(8,128)(2,1)S(1)} %collective-permute-done.2.refs_3_), custom_call_target="tpu_custom_call" | custom-call | flops 905969664 | bytes 1179648 | tf_op jit(solution)/shard_map/gram/pallas_call | solution.py:349
  70.7 13.8 %collective-permute-done.7.refs_8_ = bf16[1168,128]{1,0:T(8,128)(2,1)S(1)} collective-permute-done((bf16[1168,128]{1,0:T(8,128)(2,1)S(1)}, bf16[1168,128]{1,0:T(8,128)(2,1)S(1)}, u32[]{:S(2)}, u32[]{:S(2)}) %collective-permute-start.7) | collective-permute-done | bytes 299040 | tf_op jit(solution)/shard_map/ppermute | solution.py:341
  84.5 0.0 collective-permute-start.11
  84.6 1.3 %gram.9 = (f32[16,1,256]{2,1,0:T(1,128)S(1)}, f32[384,256]{1,0:T(8,128)S(1)}) custom-call(bf16[1168,128]{1,0:T(8,128)(2,1)S(1)} %get-tuple-element.63.refs_0_, bf16[1168,128]{1,0:T(8,128)(2,1)S(1)} %collective-permute-done.refs_1_, bf16[1168,128]{1,0:T(8,128)(2,1)S(1)} %collective-permute-done.1.refs_2_, ...), custom_call_target="tpu_custom_call" | custom-call | flops 679477248 | bytes 1769472 | tf_op jit(solution)/shard_map/gram/pallas_call | solution.py:349
  85.9 0.0 collective-permute-done.8.refs_9_
  85.9 0.1 collective-permute-start.12
  85.9 1.7 %gram.10 = (f32[16,1,256]{2,1,0:T(1,128)S(1)}, f32[384,256]{1,0:T(8,128)S(1)}) custom-call(bf16[1168,128]{1,0:T(8,128)(2,1)S(1)} %get-tuple-element.63.refs_0_, bf16[1168,128]{1,0:T(8,128)(2,1)S(1)} %collective-permute-done.refs_1_, bf16[1168,128]{1,0:T(8,128)(2,1)S(1)} %collective-permute-done.1.refs_2_, ...), custom_call_target="tpu_custom_call" | custom-call | flops 905969664 | bytes 2359296 | tf_op jit(solution)/shard_map/gram/pallas_call | solution.py:349
  87.7 2.1 %collective-permute-done.10.refs_11_ = bf16[1168,128]{1,0:T(8,128)(2,1)S(1)} collective-permute-done((bf16[1168,128]{1,0:T(8,128)(2,1)S(1)}, bf16[1168,128]{1,0:T(8,128)(2,1)S(1)}, u32[]{:S(2)}, u32[]{:S(2)}) %collective-permute-start.10) | collective-permute-done | bytes 299040 | tf_op jit(solution)/shard_map/ppermute | solution.py:341
  89.8 2.2 %collective-permute-start.14 = (bf16[1168,128]{1,0:T(8,128)(2,1)S(1)}, bf16[1168,128]{1,0:T(8,128)(2,1)S(1)}, u32[]{:S(2)}, u32[]{:S(2)}) collective-permute-start(bf16[1168,128]{1,0:T(8,128)(2,1)S(1)} %get-tuple-element.100), channel_id=1, source_target_pairs={{0,15},{1,14},{2,13},{3,12},{4,11},{5,10},{6,9},{7,8},{8,7},{9,6},... | collective-permute-start | bytes 897032 | tf_op jit(solution)/shard_map/ppermute | solution.py:341
  92.0 0.0 collective-permute-done.9.refs_10_
  92.0 0.6 collective-permute-start.13
  92.6 2.1 %gram.11 = (f32[16,1,256]{2,1,0:T(1,128)S(1)}, f32[384,256]{1,0:T(8,128)S(1)}) custom-call(bf16[1168,128]{1,0:T(8,128)(2,1)S(1)} %get-tuple-element.63.refs_0_, bf16[1168,128]{1,0:T(8,128)(2,1)S(1)} %collective-permute-done.refs_1_, bf16[1168,128]{1,0:T(8,128)(2,1)S(1)} %collective-permute-done.1.refs_2_, ...), custom_call_target="tpu_custom_call" | custom-call | flops 1132462080 | bytes 2949120 | tf_op jit(solution)/shard_map/gram/pallas_call | solution.py:349
  94.7 2.5 %gram.12 = (f32[16,1,256]{2,1,0:T(1,128)S(1)}, f32[384,256]{1,0:T(8,128)S(1)}) custom-call(bf16[1168,128]{1,0:T(8,128)(2,1)S(1)} %get-tuple-element.63.refs_0_, bf16[1168,128]{1,0:T(8,128)(2,1)S(1)} %collective-permute-done.refs_1_, bf16[1168,128]{1,0:T(8,128)(2,1)S(1)} %collective-permute-done.1.refs_2_, ...), custom_call_target="tpu_custom_call" | custom-call | flops 1358954496 | bytes 3538944 | tf_op jit(solution)/shard_map/gram/pallas_call | solution.py:349
  97.2 10.8 %collective-permute-done.11.refs_12_ = bf16[1168,128]{1,0:T(8,128)(2,1)S(1)} collective-permute-done((bf16[1168,128]{1,0:T(8,128)(2,1)S(1)}, bf16[1168,128]{1,0:T(8,128)(2,1)S(1)}, u32[]{:S(2)}, u32[]{:S(2)}) %collective-permute-start.11) | collective-permute-done | bytes 299040 | tf_op jit(solution)/shard_map/ppermute | solution.py:341
  108.0 0.0 collective-permute-done.12.refs_13_
  108.0 2.9 %gram.13 = (f32[16,1,256]{2,1,0:T(1,128)S(1)}, f32[384,256]{1,0:T(8,128)S(1)}) custom-call(bf16[1168,128]{1,0:T(8,128)(2,1)S(1)} %get-tuple-element.63.refs_0_, bf16[1168,128]{1,0:T(8,128)(2,1)S(1)} %collective-permute-done.refs_1_, bf16[1168,128]{1,0:T(8,128)(2,1)S(1)} %collective-permute-done.1.refs_2_, ...), custom_call_target="tpu_custom_call" | custom-call | flops 1585446912 | bytes 4128768 | tf_op jit(solution)/shard_map/gram/pallas_call | solution.py:349
  110.9 0.0 collective-permute-done.13.refs_14_
  110.9 0.0 copy-start.2
  110.9 1.7 %gram.14 = (f32[16,1,256]{2,1,0:T(1,128)S(1)}, f32[192,256]{1,0:T(8,128)S(1)}) custom-call(bf16[1168,128]{1,0:T(8,128)(2,1)S(1)} %get-tuple-element.63.refs_0_, bf16[1168,128]{1,0:T(8,128)(2,1)S(1)} %collective-permute-done.refs_1_, bf16[1168,128]{1,0:T(8,128)(2,1)S(1)} %collective-permute-done.1.refs_2_, ...), custom_call_target="tpu_custom_call" | custom-call | flops 849346560 | bytes 4423680 | tf_op jit(solution)/shard_map/gram/pallas_call | solution.py:349
  112.6 0.0 collective-permute-done.14.refs_15_
  112.6 1.9 %gram.15 = f32[16,1,256]{2,1,0:T(1,128)S(1)} custom-call(bf16[1168,128]{1,0:T(8,128)(2,1)S(1)} %get-tuple-element.63.refs_0_, bf16[1168,128]{1,0:T(8,128)(2,1)S(1)} %collective-permute-done.refs_1_, bf16[1168,128]{1,0:T(8,128)(2,1)S(1)} %collective-permute-done.1.refs_2_, bf16[1168,128]{1,0:T(8,128)(2,1)S(1)} %collective-permute-done.2.refs_3_, ...), custom_call_target="tpu_custom_call" | custom-call | flops 905969664 | bytes 4718592 | tf_op jit(solution)/shard_map/gram/pallas_call | solution.py:349
  114.5 13.1 %all_to_all.5.gains_ref = f32[16,1,256]{2,1,0:T(1,128)S(1)} all-to-all(f32[16,1,256]{2,1,0:T(1,128)S(1)} %gram.15), channel_id=1, replica_groups=mesh['parts'=2,'clus'=16] {'clus'}, dimensions={0} | all-to-all | bytes 32768 | tf_op jit(solution)/shard_map/all_to_all | solution.py:357
  127.6 0.0 copy-done.2
  127.6 1.3 last.1
Async XLA Ops:
  6.8 25.8 %collective-permute-start = (bf16[1168,128]{1,0:T(8,128)(2,1)}, bf16[1168,128]{1,0:T(8,128)(2,1)S(1)}, u32[]{:S(2)}, u32[]{:S(2)}) collective-permute-start(bf16[1168,128]{1,0:T(8,128)(2,1)} %get-tuple-element.65), channel_id=1, source_target_pairs={{0,8},{1,9},{2,10},{3,11},{4,12},{5,13},{6,14},{7,15},{8,0},{9,1},... | collective-permute-start | bytes 897032 | tf_op jit(solution)/shard_map/ppermute | solution.py:341
  10.9 1.9 %copy-start = (bf16[2048,768]{1,0:T(8,128)(2,1)S(1)}, bf16[2048,768]{1,0:T(8,128)(2,1)}, u32[]{:S(2)}) copy-start(bf16[2048,768]{1,0:T(8,128)(2,1)} %get-tuple-element.62.unit_ref) | copy-start | bytes 9437188
  12.8 0.8 copy-start.1
  13.6 0.8 copy-start.3
  17.5 19.9 %collective-permute-start.2 = (bf16[1168,128]{1,0:T(8,128)(2,1)S(1)}, bf16[1168,128]{1,0:T(8,128)(2,1)S(1)}, u32[]{:S(2)}, u32[]{:S(2)}) collective-permute-start(bf16[1168,128]{1,0:T(8,128)(2,1)S(1)} %get-tuple-element.71), channel_id=1, source_target_pairs={{0,4},{1,5},{2,6},{3,7},{4,0},{5,1},{6,2},{7,3},{8,12},{9,13},{10,... | collective-permute-start | bytes 897032 | tf_op jit(solution)/shard_map/ppermute | solution.py:341
  19.2 18.9 %collective-permute-start.1 = (bf16[1168,128]{1,0:T(8,128)(2,1)S(1)}, bf16[1168,128]{1,0:T(8,128)(2,1)S(1)}, u32[]{:S(2)}, u32[]{:S(2)}) collective-permute-start(bf16[1168,128]{1,0:T(8,128)(2,1)S(1)} %get-tuple-element.68), channel_id=1, source_target_pairs={{0,12},{1,13},{2,14},{3,15},{4,8},{5,9},{6,10},{7,11},{8,4},{9,5},... | collective-permute-start | bytes 897032 | tf_op jit(solution)/shard_map/ppermute | solution.py:341
  19.2 30.4 %collective-permute-start.3 = (bf16[1168,128]{1,0:T(8,128)(2,1)S(1)}, bf16[1168,128]{1,0:T(8,128)(2,1)S(1)}, u32[]{:S(2)}, u32[]{:S(2)}) collective-permute-start(bf16[1168,128]{1,0:T(8,128)(2,1)S(1)} %get-tuple-element.74), channel_id=1, source_target_pairs={{0,9},{1,8},{2,11},{3,10},{4,13},{5,12},{6,15},{7,14},{8,1},{9,0},... | collective-permute-start | bytes 897032 | tf_op jit(solution)/shard_map/ppermute | solution.py:341
  32.7 20.3 %collective-permute-start.4 = (bf16[1168,128]{1,0:T(8,128)(2,1)S(1)}, bf16[1168,128]{1,0:T(8,128)(2,1)S(1)}, u32[]{:S(2)}, u32[]{:S(2)}) collective-permute-start(bf16[1168,128]{1,0:T(8,128)(2,1)S(1)} %get-tuple-element.77), channel_id=1, source_target_pairs={{0,5},{1,4},{2,7},{3,6},{4,1},{5,0},{6,3},{7,2},{8,13},{9,12},{10,... | collective-permute-start | bytes 897032 | tf_op jit(solution)/shard_map/ppermute | solution.py:341
  37.5 26.5 %collective-permute-start.6 = (bf16[1168,128]{1,0:T(8,128)(2,1)S(1)}, bf16[1168,128]{1,0:T(8,128)(2,1)S(1)}, u32[]{:S(2)}, u32[]{:S(2)}) collective-permute-start(bf16[1168,128]{1,0:T(8,128)(2,1)S(1)} %get-tuple-element.83), channel_id=1, source_target_pairs={{0,6},{1,7},{2,4},{3,5},{4,2},{5,3},{6,0},{7,1},{8,14},{9,15},{10,... | collective-permute-start | bytes 897032 | tf_op jit(solution)/shard_map/ppermute | solution.py:341
  38.0 26.4 %collective-permute-start.5 = (bf16[1168,128]{1,0:T(8,128)(2,1)S(1)}, bf16[1168,128]{1,0:T(8,128)(2,1)S(1)}, u32[]{:S(2)}, u32[]{:S(2)}) collective-permute-start(bf16[1168,128]{1,0:T(8,128)(2,1)S(1)} %get-tuple-element.80), channel_id=1, source_target_pairs={{0,13},{1,12},{2,15},{3,14},{4,9},{5,8},{6,11},{7,10},{8,5},{9,4},... | collective-permute-start | bytes 897032 | tf_op jit(solution)/shard_map/ppermute | solution.py:341
  49.6 35.0 %collective-permute-start.7 = (bf16[1168,128]{1,0:T(8,128)(2,1)S(1)}, bf16[1168,128]{1,0:T(8,128)(2,1)S(1)}, u32[]{:S(2)}, u32[]{:S(2)}) collective-permute-start(bf16[1168,128]{1,0:T(8,128)(2,1)S(1)} %get-tuple-element.86), channel_id=1, source_target_pairs={{0,10},{1,11},{2,8},{3,9},{4,14},{5,15},{6,12},{7,13},{8,2},{9,3},... | collective-permute-start | bytes 897032 | tf_op jit(solution)/shard_map/ppermute | solution.py:341
  53.0 32.9 %collective-permute-start.8 = (bf16[1168,128]{1,0:T(8,128)(2,1)S(1)}, bf16[1168,128]{1,0:T(8,128)(2,1)S(1)}, u32[]{:S(2)}, u32[]{:S(2)}) collective-permute-start(bf16[1168,128]{1,0:T(8,128)(2,1)S(1)} %get-tuple-element.89), channel_id=1, source_target_pairs={{0,7},{1,6},{2,5},{3,4},{4,3},{5,2},{6,1},{7,0},{8,15},{9,14},{10,... | collective-permute-start | bytes 897032 | tf_op jit(solution)/shard_map/ppermute | solution.py:341
  64.0 25.8 %collective-permute-start.10 = (bf16[1168,128]{1,0:T(8,128)(2,1)S(1)}, bf16[1168,128]{1,0:T(8,128)(2,1)S(1)}, u32[]{:S(2)}, u32[]{:S(2)}) collective-permute-start(bf16[1168,128]{1,0:T(8,128)(2,1)S(1)} %get-tuple-element.95), channel_id=1, source_target_pairs={{0,2},{1,3},{2,0},{3,1},{4,6},{5,7},{6,4},{7,5},{8,10},{9,11},{10,... | collective-permute-start | bytes 897032 | tf_op jit(solution)/shard_map/ppermute | solution.py:341
  64.4 27.6 %collective-permute-start.9 = (bf16[1168,128]{1,0:T(8,128)(2,1)S(1)}, bf16[1168,128]{1,0:T(8,128)(2,1)S(1)}, u32[]{:S(2)}, u32[]{:S(2)}) collective-permute-start(bf16[1168,128]{1,0:T(8,128)(2,1)S(1)} %get-tuple-element.92), channel_id=1, source_target_pairs={{0,14},{1,15},{2,12},{3,13},{4,10},{5,11},{6,8},{7,9},{8,6},{9,7},... | collective-permute-start | bytes 897032 | tf_op jit(solution)/shard_map/ppermute | solution.py:341
  84.5 23.4 %collective-permute-start.11 = (bf16[1168,128]{1,0:T(8,128)(2,1)S(1)}, bf16[1168,128]{1,0:T(8,128)(2,1)S(1)}, u32[]{:S(2)}, u32[]{:S(2)}) collective-permute-start(bf16[1168,128]{1,0:T(8,128)(2,1)S(1)} %get-tuple-element.97), channel_id=1, source_target_pairs={{0,11},{1,10},{2,9},{3,8},{4,15},{5,14},{6,13},{7,12},{8,3},{9,2},... | collective-permute-start | bytes 897032 | tf_op jit(solution)/shard_map/ppermute | solution.py:341
  85.9 22.1 %collective-permute-start.12 = (bf16[1168,128]{1,0:T(8,128)(2,1)S(1)}, bf16[1168,128]{1,0:T(8,128)(2,1)S(1)}, u32[]{:S(2)}, u32[]{:S(2)}) collective-permute-start(bf16[1168,128]{1,0:T(8,128)(2,1)S(1)} %get-tuple-element.98), channel_id=1, source_target_pairs={{0,3},{1,2},{2,1},{3,0},{4,7},{5,6},{6,5},{7,4},{8,11},{9,10},{10,... | collective-permute-start | bytes 897032 | tf_op jit(solution)/shard_map/ppermute | solution.py:341
  89.8 22.8 %collective-permute-start.14 = (bf16[1168,128]{1,0:T(8,128)(2,1)S(1)}, bf16[1168,128]{1,0:T(8,128)(2,1)S(1)}, u32[]{:S(2)}, u32[]{:S(2)}) collective-permute-start(bf16[1168,128]{1,0:T(8,128)(2,1)S(1)} %get-tuple-element.100), channel_id=1, source_target_pairs={{0,15},{1,14},{2,13},{3,12},{4,11},{5,10},{6,9},{7,8},{8,7},{9,6},... | collective-permute-start | bytes 897032 | tf_op jit(solution)/shard_map/ppermute | solution.py:341
  92.0 18.9 %collective-permute-start.13 = (bf16[1168,128]{1,0:T(8,128)(2,1)S(1)}, bf16[1168,128]{1,0:T(8,128)(2,1)S(1)}, u32[]{:S(2)}, u32[]{:S(2)}) collective-permute-start(bf16[1168,128]{1,0:T(8,128)(2,1)S(1)} %get-tuple-element.99), channel_id=1, source_target_pairs={{0,1},{1,0},{2,3},{3,2},{4,5},{5,4},{6,7},{7,6},{8,9},{9,8},{10,11... | collective-permute-start | bytes 897032 | tf_op jit(solution)/shard_map/ppermute | solution.py:341
  110.9 16.7 %copy-start.2 = (s32[3,2048]{1,0:T(4,128)S(1)}, s32[3,2048]{1,0:T(4,128)}, u32[]{:S(2)}) copy-start(s32[3,2048]{1,0:T(4,128)} %get-tuple-element.60.where_ref) | copy-start | bytes 73732

commit v6 on v5

--- a/solution.py
+++ b/solution.py
@@ -66,10 +66,11 @@
     seg = PARTS * cap
     wide = lanes(seg)
 
-    def kernel(ids_ref, cover_ref, emb_ref, unit_ref, where_ref, meta_ref, *rest):
+    def kernel(ids_hbm, cover_hbm, emb_ref, unit_ref, where_hbm, meta_hbm, *rest):
         count = len(offsets)
         outs, scratch = rest[:count], rest[count:]
-        raw_ref, rows_ref, piece_ref, in_sems, rows_sems, out_sems = scratch
+        ids_ref, cover_ref, raw_ref, rows_ref, where_ref, meta_ref, piece_ref = scratch[:7]
+        in_sems, rows_sems, out_sems, small_sems = scratch[7:]
         me = lax.axis_index("clus")
         block = raw_ref.shape[0] // steps
 
@@ -81,8 +82,18 @@
             part = pl.ds(i * block, block)
             return pltpu.make_async_copy(rows_ref.at[part], unit_ref.at[part], rows_sems.at[i])
 
+        small = [
+            pltpu.make_async_copy(ids_hbm, ids_ref, small_sems.at[0]),
+            pltpu.make_async_copy(cover_hbm, cover_ref, small_sems.at[1]),
+            pltpu.make_async_copy(where_ref, where_hbm, small_sems.at[2]),
+            pltpu.make_async_copy(meta_ref, meta_hbm, small_sems.at[3]),
+        ]
+        small[0].start()
+        small[1].start()
         for i in range(steps):
-            load(i).start()
+            load(i).start(priority=i % 2)
+        small[0].wait()
+        small[1].wait()
         ids = ids_ref[...]
         owner = ids // CL_DEV
         position = place(ids, devices, cap)
@@ -97,14 +108,21 @@
         which = (ids - owner * CL_DEV).astype(jnp.float32)
         meta_ref[:, 0, :wide] = dot(own * cover.astype(jnp.bfloat16), there, NT)
         meta_ref[:, 0, wide:] = dot(own * which.astype(jnp.bfloat16), there, NT)
+        small[2].start()
+        small[3].start()
         for i in range(steps):
             load(i).wait()
+            if i == steps - 1:
+                for before in range(steps - 1):
+                    store(before).start(priority=before % 2)
             raw = raw_ref[i * block : (i + 1) * block, :]
             sums = jnp.sum(raw * raw, axis=-1, keepdims=True)
             unit = (raw * lax.rsqrt(sums + 1e-06)).astype(jnp.bfloat16)
             rows_ref[i * block : (i + 1) * block, :] = unit
-            store(i).start()
+        store(steps - 1).start()
         send_pieces(code, rows_ref, meta_ref, seg, me, offsets, outs, piece_ref, out_sems)
+        small[2].wait()
+        small[3].wait()
         for i in range(steps):
             store(i).wait()
 
@@ -308,18 +326,21 @@
 
     full = pl.BlockSpec(memory_space=pltpu.VMEM)
     hbm = pl.BlockSpec(memory_space=pltpu.HBM)
-    steps = 8
+    steps = 4
     lead = pieces_of(early)
     unit, where, meta, *sent = call(
         first_kernel(devices, cap, steps, offsets[1 : 1 + early]),
         [S((rows, width), bf16), S((3, rows), jnp.int32), S((devices, 1, 2 * wide), f32)] + [piece] * early,
         (2 * early * seg * rows * width, 4 * rows * width),
         "first",
-        in_specs=[full, full, hbm],
-        out_specs=[hbm, full, full] + lead["out_specs"],
-        scratch_shapes=[pltpu.VMEM((rows, width), f32), pltpu.VMEM((rows, width), bf16)]
-        + [lead["scratch_shapes"][0], pltpu.SemaphoreType.DMA((steps,))]
-        + [pltpu.SemaphoreType.DMA((steps,)), lead["scratch_shapes"][1]],
+        in_specs=[hbm] * 3,
+        out_specs=[hbm] * 3 + lead["out_specs"],
+        scratch_shapes=[pltpu.VMEM((1, rows), jnp.int32), pltpu.VMEM((rows // 128, 128), bf16)]
+        + [pltpu.VMEM((rows, width), f32), pltpu.VMEM((rows, width), bf16)]
+        + [pltpu.VMEM((3, rows), jnp.int32), pltpu.VMEM((devices, 1, 2 * wide), f32)]
+        + [lead["scratch_shapes"][0]]
+        + [pltpu.SemaphoreType.DMA((steps,))] * 2
+        + [lead["scratch_shapes"][1], pltpu.SemaphoreType.DMA((4,))],
         vmem=56,
     )(ids, cover, embeddings)
     for name, ks in (("second", offsets[1 + early : 1 + depth]), ("rest", offsets[1 + depth :] + [0])):
@@ -339,7 +360,10 @@
         if i >= depth:
             x, got[i - depth] = lax.optimization_barrier((x, got[i - depth]))
         got.append(lax.ppermute(x, "clus", [(d, d ^ offsets[1 + i]) for d in range(devices)]))
-    pieces = [own] + got
+    where_from = dict(zip(offsets, [own] + got))
+    late = [o for o in offsets if o >= devices // 2][-2:]
+    order = [o for o in offsets if o not in late] + late
+    pieces = [where_from[o] for o in order]
 
     gain_shape = S((devices, 1, wide), f32)
     stops = [stop * unitg for stop in STOPS]
@@ -347,7 +371,7 @@
     for g, new in enumerate(stops):
         fresh = new - (stops[g - 1] if g else 0)
         gains, *more = call(
-            gram_kernel(devices, cap, offsets, stops, g),
+            gram_kernel(devices, cap, order, stops, g),
             [gain_shape] + [S((fresh * seg, 256), f32)] * (new < devices),
             (2 * new * seg * fresh * seg * width, 2 * new * seg * width),
             "gram",

time: 129 us -> 139 us (1.078)
  waiting for transfers between devices: 47.1 us -> 66.1 us
  starting transfers between devices: 25.3 us -> 20.2 us
  blocking collectives: 13.1 us -> 10.2 us
  Pallas kernels: 39.9 us -> 38.5 us
    ppermute x15, waiting for transfers between devices: 47.1 us -> 66.1 us  [body(): lax.ppermute(x, 'clus', [(d, d ^ offsets[1 + i]) for d in range(devices)])]
    ppermute x15, starting transfers between devices: 25.3 us -> 20.2 us  [body(): lax.ppermute(x, 'clus', [(d, d ^ offsets[1 + i]) for d in range(devices)])]
    all_to_all x1, blocking collectives: 13.1 us -> 10.2 us  [body(): back = lax.all_to_all(gains, 'clus', 0, 0, tiled=True)]
  transfers between devices with their start and end apart: 15 -> 15, of which waited for: 6 -> 8; matrix products, arithmetic and copies ran while one was open for 0% -> 0% of each run, Pallas kernels for 23% -> 19%
where the time goes in v6:
time: 139 us; the launch traced here: 138 us
  waiting for transfers between devices  66.1 us (48%)
  Pallas kernels  38.5 us (28%)
  starting transfers between devices  20.2 us (15%)
  blocking collectives  10.2 us (7%)
  local copies, waits for them, and re-layouts  3.4 us (2%)
    ppermute x15, waiting for transfers between devices, body(): lax.ppermute(x, 'clus', [(d, d ^ offsets[1 + i]) for d in range(devices)])  66.1 us
    ppermute x15, starting transfers between devices, body(): lax.ppermute(x, 'clus', [(d, d ^ offsets[1 + i]) for d in range(devices)])  20.2 us
    pallas_call x2, Pallas kernels, body(): call(rest_kernel(devices, cap, ks), [piece] * len(ks), (0, 0), name, in_s...  16.1 us
    pallas_call x8, Pallas kernels, body(): call(gram_kernel(devices, cap, order, stops, g), [gain_shape] + [S((fresh...  15.6 us
    all_to_all x1, blocking collectives, body(): back = lax.all_to_all(gains, 'clus', 0, 0, tiled=True)  10.2 us
    pallas_call x1, Pallas kernels, body(): call(first_kernel(devices, cap, steps, offsets[1:1 + early]), [S((rows, w...  5.53 us
    unnamed x8, local copies, waits for them, and re-layouts  3.4 us
  transfers between devices with their start and end apart: 15, of which 8 were waited for; matrix products, arithmetic and copies ran while one was open for 0% of the time, Pallas kernels for 19%

profile of v6, /device:TPU:0, one launch (start us, length us, event | category | flops | bytes accessed | tf_op | source)
XLA Modules:
  0.0 138.5 jit_solution(15399680354796652903)
XLA Ops:
  0.0 5.5 %first.1 = (bf16[2048,768]{1,0:T(8,128)(2,1)}, s32[3,2048]{1,0:T(4,128)}, f32[16,1,512]{2,1,0:T(1,128)}, bf16[1168,128]{1,0:T(8,128)(2,1)}) custom-call(s32[1,2048]{1,0:T(1,128)} %bitcast.3, bf16[16,128]{1,0:T(8,128)(2,1)} %bitcast.4, f32[2048,768]{1,0:T(8,128)} %emb_ref.1), custom_call_target="tpu_custom_call" | custom-call | flops 603979776 | bytes 6291456 | tf_op jit(solution)/shard_map/first/pallas_call | solution.py:331
  5.5 0.0 copy-start
  5.5 1.9 %copy-done = bf16[2048,768]{1,0:T(8,128)(2,1)S(1)} copy-done((bf16[2048,768]{1,0:T(8,128)(2,1)S(1)}, bf16[2048,768]{1,0:T(8,128)(2,1)}, u32[]{:S(2)}) %copy-start) | copy-done | bytes 3145752
  7.4 0.0 copy-start.1
  7.4 0.8 copy-done.1
  8.2 0.0 copy-start.3
  8.2 0.8 copy-done.3
  8.9 3.2 %second.1 = (bf16[1168,128]{1,0:T(8,128)(2,1)S(1)}, bf16[1168,128]{1,0:T(8,128)(2,1)S(1)}, bf16[1168,128]{1,0:T(8,128)(2,1)S(1)}) custom-call(s32[3,2048]{1,0:T(4,128)S(1)} %copy-done.1, f32[16,1,512]{2,1,0:T(1,128)S(1)} %copy-done.3, bf16[2048,768]{1,0:T(8,128)(2,1)S(1)} %copy-done), custom_call_target="tpu_custom_call" | custom-call | tf_op jit(solution)/shard_map/second/pallas_call | solution.py:347
  12.1 5.1 %collective-permute-start.1 = (bf16[1168,128]{1,0:T(8,128)(2,1)S(1)}, bf16[1168,128]{1,0:T(8,128)(2,1)S(1)}, u32[]{:S(2)}, u32[]{:S(2)}) collective-permute-start(bf16[1168,128]{1,0:T(8,128)(2,1)S(1)} %get-tuple-element.68), channel_id=1, source_target_pairs={{0,12},{1,13},{2,14},{3,15},{4,8},{5,9},{6,10},{7,11},{8,4},{9,5},... | collective-permute-start | bytes 897032 | tf_op jit(solution)/shard_map/ppermute | solution.py:362
  17.2 0.0 collective-permute-start
  17.2 0.6 collective-permute-start.2
  17.9 1.2 collective-permute-start.3
  19.0 13.0 %rest.1 = (bf16[1168,128]{1,0:T(8,128)(2,1)S(1)}, bf16[1168,128]{1,0:T(8,128)(2,1)S(1)}, bf16[1168,128]{1,0:T(8,128)(2,1)S(1)}, bf16[1168,128]{1,0:T(8,128)(2,1)...) custom-call(s32[3,2048]{1,0:T(4,128)S(1)} %copy-done.1, ...), custom_call_target="tpu_custom_call" | custom-call | tf_op jit(solution)/shard_map/rest/pallas_call | solution.py:347
  32.0 0.0 collective-permute-done.1.refs_2_
  32.0 2.4 %collective-permute-start.5 = (bf16[1168,128]{1,0:T(8,128)(2,1)S(1)}, bf16[1168,128]{1,0:T(8,128)(2,1)S(1)}, u32[]{:S(2)}, u32[]{:S(2)}) collective-permute-start(bf16[1168,128]{1,0:T(8,128)(2,1)S(1)} %get-tuple-element.80), channel_id=1, source_target_pairs={{0,13},{1,12},{2,15},{3,14},{4,9},{5,8},{6,11},{7,10},{8,5},{9,4},... | collective-permute-start | bytes 897032 | tf_op jit(solution)/shard_map/ppermute | solution.py:362
  34.4 22.1 %collective-permute-done.refs_1_ = bf16[1168,128]{1,0:T(8,128)(2,1)S(1)} collective-permute-done((bf16[1168,128]{1,0:T(8,128)(2,1)}, bf16[1168,128]{1,0:T(8,128)(2,1)S(1)}, u32[]{:S(2)}, u32[]{:S(2)}) %collective-permute-start) | collective-permute-done | bytes 299040 | tf_op jit(solution)/shard_map/ppermute | solution.py:362
  56.5 0.0 collective-permute-start.4
  56.5 0.0 collective-permute-done.2.refs_3_
  56.5 0.9 collective-permute-start.6
  57.4 3.7 %collective-permute-done.3.refs_4_ = bf16[1168,128]{1,0:T(8,128)(2,1)S(1)} collective-permute-done((bf16[1168,128]{1,0:T(8,128)(2,1)S(1)}, bf16[1168,128]{1,0:T(8,128)(2,1)S(1)}, u32[]{:S(2)}, u32[]{:S(2)}) %collective-permute-start.3) | collective-permute-done | bytes 299040 | tf_op jit(solution)/shard_map/ppermute | solution.py:362
  61.1 2.4 %collective-permute-start.7 = (bf16[1168,128]{1,0:T(8,128)(2,1)S(1)}, bf16[1168,128]{1,0:T(8,128)(2,1)S(1)}, u32[]{:S(2)}, u32[]{:S(2)}) collective-permute-start(bf16[1168,128]{1,0:T(8,128)(2,1)S(1)} %get-tuple-element.86), channel_id=1, source_target_pairs={{0,10},{1,11},{2,8},{3,9},{4,14},{5,15},{6,12},{7,13},{8,2},{9,3},... | collective-permute-start | bytes 897032 | tf_op jit(solution)/shard_map/ppermute | solution.py:362
  63.4 0.0 collective-permute-done.5.refs_6_
  63.4 2.6 %collective-permute-start.9 = (bf16[1168,128]{1,0:T(8,128)(2,1)S(1)}, bf16[1168,128]{1,0:T(8,128)(2,1)S(1)}, u32[]{:S(2)}, u32[]{:S(2)}) collective-permute-start(bf16[1168,128]{1,0:T(8,128)(2,1)S(1)} %get-tuple-element.92), channel_id=1, source_target_pairs={{0,14},{1,15},{2,12},{3,13},{4,10},{5,11},{6,8},{7,9},{8,6},{9,7},... | collective-permute-start | bytes 897032 | tf_op jit(solution)/shard_map/ppermute | solution.py:362
  66.0 3.4 %collective-permute-done.4.refs_5_ = bf16[1168,128]{1,0:T(8,128)(2,1)S(1)} collective-permute-done((bf16[1168,128]{1,0:T(8,128)(2,1)S(1)}, bf16[1168,128]{1,0:T(8,128)(2,1)S(1)}, u32[]{:S(2)}, u32[]{:S(2)}) %collective-permute-start.4) | collective-permute-done | bytes 299040 | tf_op jit(solution)/shard_map/ppermute | solution.py:362
  69.4 2.4 %collective-permute-start.8 = (bf16[1168,128]{1,0:T(8,128)(2,1)S(1)}, bf16[1168,128]{1,0:T(8,128)(2,1)S(1)}, u32[]{:S(2)}, u32[]{:S(2)}) collective-permute-start(bf16[1168,128]{1,0:T(8,128)(2,1)S(1)} %get-tuple-element.89), channel_id=1, source_target_pairs={{0,7},{1,6},{2,5},{3,4},{4,3},{5,2},{6,1},{7,0},{8,15},{9,14},{10,... | collective-permute-start | bytes 897032 | tf_op jit(solution)/shard_map/ppermute | solution.py:362
  71.8 9.1 %collective-permute-done.6.refs_7_ = bf16[1168,128]{1,0:T(8,128)(2,1)S(1)} collective-permute-done((bf16[1168,128]{1,0:T(8,128)(2,1)S(1)}, bf16[1168,128]{1,0:T(8,128)(2,1)S(1)}, u32[]{:S(2)}, u32[]{:S(2)}) %collective-permute-start.6) | collective-permute-done | bytes 299040 | tf_op jit(solution)/shard_map/ppermute | solution.py:362
  80.9 0.4 collective-permute-start.10
  81.3 1.5 %gram.8 = (f32[16,1,256]{2,1,0:T(1,128)S(1)}, f32[768,256]{1,0:T(8,128)S(1)}) custom-call(bf16[1168,128]{1,0:T(8,128)(2,1)S(1)} %get-tuple-element.63.refs_0_, bf16[1168,128]{1,0:T(8,128)(2,1)S(1)} %collective-permute-done.refs_1_, bf16[1168,128]{1,0:T(8,128)(2,1)S(1)} %collective-permute-done.1.refs_2_, bf16[1168,128]{1,0:T(8,128)(2,1)S(1)} %collective-permute-done.2.refs_3_), custom_call_target="tpu_custom_call" | custom-call | flops 905969664 | bytes 1179648 | tf_op jit(solution)/shard_map/gram/pallas_call | solution.py:373
  82.8 6.9 %collective-permute-done.7.refs_8_ = bf16[1168,128]{1,0:T(8,128)(2,1)S(1)} collective-permute-done((bf16[1168,128]{1,0:T(8,128)(2,1)S(1)}, bf16[1168,128]{1,0:T(8,128)(2,1)S(1)}, u32[]{:S(2)}, u32[]{:S(2)}) %collective-permute-start.7) | collective-permute-done | bytes 299040 | tf_op jit(solution)/shard_map/ppermute | solution.py:362
  89.7 0.0 collective-permute-start.13
  89.7 1.3 gram.9
  91.0 0.0 collective-permute-done.9.refs_10_
  91.0 0.1 collective-permute-start.12
  91.1 4.0 %collective-permute-done.8.refs_9_ = bf16[1168,128]{1,0:T(8,128)(2,1)S(1)} collective-permute-done((bf16[1168,128]{1,0:T(8,128)(2,1)S(1)}, bf16[1168,128]{1,0:T(8,128)(2,1)S(1)}, u32[]{:S(2)}, u32[]{:S(2)}) %collective-permute-start.8) | collective-permute-done | bytes 299040 | tf_op jit(solution)/shard_map/ppermute | solution.py:362
  95.0 0.1 collective-permute-start.11
  95.1 1.7 %gram.10 = (f32[16,1,256]{2,1,0:T(1,128)S(1)}, f32[384,256]{1,0:T(8,128)S(1)}) custom-call(bf16[1168,128]{1,0:T(8,128)(2,1)S(1)} %get-tuple-element.63.refs_0_, bf16[1168,128]{1,0:T(8,128)(2,1)S(1)} %collective-permute-done.refs_1_, bf16[1168,128]{1,0:T(8,128)(2,1)S(1)} %collective-permute-done.1.refs_2_, ...), custom_call_target="tpu_custom_call" | custom-call | flops 905969664 | bytes 2359296 | tf_op jit(solution)/shard_map/gram/pallas_call | solution.py:373
  96.8 4.5 %collective-permute-done.10.refs_11_ = bf16[1168,128]{1,0:T(8,128)(2,1)S(1)} collective-permute-done((bf16[1168,128]{1,0:T(8,128)(2,1)S(1)}, bf16[1168,128]{1,0:T(8,128)(2,1)S(1)}, u32[]{:S(2)}, u32[]{:S(2)}) %collective-permute-start.10) | collective-permute-done | bytes 299040 | tf_op jit(solution)/shard_map/ppermute | solution.py:362
  101.4 2.1 %collective-permute-start.14 = (bf16[1168,128]{1,0:T(8,128)(2,1)S(1)}, bf16[1168,128]{1,0:T(8,128)(2,1)S(1)}, u32[]{:S(2)}, u32[]{:S(2)}) collective-permute-start(bf16[1168,128]{1,0:T(8,128)(2,1)S(1)} %get-tuple-element.100), channel_id=1, source_target_pairs={{0,15},{1,14},{2,13},{3,12},{4,11},{5,10},{6,9},{7,8},{8,7},{9,6},... | collective-permute-start | bytes 897032 | tf_op jit(solution)/shard_map/ppermute | solution.py:362
  103.4 2.1 %gram.11 = (f32[16,1,256]{2,1,0:T(1,128)S(1)}, f32[384,256]{1,0:T(8,128)S(1)}) custom-call(bf16[1168,128]{1,0:T(8,128)(2,1)S(1)} %get-tuple-element.63.refs_0_, bf16[1168,128]{1,0:T(8,128)(2,1)S(1)} %collective-permute-done.refs_1_, bf16[1168,128]{1,0:T(8,128)(2,1)S(1)} %collective-permute-done.1.refs_2_, ...), custom_call_target="tpu_custom_call" | custom-call | flops 1132462080 | bytes 2949120 | tf_op jit(solution)/shard_map/gram/pallas_call | solution.py:373
  105.5 2.5 %gram.12 = (f32[16,1,256]{2,1,0:T(1,128)S(1)}, f32[384,256]{1,0:T(8,128)S(1)}) custom-call(bf16[1168,128]{1,0:T(8,128)(2,1)S(1)} %get-tuple-element.63.refs_0_, bf16[1168,128]{1,0:T(8,128)(2,1)S(1)} %collective-permute-done.refs_1_, bf16[1168,128]{1,0:T(8,128)(2,1)S(1)} %collective-permute-done.1.refs_2_, ...), custom_call_target="tpu_custom_call" | custom-call | flops 1358954496 | bytes 3538944 | tf_op jit(solution)/shard_map/gram/pallas_call | solution.py:373
  108.0 0.0 collective-permute-done.12.refs_13_
  108.0 12.5 %collective-permute-done.11.refs_12_ = bf16[1168,128]{1,0:T(8,128)(2,1)S(1)} collective-permute-done((bf16[1168,128]{1,0:T(8,128)(2,1)S(1)}, bf16[1168,128]{1,0:T(8,128)(2,1)S(1)}, u32[]{:S(2)}, u32[]{:S(2)}) %collective-permute-start.11) | collective-permute-done | bytes 299040 | tf_op jit(solution)/shard_map/ppermute | solution.py:362
  120.5 2.9 %gram.13 = (f32[16,1,256]{2,1,0:T(1,128)S(1)}, f32[384,256]{1,0:T(8,128)S(1)}) custom-call(bf16[1168,128]{1,0:T(8,128)(2,1)S(1)} %get-tuple-element.63.refs_0_, bf16[1168,128]{1,0:T(8,128)(2,1)S(1)} %collective-permute-done.refs_1_, bf16[1168,128]{1,0:T(8,128)(2,1)S(1)} %collective-permute-done.1.refs_2_, ...), custom_call_target="tpu_custom_call" | custom-call | flops 1585446912 | bytes 4128768 | tf_op jit(solution)/shard_map/gram/pallas_call | solution.py:373
  123.4 0.0 collective-permute-done.13.refs_14_
  123.4 0.0 copy-start.2
  123.4 1.7 %gram.14 = (f32[16,1,256]{2,1,0:T(1,128)S(1)}, f32[192,256]{1,0:T(8,128)S(1)}) custom-call(bf16[1168,128]{1,0:T(8,128)(2,1)S(1)} %get-tuple-element.63.refs_0_, bf16[1168,128]{1,0:T(8,128)(2,1)S(1)} %collective-permute-done.refs_1_, bf16[1168,128]{1,0:T(8,128)(2,1)S(1)} %collective-permute-done.1.refs_2_, ...), custom_call_target="tpu_custom_call" | custom-call | flops 849346560 | bytes 4423680 | tf_op jit(solution)/shard_map/gram/pallas_call | solution.py:373
  125.1 0.0 collective-permute-done.14.refs_15_
  125.1 1.9 %gram.15 = f32[16,1,256]{2,1,0:T(1,128)S(1)} custom-call(bf16[1168,128]{1,0:T(8,128)(2,1)S(1)} %get-tuple-element.63.refs_0_, bf16[1168,128]{1,0:T(8,128)(2,1)S(1)} %collective-permute-done.refs_1_, bf16[1168,128]{1,0:T(8,128)(2,1)S(1)} %collective-permute-done.1.refs_2_, bf16[1168,128]{1,0:T(8,128)(2,1)S(1)} %collective-permute-done.2.refs_3_, ...), custom_call_target="tpu_custom_call" | custom-call | flops 905969664 | bytes 4718592 | tf_op jit(solution)/shard_map/gram/pallas_call | solution.py:373
  127.0 10.2 %all_to_all.5.gains_ref = f32[16,1,256]{2,1,0:T(1,128)S(1)} all-to-all(f32[16,1,256]{2,1,0:T(1,128)S(1)} %gram.15), channel_id=1, replica_groups=mesh['parts'=2,'clus'=16] {'clus'}, dimensions={0} | all-to-all | bytes 32768 | tf_op jit(solution)/shard_map/all_to_all | solution.py:381
  137.2 0.0 copy-done.2
  137.2 1.3 last.1
Async XLA Ops:
  5.5 1.9 %copy-start = (bf16[2048,768]{1,0:T(8,128)(2,1)S(1)}, bf16[2048,768]{1,0:T(8,128)(2,1)}, u32[]{:S(2)}) copy-start(bf16[2048,768]{1,0:T(8,128)(2,1)} %get-tuple-element.62.unit_ref) | copy-start | bytes 9437188
  7.4 0.8 copy-start.1
  8.2 0.8 copy-start.3
  12.1 19.9 %collective-permute-start.1 = (bf16[1168,128]{1,0:T(8,128)(2,1)S(1)}, bf16[1168,128]{1,0:T(8,128)(2,1)S(1)}, u32[]{:S(2)}, u32[]{:S(2)}) collective-permute-start(bf16[1168,128]{1,0:T(8,128)(2,1)S(1)} %get-tuple-element.68), channel_id=1, source_target_pairs={{0,12},{1,13},{2,14},{3,15},{4,8},{5,9},{6,10},{7,11},{8,4},{9,5},... | collective-permute-start | bytes 897032 | tf_op jit(solution)/shard_map/ppermute | solution.py:362
  17.2 39.3 %collective-permute-start = (bf16[1168,128]{1,0:T(8,128)(2,1)}, bf16[1168,128]{1,0:T(8,128)(2,1)S(1)}, u32[]{:S(2)}, u32[]{:S(2)}) collective-permute-start(bf16[1168,128]{1,0:T(8,128)(2,1)} %get-tuple-element.65), channel_id=1, source_target_pairs={{0,8},{1,9},{2,10},{3,11},{4,12},{5,13},{6,14},{7,15},{8,0},{9,1},... | collective-permute-start | bytes 897032 | tf_op jit(solution)/shard_map/ppermute | solution.py:362
  17.2 39.3 %collective-permute-start.2 = (bf16[1168,128]{1,0:T(8,128)(2,1)S(1)}, bf16[1168,128]{1,0:T(8,128)(2,1)S(1)}, u32[]{:S(2)}, u32[]{:S(2)}) collective-permute-start(bf16[1168,128]{1,0:T(8,128)(2,1)S(1)} %get-tuple-element.71), channel_id=1, source_target_pairs={{0,4},{1,5},{2,6},{3,7},{4,0},{5,1},{6,2},{7,3},{8,12},{9,13},{10,... | collective-permute-start | bytes 897032 | tf_op jit(solution)/shard_map/ppermute | solution.py:362
  17.9 43.2 %collective-permute-start.3 = (bf16[1168,128]{1,0:T(8,128)(2,1)S(1)}, bf16[1168,128]{1,0:T(8,128)(2,1)S(1)}, u32[]{:S(2)}, u32[]{:S(2)}) collective-permute-start(bf16[1168,128]{1,0:T(8,128)(2,1)S(1)} %get-tuple-element.74), channel_id=1, source_target_pairs={{0,9},{1,8},{2,11},{3,10},{4,13},{5,12},{6,15},{7,14},{8,1},{9,0},... | collective-permute-start | bytes 897032 | tf_op jit(solution)/shard_map/ppermute | solution.py:362
  32.0 31.4 %collective-permute-start.5 = (bf16[1168,128]{1,0:T(8,128)(2,1)S(1)}, bf16[1168,128]{1,0:T(8,128)(2,1)S(1)}, u32[]{:S(2)}, u32[]{:S(2)}) collective-permute-start(bf16[1168,128]{1,0:T(8,128)(2,1)S(1)} %get-tuple-element.80), channel_id=1, source_target_pairs={{0,13},{1,12},{2,15},{3,14},{4,9},{5,8},{6,11},{7,10},{8,5},{9,4},... | collective-permute-start | bytes 897032 | tf_op jit(solution)/shard_map/ppermute | solution.py:362
  56.5 12.9 %collective-permute-start.4 = (bf16[1168,128]{1,0:T(8,128)(2,1)S(1)}, bf16[1168,128]{1,0:T(8,128)(2,1)S(1)}, u32[]{:S(2)}, u32[]{:S(2)}) collective-permute-start(bf16[1168,128]{1,0:T(8,128)(2,1)S(1)} %get-tuple-element.77), channel_id=1, source_target_pairs={{0,5},{1,4},{2,7},{3,6},{4,1},{5,0},{6,3},{7,2},{8,13},{9,12},{10,... | collective-permute-start | bytes 897032 | tf_op jit(solution)/shard_map/ppermute | solution.py:362
  56.5 24.4 %collective-permute-start.6 = (bf16[1168,128]{1,0:T(8,128)(2,1)S(1)}, bf16[1168,128]{1,0:T(8,128)(2,1)S(1)}, u32[]{:S(2)}, u32[]{:S(2)}) collective-permute-start(bf16[1168,128]{1,0:T(8,128)(2,1)S(1)} %get-tuple-element.83), channel_id=1, source_target_pairs={{0,6},{1,7},{2,4},{3,5},{4,2},{5,3},{6,0},{7,1},{8,14},{9,15},{10,... | collective-permute-start | bytes 897032 | tf_op jit(solution)/shard_map/ppermute | solution.py:362
  61.1 28.6 %collective-permute-start.7 = (bf16[1168,128]{1,0:T(8,128)(2,1)S(1)}, bf16[1168,128]{1,0:T(8,128)(2,1)S(1)}, u32[]{:S(2)}, u32[]{:S(2)}) collective-permute-start(bf16[1168,128]{1,0:T(8,128)(2,1)S(1)} %get-tuple-element.86), channel_id=1, source_target_pairs={{0,10},{1,11},{2,8},{3,9},{4,14},{5,15},{6,12},{7,13},{8,2},{9,3},... | collective-permute-start | bytes 897032 | tf_op jit(solution)/shard_map/ppermute | solution.py:362
  63.4 27.5 %collective-permute-start.9 = (bf16[1168,128]{1,0:T(8,128)(2,1)S(1)}, bf16[1168,128]{1,0:T(8,128)(2,1)S(1)}, u32[]{:S(2)}, u32[]{:S(2)}) collective-permute-start(bf16[1168,128]{1,0:T(8,128)(2,1)S(1)} %get-tuple-element.92), channel_id=1, source_target_pairs={{0,14},{1,15},{2,12},{3,13},{4,10},{5,11},{6,8},{7,9},{8,6},{9,7},... | collective-permute-start | bytes 897032 | tf_op jit(solution)/shard_map/ppermute | solution.py:362
  69.4 25.6 %collective-permute-start.8 = (bf16[1168,128]{1,0:T(8,128)(2,1)S(1)}, bf16[1168,128]{1,0:T(8,128)(2,1)S(1)}, u32[]{:S(2)}, u32[]{:S(2)}) collective-permute-start(bf16[1168,128]{1,0:T(8,128)(2,1)S(1)} %get-tuple-element.89), channel_id=1, source_target_pairs={{0,7},{1,6},{2,5},{3,4},{4,3},{5,2},{6,1},{7,0},{8,15},{9,14},{10,... | collective-permute-start | bytes 897032 | tf_op jit(solution)/shard_map/ppermute | solution.py:362
  80.9 20.5 %collective-permute-start.10 = (bf16[1168,128]{1,0:T(8,128)(2,1)S(1)}, bf16[1168,128]{1,0:T(8,128)(2,1)S(1)}, u32[]{:S(2)}, u32[]{:S(2)}) collective-permute-start(bf16[1168,128]{1,0:T(8,128)(2,1)S(1)} %get-tuple-element.95), channel_id=1, source_target_pairs={{0,2},{1,3},{2,0},{3,1},{4,6},{5,7},{6,4},{7,5},{8,10},{9,11},{10,... | collective-permute-start | bytes 897032 | tf_op jit(solution)/shard_map/ppermute | solution.py:362
  89.7 33.7 %collective-permute-start.13 = (bf16[1168,128]{1,0:T(8,128)(2,1)S(1)}, bf16[1168,128]{1,0:T(8,128)(2,1)S(1)}, u32[]{:S(2)}, u32[]{:S(2)}) collective-permute-start(bf16[1168,128]{1,0:T(8,128)(2,1)S(1)} %get-tuple-element.99), channel_id=1, source_target_pairs={{0,11},{1,10},{2,9},{3,8},{4,15},{5,14},{6,13},{7,12},{8,3},{9,2},... | collective-permute-start | bytes 897032 | tf_op jit(solution)/shard_map/ppermute | solution.py:362
  91.0 17.0 %collective-permute-start.12 = (bf16[1168,128]{1,0:T(8,128)(2,1)S(1)}, bf16[1168,128]{1,0:T(8,128)(2,1)S(1)}, u32[]{:S(2)}, u32[]{:S(2)}) collective-permute-start(bf16[1168,128]{1,0:T(8,128)(2,1)S(1)} %get-tuple-element.98), channel_id=1, source_target_pairs={{0,1},{1,0},{2,3},{3,2},{4,5},{5,4},{6,7},{7,6},{8,9},{9,8},{10,11... | collective-permute-start | bytes 897032 | tf_op jit(solution)/shard_map/ppermute | solution.py:362
  95.0 25.5 %collective-permute-start.11 = (bf16[1168,128]{1,0:T(8,128)(2,1)S(1)}, bf16[1168,128]{1,0:T(8,128)(2,1)S(1)}, u32[]{:S(2)}, u32[]{:S(2)}) collective-permute-start(bf16[1168,128]{1,0:T(8,128)(2,1)S(1)} %get-tuple-element.97), channel_id=1, source_target_pairs={{0,3},{1,2},{2,1},{3,0},{4,7},{5,6},{6,5},{7,4},{8,11},{9,10},{10,... | collective-permute-start | bytes 897032 | tf_op jit(solution)/shard_map/ppermute | solution.py:362
  101.4 23.7 %collective-permute-start.14 = (bf16[1168,128]{1,0:T(8,128)(2,1)S(1)}, bf16[1168,128]{1,0:T(8,128)(2,1)S(1)}, u32[]{:S(2)}, u32[]{:S(2)}) collective-permute-start(bf16[1168,128]{1,0:T(8,128)(2,1)S(1)} %get-tuple-element.100), channel_id=1, source_target_pairs={{0,15},{1,14},{2,13},{3,12},{4,11},{5,10},{6,9},{7,8},{8,7},{9,6},... | collective-permute-start | bytes 897032 | tf_op jit(solution)/shard_map/ppermute | solution.py:362
  123.4 13.8 %copy-start.2 = (s32[3,2048]{1,0:T(4,128)S(1)}, s32[3,2048]{1,0:T(4,128)}, u32[]{:S(2)}) copy-start(s32[3,2048]{1,0:T(4,128)} %get-tuple-element.60.where_ref) | copy-start | bytes 73732

commit v7 on v6

--- a/solution.py
+++ b/solution.py
@@ -360,10 +360,7 @@
         if i >= depth:
             x, got[i - depth] = lax.optimization_barrier((x, got[i - depth]))
         got.append(lax.ppermute(x, "clus", [(d, d ^ offsets[1 + i]) for d in range(devices)]))
-    where_from = dict(zip(offsets, [own] + got))
-    late = [o for o in offsets if o >= devices // 2][-2:]
-    order = [o for o in offsets if o not in late] + late
-    pieces = [where_from[o] for o in order]
+    pieces = [own] + got
 
     gain_shape = S((devices, 1, wide), f32)
     stops = [stop * unitg for stop in STOPS]
@@ -371,7 +368,7 @@
     for g, new in enumerate(stops):
         fresh = new - (stops[g - 1] if g else 0)
         gains, *more = call(
-            gram_kernel(devices, cap, order, stops, g),
+            gram_kernel(devices, cap, offsets, stops, g),
             [gain_shape] + [S((fresh * seg, 256), f32)] * (new < devices),
             (2 * new * seg * fresh * seg * width, 2 * new * seg * width),
             "gram",

time: 139 us -> 128 us (0.921)
  waiting for transfers between devices: 66.1 us -> 47.1 us
  starting transfers between devices: 20.2 us -> 25.3 us
  blocking collectives: 10.2 us -> 13.1 us
    ppermute x15, waiting for transfers between devices: 66.1 us -> 47.1 us  [body(): lax.ppermute(x, 'clus', [(d, d ^ offsets[1 + i]) for d in range(devices)])]
    ppermute x15, starting transfers between devices: 20.2 us -> 25.3 us  [body(): lax.ppermute(x, 'clus', [(d, d ^ offsets[1 + i]) for d in range(devices)])]
    all_to_all x1, blocking collectives: 10.2 us -> 13.1 us  [body(): back = lax.all_to_all(gains, 'clus', 0, 0, tiled=True)]
  transfers between devices with their start and end apart: 15 -> 15, of which waited for: 8 -> 6; matrix products, arithmetic and copies ran while one was open for 0% -> 0% of each run, Pallas kernels for 19% -> 23%
where the time goes in v7:
time: 128 us
  waiting for transfers between devices  47.1 us (37%)
  Pallas kernels  38.6 us (30%)
  starting transfers between devices  25.3 us (20%)
  blocking collectives  13.1 us (10%)
  local copies, waits for them, and re-layouts  3.41 us (3%)
    ppermute x15, waiting for transfers between devices, body(): lax.ppermute(x, 'clus', [(d, d ^ offsets[1 + i]) for d in range(devices)])  47.1 us
    ppermute x15, starting transfers between devices, body(): lax.ppermute(x, 'clus', [(d, d ^ offsets[1 + i]) for d in range(devices)])  25.3 us
    pallas_call x2, Pallas kernels, body(): call(rest_kernel(devices, cap, ks), [piece] * len(ks), (0, 0), name, in_s...  16.1 us
    pallas_call x8, Pallas kernels, body(): call(gram_kernel(devices, cap, offsets, stops, g), [gain_shape] + [S((fre...  15.7 us
    all_to_all x1, blocking collectives, body(): back = lax.all_to_all(gains, 'clus', 0, 0, tiled=True)  13.1 us
    pallas_call x1, Pallas kernels, body(): call(first_kernel(devices, cap, steps, offsets[1:1 + early]), [S((rows, w...  5.53 us
    unnamed x8, local copies, waits for them, and re-layouts  3.41 us
  transfers between devices with their start and end apart: 15, of which 6 were waited for; matrix products, arithmetic and copies ran while one was open for 0% of the time, Pallas kernels for 23%

profile of v7, /device:TPU:0, one launch (start us, length us, event | category | flops | bytes accessed | tf_op | source)
XLA Modules:
  0.0 127.6 jit_solution(1978976526226095383)
XLA Ops:
  0.0 5.5 %first.1 = (bf16[2048,768]{1,0:T(8,128)(2,1)}, s32[3,2048]{1,0:T(4,128)}, f32[16,1,512]{2,1,0:T(1,128)}, bf16[1168,128]{1,0:T(8,128)(2,1)}) custom-call(s32[1,2048]{1,0:T(1,128)} %bitcast.3, bf16[16,128]{1,0:T(8,128)(2,1)} %bitcast.4, f32[2048,768]{1,0:T(8,128)} %emb_ref.1), custom_call_target="tpu_custom_call" | custom-call | flops 603979776 | bytes 6291456 | tf_op jit(solution)/shard_map/first/pallas_call | solution.py:331
  5.5 4.1 %collective-permute-start = (bf16[1168,128]{1,0:T(8,128)(2,1)}, bf16[1168,128]{1,0:T(8,128)(2,1)S(1)}, u32[]{:S(2)}, u32[]{:S(2)}) collective-permute-start(bf16[1168,128]{1,0:T(8,128)(2,1)} %get-tuple-element.65), channel_id=1, source_target_pairs={{0,8},{1,9},{2,10},{3,11},{4,12},{5,13},{6,14},{7,15},{8,0},{9,1},... | collective-permute-start | bytes 897032 | tf_op jit(solution)/shard_map/ppermute | solution.py:362
  9.6 0.0 copy-start
  9.6 1.9 %copy-done = bf16[2048,768]{1,0:T(8,128)(2,1)S(1)} copy-done((bf16[2048,768]{1,0:T(8,128)(2,1)S(1)}, bf16[2048,768]{1,0:T(8,128)(2,1)}, u32[]{:S(2)}) %copy-start) | copy-done | bytes 3145752
  11.5 0.0 copy-start.1
  11.5 0.8 copy-done.1
  12.3 0.0 copy-start.3
  12.3 0.8 copy-done.3
  13.0 3.2 %second.1 = (bf16[1168,128]{1,0:T(8,128)(2,1)S(1)}, bf16[1168,128]{1,0:T(8,128)(2,1)S(1)}, bf16[1168,128]{1,0:T(8,128)(2,1)S(1)}) custom-call(s32[3,2048]{1,0:T(4,128)S(1)} %copy-done.1, f32[16,1,512]{2,1,0:T(1,128)S(1)} %copy-done.3, bf16[2048,768]{1,0:T(8,128)(2,1)S(1)} %copy-done), custom_call_target="tpu_custom_call" | custom-call | tf_op jit(solution)/shard_map/second/pallas_call | solution.py:347
  16.2 1.6 %collective-permute-start.2 = (bf16[1168,128]{1,0:T(8,128)(2,1)S(1)}, bf16[1168,128]{1,0:T(8,128)(2,1)S(1)}, u32[]{:S(2)}, u32[]{:S(2)}) collective-permute-start(bf16[1168,128]{1,0:T(8,128)(2,1)S(1)} %get-tuple-element.71), channel_id=1, source_target_pairs={{0,4},{1,5},{2,6},{3,7},{4,0},{5,1},{6,2},{7,3},{8,12},{9,13},{10,... | collective-permute-start | bytes 897032 | tf_op jit(solution)/shard_map/ppermute | solution.py:362
  17.9 0.0 collective-permute-start.1
  17.9 0.5 collective-permute-start.3
  18.4 13.0 %rest.1 = (bf16[1168,128]{1,0:T(8,128)(2,1)S(1)}, bf16[1168,128]{1,0:T(8,128)(2,1)S(1)}, bf16[1168,128]{1,0:T(8,128)(2,1)S(1)}, bf16[1168,128]{1,0:T(8,128)(2,1)...) custom-call(s32[3,2048]{1,0:T(4,128)S(1)} %copy-done.1, ...), custom_call_target="tpu_custom_call" | custom-call | tf_op jit(solution)/shard_map/rest/pallas_call | solution.py:347
  31.3 0.0 collective-permute-done.refs_1_
  31.4 3.7 %collective-permute-start.4 = (bf16[1168,128]{1,0:T(8,128)(2,1)S(1)}, bf16[1168,128]{1,0:T(8,128)(2,1)S(1)}, u32[]{:S(2)}, u32[]{:S(2)}) collective-permute-start(bf16[1168,128]{1,0:T(8,128)(2,1)S(1)} %get-tuple-element.77), channel_id=1, source_target_pairs={{0,5},{1,4},{2,7},{3,6},{4,1},{5,0},{6,3},{7,2},{8,13},{9,12},{10,... | collective-permute-start | bytes 897032 | tf_op jit(solution)/shard_map/ppermute | solution.py:362
  35.0 1.2 collective-permute-done.2.refs_3_
  36.2 0.6 collective-permute-start.6
  36.7 0.0 collective-permute-done.1.refs_2_
  36.7 1.2 collective-permute-start.5
  37.9 10.4 %collective-permute-done.3.refs_4_ = bf16[1168,128]{1,0:T(8,128)(2,1)S(1)} collective-permute-done((bf16[1168,128]{1,0:T(8,128)(2,1)S(1)}, bf16[1168,128]{1,0:T(8,128)(2,1)S(1)}, u32[]{:S(2)}, u32[]{:S(2)}) %collective-permute-start.3) | collective-permute-done | bytes 299040 | tf_op jit(solution)/shard_map/ppermute | solution.py:362
  48.3 3.4 %collective-permute-start.7 = (bf16[1168,128]{1,0:T(8,128)(2,1)S(1)}, bf16[1168,128]{1,0:T(8,128)(2,1)S(1)}, u32[]{:S(2)}, u32[]{:S(2)}) collective-permute-start(bf16[1168,128]{1,0:T(8,128)(2,1)S(1)} %get-tuple-element.86), channel_id=1, source_target_pairs={{0,10},{1,11},{2,8},{3,9},{4,14},{5,15},{6,12},{7,13},{8,2},{9,3},... | collective-permute-start | bytes 897032 | tf_op jit(solution)/shard_map/ppermute | solution.py:362
  51.7 0.0 collective-permute-done.4.refs_5_
  51.7 2.2 %collective-permute-start.8 = (bf16[1168,128]{1,0:T(8,128)(2,1)S(1)}, bf16[1168,128]{1,0:T(8,128)(2,1)S(1)}, u32[]{:S(2)}, u32[]{:S(2)}) collective-permute-start(bf16[1168,128]{1,0:T(8,128)(2,1)S(1)} %get-tuple-element.89), channel_id=1, source_target_pairs={{0,7},{1,6},{2,5},{3,4},{4,3},{5,2},{6,1},{7,0},{8,15},{9,14},{10,... | collective-permute-start | bytes 897032 | tf_op jit(solution)/shard_map/ppermute | solution.py:362
  53.9 8.8 %collective-permute-done.6.refs_7_ = bf16[1168,128]{1,0:T(8,128)(2,1)S(1)} collective-permute-done((bf16[1168,128]{1,0:T(8,128)(2,1)S(1)}, bf16[1168,128]{1,0:T(8,128)(2,1)S(1)}, u32[]{:S(2)}, u32[]{:S(2)}) %collective-permute-start.6) | collective-permute-done | bytes 299040 | tf_op jit(solution)/shard_map/ppermute | solution.py:362
  62.7 0.4 collective-permute-start.10
  63.1 0.0 collective-permute-done.5.refs_6_
  63.1 4.8 %collective-permute-start.9 = (bf16[1168,128]{1,0:T(8,128)(2,1)S(1)}, bf16[1168,128]{1,0:T(8,128)(2,1)S(1)}, u32[]{:S(2)}, u32[]{:S(2)}) collective-permute-start(bf16[1168,128]{1,0:T(8,128)(2,1)S(1)} %get-tuple-element.92), channel_id=1, source_target_pairs={{0,14},{1,15},{2,12},{3,13},{4,10},{5,11},{6,8},{7,9},{8,6},{9,7},... | collective-permute-start | bytes 897032 | tf_op jit(solution)/shard_map/ppermute | solution.py:362
  67.9 1.5 %gram.8 = (f32[16,1,256]{2,1,0:T(1,128)S(1)}, f32[768,256]{1,0:T(8,128)S(1)}) custom-call(bf16[1168,128]{1,0:T(8,128)(2,1)S(1)} %get-tuple-element.63.refs_0_, bf16[1168,128]{1,0:T(8,128)(2,1)S(1)} %collective-permute-done.refs_1_, bf16[1168,128]{1,0:T(8,128)(2,1)S(1)} %collective-permute-done.1.refs_2_, bf16[1168,128]{1,0:T(8,128)(2,1)S(1)} %collective-permute-done.2.refs_3_), custom_call_target="tpu_custom_call" | custom-call | flops 905969664 | bytes 1179648 | tf_op jit(solution)/shard_map/gram/pallas_call | solution.py:370
  69.4 13.8 %collective-permute-done.7.refs_8_ = bf16[1168,128]{1,0:T(8,128)(2,1)S(1)} collective-permute-done((bf16[1168,128]{1,0:T(8,128)(2,1)S(1)}, bf16[1168,128]{1,0:T(8,128)(2,1)S(1)}, u32[]{:S(2)}, u32[]{:S(2)}) %collective-permute-start.7) | collective-permute-done | bytes 299040 | tf_op jit(solution)/shard_map/ppermute | solution.py:362
  83.2 0.0 collective-permute-start.11
  83.2 1.3 %gram.9 = (f32[16,1,256]{2,1,0:T(1,128)S(1)}, f32[384,256]{1,0:T(8,128)S(1)}) custom-call(bf16[1168,128]{1,0:T(8,128)(2,1)S(1)} %get-tuple-element.63.refs_0_, bf16[1168,128]{1,0:T(8,128)(2,1)S(1)} %collective-permute-done.refs_1_, bf16[1168,128]{1,0:T(8,128)(2,1)S(1)} %collective-permute-done.1.refs_2_, ...), custom_call_target="tpu_custom_call" | custom-call | flops 679477248 | bytes 1769472 | tf_op jit(solution)/shard_map/gram/pallas_call | solution.py:370
  84.5 0.0 collective-permute-done.8.refs_9_
  84.6 0.1 collective-permute-start.12
  84.6 1.7 %gram.10 = (f32[16,1,256]{2,1,0:T(1,128)S(1)}, f32[384,256]{1,0:T(8,128)S(1)}) custom-call(bf16[1168,128]{1,0:T(8,128)(2,1)S(1)} %get-tuple-element.63.refs_0_, bf16[1168,128]{1,0:T(8,128)(2,1)S(1)} %collective-permute-done.refs_1_, bf16[1168,128]{1,0:T(8,128)(2,1)S(1)} %collective-permute-done.1.refs_2_, ...), custom_call_target="tpu_custom_call" | custom-call | flops 905969664 | bytes 2359296 | tf_op jit(solution)/shard_map/gram/pallas_call | solution.py:370
  86.4 2.1 %collective-permute-done.10.refs_11_ = bf16[1168,128]{1,0:T(8,128)(2,1)S(1)} collective-permute-done((bf16[1168,128]{1,0:T(8,128)(2,1)S(1)}, bf16[1168,128]{1,0:T(8,128)(2,1)S(1)}, u32[]{:S(2)}, u32[]{:S(2)}) %collective-permute-start.10) | collective-permute-done | bytes 299040 | tf_op jit(solution)/shard_map/ppermute | solution.py:362
  88.5 2.2 %collective-permute-start.14 = (bf16[1168,128]{1,0:T(8,128)(2,1)S(1)}, bf16[1168,128]{1,0:T(8,128)(2,1)S(1)}, u32[]{:S(2)}, u32[]{:S(2)}) collective-permute-start(bf16[1168,128]{1,0:T(8,128)(2,1)S(1)} %get-tuple-element.100), channel_id=1, source_target_pairs={{0,15},{1,14},{2,13},{3,12},{4,11},{5,10},{6,9},{7,8},{8,7},{9,6},... | collective-permute-start | bytes 897032 | tf_op jit(solution)/shard_map/ppermute | solution.py:362
  90.7 0.0 collective-permute-done.9.refs_10_
  90.7 0.6 collective-permute-start.13
  91.3 2.1 %gram.11 = (f32[16,1,256]{2,1,0:T(1,128)S(1)}, f32[384,256]{1,0:T(8,128)S(1)}) custom-call(bf16[1168,128]{1,0:T(8,128)(2,1)S(1)} %get-tuple-element.63.refs_0_, bf16[1168,128]{1,0:T(8,128)(2,1)S(1)} %collective-permute-done.refs_1_, bf16[1168,128]{1,0:T(8,128)(2,1)S(1)} %collective-permute-done.1.refs_2_, ...), custom_call_target="tpu_custom_call" | custom-call | flops 1132462080 | bytes 2949120 | tf_op jit(solution)/shard_map/gram/pallas_call | solution.py:370
  93.4 2.5 %gram.12 = (f32[16,1,256]{2,1,0:T(1,128)S(1)}, f32[384,256]{1,0:T(8,128)S(1)}) custom-call(bf16[1168,128]{1,0:T(8,128)(2,1)S(1)} %get-tuple-element.63.refs_0_, bf16[1168,128]{1,0:T(8,128)(2,1)S(1)} %collective-permute-done.refs_1_, bf16[1168,128]{1,0:T(8,128)(2,1)S(1)} %collective-permute-done.1.refs_2_, ...), custom_call_target="tpu_custom_call" | custom-call | flops 1358954496 | bytes 3538944 | tf_op jit(solution)/shard_map/gram/pallas_call | solution.py:370
  95.9 10.8 %collective-permute-done.11.refs_12_ = bf16[1168,128]{1,0:T(8,128)(2,1)S(1)} collective-permute-done((bf16[1168,128]{1,0:T(8,128)(2,1)S(1)}, bf16[1168,128]{1,0:T(8,128)(2,1)S(1)}, u32[]{:S(2)}, u32[]{:S(2)}) %collective-permute-start.11) | collective-permute-done | bytes 299040 | tf_op jit(solution)/shard_map/ppermute | solution.py:362
  106.7 0.0 collective-permute-done.12.refs_13_
  106.7 2.9 %gram.13 = (f32[16,1,256]{2,1,0:T(1,128)S(1)}, f32[384,256]{1,0:T(8,128)S(1)}) custom-call(bf16[1168,128]{1,0:T(8,128)(2,1)S(1)} %get-tuple-element.63.refs_0_, bf16[1168,128]{1,0:T(8,128)(2,1)S(1)} %collective-permute-done.refs_1_, bf16[1168,128]{1,0:T(8,128)(2,1)S(1)} %collective-permute-done.1.refs_2_, ...), custom_call_target="tpu_custom_call" | custom-call | flops 1585446912 | bytes 4128768 | tf_op jit(solution)/shard_map/gram/pallas_call | solution.py:370
  109.6 0.0 collective-permute-done.13.refs_14_
  109.6 0.0 copy-start.2
  109.6 1.7 %gram.14 = (f32[16,1,256]{2,1,0:T(1,128)S(1)}, f32[192,256]{1,0:T(8,128)S(1)}) custom-call(bf16[1168,128]{1,0:T(8,128)(2,1)S(1)} %get-tuple-element.63.refs_0_, bf16[1168,128]{1,0:T(8,128)(2,1)S(1)} %collective-permute-done.refs_1_, bf16[1168,128]{1,0:T(8,128)(2,1)S(1)} %collective-permute-done.1.refs_2_, ...), custom_call_target="tpu_custom_call" | custom-call | flops 849346560 | bytes 4423680 | tf_op jit(solution)/shard_map/gram/pallas_call | solution.py:370
  111.3 0.0 collective-permute-done.14.refs_15_
  111.3 1.9 %gram.15 = f32[16,1,256]{2,1,0:T(1,128)S(1)} custom-call(bf16[1168,128]{1,0:T(8,128)(2,1)S(1)} %get-tuple-element.63.refs_0_, bf16[1168,128]{1,0:T(8,128)(2,1)S(1)} %collective-permute-done.refs_1_, bf16[1168,128]{1,0:T(8,128)(2,1)S(1)} %collective-permute-done.1.refs_2_, bf16[1168,128]{1,0:T(8,128)(2,1)S(1)} %collective-permute-done.2.refs_3_, ...), custom_call_target="tpu_custom_call" | custom-call | flops 905969664 | bytes 4718592 | tf_op jit(solution)/shard_map/gram/pallas_call | solution.py:370
  113.2 13.1 %all_to_all.5.gains_ref = f32[16,1,256]{2,1,0:T(1,128)S(1)} all-to-all(f32[16,1,256]{2,1,0:T(1,128)S(1)} %gram.15), channel_id=1, replica_groups=mesh['parts'=2,'clus'=16] {'clus'}, dimensions={0} | all-to-all | bytes 32768 | tf_op jit(solution)/shard_map/all_to_all | solution.py:378
  126.3 0.0 copy-done.2
  126.3 1.3 last.1
Async XLA Ops:
  5.5 25.8 %collective-permute-start = (bf16[1168,128]{1,0:T(8,128)(2,1)}, bf16[1168,128]{1,0:T(8,128)(2,1)S(1)}, u32[]{:S(2)}, u32[]{:S(2)}) collective-permute-start(bf16[1168,128]{1,0:T(8,128)(2,1)} %get-tuple-element.65), channel_id=1, source_target_pairs={{0,8},{1,9},{2,10},{3,11},{4,12},{5,13},{6,14},{7,15},{8,0},{9,1},... | collective-permute-start | bytes 897032 | tf_op jit(solution)/shard_map/ppermute | solution.py:362
  9.6 1.9 %copy-start = (bf16[2048,768]{1,0:T(8,128)(2,1)S(1)}, bf16[2048,768]{1,0:T(8,128)(2,1)}, u32[]{:S(2)}) copy-start(bf16[2048,768]{1,0:T(8,128)(2,1)} %get-tuple-element.62.unit_ref) | copy-start | bytes 9437188
  11.5 0.8 copy-start.1
  12.3 0.8 copy-start.3
  16.2 20.0 %collective-permute-start.2 = (bf16[1168,128]{1,0:T(8,128)(2,1)S(1)}, bf16[1168,128]{1,0:T(8,128)(2,1)S(1)}, u32[]{:S(2)}, u32[]{:S(2)}) collective-permute-start(bf16[1168,128]{1,0:T(8,128)(2,1)S(1)} %get-tuple-element.71), channel_id=1, source_target_pairs={{0,4},{1,5},{2,6},{3,7},{4,0},{5,1},{6,2},{7,3},{8,12},{9,13},{10,... | collective-permute-start | bytes 897032 | tf_op jit(solution)/shard_map/ppermute | solution.py:362
  17.9 18.9 %collective-permute-start.1 = (bf16[1168,128]{1,0:T(8,128)(2,1)S(1)}, bf16[1168,128]{1,0:T(8,128)(2,1)S(1)}, u32[]{:S(2)}, u32[]{:S(2)}) collective-permute-start(bf16[1168,128]{1,0:T(8,128)(2,1)S(1)} %get-tuple-element.68), channel_id=1, source_target_pairs={{0,12},{1,13},{2,14},{3,15},{4,8},{5,9},{6,10},{7,11},{8,4},{9,5},... | collective-permute-start | bytes 897032 | tf_op jit(solution)/shard_map/ppermute | solution.py:362
  17.9 30.4 %collective-permute-start.3 = (bf16[1168,128]{1,0:T(8,128)(2,1)S(1)}, bf16[1168,128]{1,0:T(8,128)(2,1)S(1)}, u32[]{:S(2)}, u32[]{:S(2)}) collective-permute-start(bf16[1168,128]{1,0:T(8,128)(2,1)S(1)} %get-tuple-element.74), channel_id=1, source_target_pairs={{0,9},{1,8},{2,11},{3,10},{4,13},{5,12},{6,15},{7,14},{8,1},{9,0},... | collective-permute-start | bytes 897032 | tf_op jit(solution)/shard_map/ppermute | solution.py:362
  31.4 20.3 %collective-permute-start.4 = (bf16[1168,128]{1,0:T(8,128)(2,1)S(1)}, bf16[1168,128]{1,0:T(8,128)(2,1)S(1)}, u32[]{:S(2)}, u32[]{:S(2)}) collective-permute-start(bf16[1168,128]{1,0:T(8,128)(2,1)S(1)} %get-tuple-element.77), channel_id=1, source_target_pairs={{0,5},{1,4},{2,7},{3,6},{4,1},{5,0},{6,3},{7,2},{8,13},{9,12},{10,... | collective-permute-start | bytes 897032 | tf_op jit(solution)/shard_map/ppermute | solution.py:362
  36.2 26.5 %collective-permute-start.6 = (bf16[1168,128]{1,0:T(8,128)(2,1)S(1)}, bf16[1168,128]{1,0:T(8,128)(2,1)S(1)}, u32[]{:S(2)}, u32[]{:S(2)}) collective-permute-start(bf16[1168,128]{1,0:T(8,128)(2,1)S(1)} %get-tuple-element.83), channel_id=1, source_target_pairs={{0,6},{1,7},{2,4},{3,5},{4,2},{5,3},{6,0},{7,1},{8,14},{9,15},{10,... | collective-permute-start | bytes 897032 | tf_op jit(solution)/shard_map/ppermute | solution.py:362
  36.7 26.4 %collective-permute-start.5 = (bf16[1168,128]{1,0:T(8,128)(2,1)S(1)}, bf16[1168,128]{1,0:T(8,128)(2,1)S(1)}, u32[]{:S(2)}, u32[]{:S(2)}) collective-permute-start(bf16[1168,128]{1,0:T(8,128)(2,1)S(1)} %get-tuple-element.80), channel_id=1, source_target_pairs={{0,13},{1,12},{2,15},{3,14},{4,9},{5,8},{6,11},{7,10},{8,5},{9,4},... | collective-permute-start | bytes 897032 | tf_op jit(solution)/shard_map/ppermute | solution.py:362
  48.3 34.9 %collective-permute-start.7 = (bf16[1168,128]{1,0:T(8,128)(2,1)S(1)}, bf16[1168,128]{1,0:T(8,128)(2,1)S(1)}, u32[]{:S(2)}, u32[]{:S(2)}) collective-permute-start(bf16[1168,128]{1,0:T(8,128)(2,1)S(1)} %get-tuple-element.86), channel_id=1, source_target_pairs={{0,10},{1,11},{2,8},{3,9},{4,14},{5,15},{6,12},{7,13},{8,2},{9,3},... | collective-permute-start | bytes 897032 | tf_op jit(solution)/shard_map/ppermute | solution.py:362
  51.7 32.9 %collective-permute-start.8 = (bf16[1168,128]{1,0:T(8,128)(2,1)S(1)}, bf16[1168,128]{1,0:T(8,128)(2,1)S(1)}, u32[]{:S(2)}, u32[]{:S(2)}) collective-permute-start(bf16[1168,128]{1,0:T(8,128)(2,1)S(1)} %get-tuple-element.89), channel_id=1, source_target_pairs={{0,7},{1,6},{2,5},{3,4},{4,3},{5,2},{6,1},{7,0},{8,15},{9,14},{10,... | collective-permute-start | bytes 897032 | tf_op jit(solution)/shard_map/ppermute | solution.py:362
  62.7 25.8 %collective-permute-start.10 = (bf16[1168,128]{1,0:T(8,128)(2,1)S(1)}, bf16[1168,128]{1,0:T(8,128)(2,1)S(1)}, u32[]{:S(2)}, u32[]{:S(2)}) collective-permute-start(bf16[1168,128]{1,0:T(8,128)(2,1)S(1)} %get-tuple-element.95), channel_id=1, source_target_pairs={{0,2},{1,3},{2,0},{3,1},{4,6},{5,7},{6,4},{7,5},{8,10},{9,11},{10,... | collective-permute-start | bytes 897032 | tf_op jit(solution)/shard_map/ppermute | solution.py:362
  63.1 27.6 %collective-permute-start.9 = (bf16[1168,128]{1,0:T(8,128)(2,1)S(1)}, bf16[1168,128]{1,0:T(8,128)(2,1)S(1)}, u32[]{:S(2)}, u32[]{:S(2)}) collective-permute-start(bf16[1168,128]{1,0:T(8,128)(2,1)S(1)} %get-tuple-element.92), channel_id=1, source_target_pairs={{0,14},{1,15},{2,12},{3,13},{4,10},{5,11},{6,8},{7,9},{8,6},{9,7},... | collective-permute-start | bytes 897032 | tf_op jit(solution)/shard_map/ppermute | solution.py:362
  83.2 23.4 %collective-permute-start.11 = (bf16[1168,128]{1,0:T(8,128)(2,1)S(1)}, bf16[1168,128]{1,0:T(8,128)(2,1)S(1)}, u32[]{:S(2)}, u32[]{:S(2)}) collective-permute-start(bf16[1168,128]{1,0:T(8,128)(2,1)S(1)} %get-tuple-element.97), channel_id=1, source_target_pairs={{0,11},{1,10},{2,9},{3,8},{4,15},{5,14},{6,13},{7,12},{8,3},{9,2},... | collective-permute-start | bytes 897032 | tf_op jit(solution)/shard_map/ppermute | solution.py:362
  84.6 22.1 %collective-permute-start.12 = (bf16[1168,128]{1,0:T(8,128)(2,1)S(1)}, bf16[1168,128]{1,0:T(8,128)(2,1)S(1)}, u32[]{:S(2)}, u32[]{:S(2)}) collective-permute-start(bf16[1168,128]{1,0:T(8,128)(2,1)S(1)} %get-tuple-element.98), channel_id=1, source_target_pairs={{0,3},{1,2},{2,1},{3,0},{4,7},{5,6},{6,5},{7,4},{8,11},{9,10},{10,... | collective-permute-start | bytes 897032 | tf_op jit(solution)/shard_map/ppermute | solution.py:362
  88.5 22.8 %collective-permute-start.14 = (bf16[1168,128]{1,0:T(8,128)(2,1)S(1)}, bf16[1168,128]{1,0:T(8,128)(2,1)S(1)}, u32[]{:S(2)}, u32[]{:S(2)}) collective-permute-start(bf16[1168,128]{1,0:T(8,128)(2,1)S(1)} %get-tuple-element.100), channel_id=1, source_target_pairs={{0,15},{1,14},{2,13},{3,12},{4,11},{5,10},{6,9},{7,8},{8,7},{9,6},... | collective-permute-start | bytes 897032 | tf_op jit(solution)/shard_map/ppermute | solution.py:362
  90.7 18.9 %collective-permute-start.13 = (bf16[1168,128]{1,0:T(8,128)(2,1)S(1)}, bf16[1168,128]{1,0:T(8,128)(2,1)S(1)}, u32[]{:S(2)}, u32[]{:S(2)}) collective-permute-start(bf16[1168,128]{1,0:T(8,128)(2,1)S(1)} %get-tuple-element.99), channel_id=1, source_target_pairs={{0,1},{1,0},{2,3},{3,2},{4,5},{5,4},{6,7},{7,6},{8,9},{9,8},{10,11... | collective-permute-start | bytes 897032 | tf_op jit(solution)/shard_map/ppermute | solution.py:362
  109.6 16.7 %copy-start.2 = (s32[3,2048]{1,0:T(4,128)S(1)}, s32[3,2048]{1,0:T(4,128)}, u32[]{:S(2)}) copy-start(s32[3,2048]{1,0:T(4,128)} %get-tuple-element.60.where_ref) | copy-start | bytes 73732

commit v8 on v7

--- a/solution.py
+++ b/solution.py
@@ -290,15 +290,15 @@
 
 def sequence(devices):
     half = devices // 2
-    quarter = max(1, half // 2)
+    quarter = half // 2
     far = []
     for i in range(quarter):
         far += [half + i, half + quarter + i]
-    near = sorted(range(1, half), key=lambda k: (-k.bit_length(), k))
-    order = [0, far[0]]
-    for i in range(half - 2):
-        order += [far[i + 1], near[i]]
-    return order + [near[-1], far[-1]]
+    near = sorted(range(4, half), key=lambda k: (-k.bit_length(), k))
+    chain = [far[0]]
+    for i, k in enumerate(near):
+        chain += [far[i + 1], k]
+    return chain + far[len(near) + 1 :]
 
 
 def body(embeddings, coverage, cluster_ids):
@@ -307,7 +307,7 @@
     cap = 2 * rows // (CL_DEV * devices)
     seg = PARTS * cap
     wide = lanes(seg)
-    offsets = sequence(devices)
+    chain = sequence(devices)
     f32, bf16 = jnp.float32, jnp.bfloat16
     S = jax.ShapeDtypeStruct
     ids = cluster_ids.reshape(1, rows)
@@ -329,7 +329,7 @@
     steps = 4
     lead = pieces_of(early)
     unit, where, meta, *sent = call(
-        first_kernel(devices, cap, steps, offsets[1 : 1 + early]),
+        first_kernel(devices, cap, steps, chain[:early]),
         [S((rows, width), bf16), S((3, rows), jnp.int32), S((devices, 1, 2 * wide), f32)] + [piece] * early,
         (2 * early * seg * rows * width, 4 * rows * width),
         "first",
@@ -343,24 +343,26 @@
         + [lead["scratch_shapes"][1], pltpu.SemaphoreType.DMA((4,))],
         vmem=56,
     )(ids, cover, embeddings)
-    for name, ks in (("second", offsets[1 + early : 1 + depth]), ("rest", offsets[1 + depth :] + [0])):
+    for name, ks in (("second", chain[early:depth]), ("rest", chain[depth:] + [2, 3, 1, 0])):
         sent += call(
             rest_kernel(devices, cap, ks),
             [piece] * len(ks),
-            (0, 0),
+            (len(ks) * 2 * seg * rows * width, 0),
             name,
             in_specs=[full] * 3,
             vmem=20,
             **pieces_of(len(ks)),
         )(where, meta, unit)
-    own = sent.pop()
-
-    got = []
-    for i, x in enumerate(sent):
-        if i >= depth:
-            x, got[i - depth] = lax.optimization_barrier((x, got[i - depth]))
-        got.append(lax.ppermute(x, "clus", [(d, d ^ offsets[1 + i]) for d in range(devices)]))
-    pieces = [own] + got
+    pieces = dict(zip(chain + [2, 3, 1, 0], sent))
+    leader = {k: chain[i] for i, k in enumerate(chain[depth:])}
+    leader.update({2: chain[3 * unitg], 3: chain[5 * unitg], 1: chain[7 * unitg]})
+    for k in chain + [2, 3, 1]:
+        x = pieces[k]
+        if k in leader:
+            x, pieces[leader[k]] = lax.optimization_barrier((x, pieces[leader[k]]))
+        pieces[k] = lax.ppermute(x, "clus", [(d, d ^ k) for d in range(devices)])
+    order = [0] + chain[:-5] + [2, 3] + chain[-5:-3] + [1] + chain[-3:]
+    pieces = [pieces[k] for k in order]
 
     gain_shape = S((devices, 1, wide), f32)
     stops = [stop * unitg for stop in STOPS]
@@ -368,7 +370,7 @@
     for g, new in enumerate(stops):
         fresh = new - (stops[g - 1] if g else 0)
         gains, *more = call(
-            gram_kernel(devices, cap, offsets, stops, g),
+            gram_kernel(devices, cap, order, stops, g),
             [gain_shape] + [S((fresh * seg, 256), f32)] * (new < devices),
             (2 * new * seg * fresh * seg * width, 2 * new * seg * width),
             "gram",

time: 128 us -> 138 us (1.078)
  starting transfers between devices: 25.3 us -> 47.4 us
  waiting for transfers between devices: 47.1 us -> 37.9 us
  blocking collectives: 13.1 us -> 10.8 us
    ppermute x15, starting transfers between devices: 25.3 us -> 47.4 us  [body(): pieces[k] = lax.ppermute(x, 'clus', [(d, d ^ k) for d in range(devices)])]
    ppermute x15, waiting for transfers between devices: 47.1 us -> 37.9 us  [body(): pieces[k] = lax.ppermute(x, 'clus', [(d, d ^ k) for d in range(devices)])]
    all_to_all x1, blocking collectives: 13.1 us -> 10.8 us  [body(): back = lax.all_to_all(gains, 'clus', 0, 0, tiled=True)]
  transfers between devices with their start and end apart: 15 -> 15, of which waited for: 6 -> 5; matrix products, arithmetic and copies ran while one was open for 0% -> 0% of each run, Pallas kernels for 23% -> 22%
where the time goes in v8:
time: 138 us
  starting transfers between devices  47.4 us (34%)
  Pallas kernels  38.5 us (28%)
  waiting for transfers between devices  37.9 us (27%)
  blocking collectives  10.8 us (8%)
  local copies, waits for them, and re-layouts  3.41 us (2%)
    ppermute x15, starting transfers between devices, body(): pieces[k] = lax.ppermute(x, 'clus', [(d, d ^ k) for d in range(devices)])  47.4 us
    ppermute x15, waiting for transfers between devices, body(): pieces[k] = lax.ppermute(x, 'clus', [(d, d ^ k) for d in range(devices)])  37.9 us
    pallas_call x2, Pallas kernels, body(): call(rest_kernel(devices, cap, ks), [piece] * len(ks), (len(ks) * 2 * seg...  16.1 us
    pallas_call x8, Pallas kernels, body(): call(gram_kernel(devices, cap, order, stops, g), [gain_shape] + [S((fresh...  15.6 us
    all_to_all x1, blocking collectives, body(): back = lax.all_to_all(gains, 'clus', 0, 0, tiled=True)  10.8 us
    pallas_call x1, Pallas kernels, body(): call(first_kernel(devices, cap, steps, chain[:early]), [S((rows, width),...  5.53 us
    unnamed x8, local copies, waits for them, and re-layouts  3.41 us
  transfers between devices with their start and end apart: 15, of which 5 were waited for; matrix products, arithmetic and copies ran while one was open for 0% of the time, Pallas kernels for 22%

profile of v8, /device:TPU:0, one launch (start us, length us, event | category | flops | bytes accessed | tf_op | source)
XLA Modules:
  0.0 138.2 jit_solution(17539731295803214823)
XLA Ops:
  0.0 5.5 %first.1 = (bf16[2048,768]{1,0:T(8,128)(2,1)}, s32[3,2048]{1,0:T(4,128)}, f32[16,1,512]{2,1,0:T(1,128)}, bf16[1168,128]{1,0:T(8,128)(2,1)}) custom-call(s32[1,2048]{1,0:T(1,128)} %bitcast.3, bf16[16,128]{1,0:T(8,128)(2,1)} %bitcast.4, f32[2048,768]{1,0:T(8,128)} %emb_ref.1), custom_call_target="tpu_custom_call" | custom-call | flops 603979776 | bytes 6291456 | tf_op jit(solution)/shard_map/first/pallas_call | solution.py:331
  5.5 4.1 %collective-permute-start = (bf16[1168,128]{1,0:T(8,128)(2,1)}, bf16[1168,128]{1,0:T(8,128)(2,1)S(1)}, u32[]{:S(2)}, u32[]{:S(2)}) collective-permute-start(bf16[1168,128]{1,0:T(8,128)(2,1)} %get-tuple-element.65), channel_id=1, source_target_pairs={{0,8},{1,9},{2,10},{3,11},{4,12},{5,13},{6,14},{7,15},{8,0},{9,1},... | collective-permute-start | bytes 897032 | tf_op jit(solution)/shard_map/ppermute | solution.py:363
  9.6 0.0 copy-start
  9.6 1.9 %copy-done = bf16[2048,768]{1,0:T(8,128)(2,1)S(1)} copy-done((bf16[2048,768]{1,0:T(8,128)(2,1)S(1)}, bf16[2048,768]{1,0:T(8,128)(2,1)}, u32[]{:S(2)}) %copy-start) | copy-done | bytes 3145752
  11.5 0.0 copy-start.1
  11.5 0.8 copy-done.1
  12.3 0.0 copy-start.3
  12.3 0.8 copy-done.3
  13.0 3.2 %second.1 = (bf16[1168,128]{1,0:T(8,128)(2,1)S(1)}, bf16[1168,128]{1,0:T(8,128)(2,1)S(1)}, bf16[1168,128]{1,0:T(8,128)(2,1)S(1)}) custom-call(s32[3,2048]{1,0:T(4,128)S(1)} %copy-done.1, f32[16,1,512]{2,1,0:T(1,128)S(1)} %copy-done.3, bf16[2048,768]{1,0:T(8,128)(2,1)S(1)} %copy-done), custom_call_target="tpu_custom_call" | custom-call | flops 1811939328 | tf_op jit(solution)/shard_map/second/pallas_call | solution.py:347
  16.2 1.4 %collective-permute-start.1 = (bf16[1168,128]{1,0:T(8,128)(2,1)S(1)}, bf16[1168,128]{1,0:T(8,128)(2,1)S(1)}, u32[]{:S(2)}, u32[]{:S(2)}) collective-permute-start(bf16[1168,128]{1,0:T(8,128)(2,1)S(1)} %get-tuple-element.68), channel_id=1, source_target_pairs={{0,12},{1,13},{2,14},{3,15},{4,8},{5,9},{6,10},{7,11},{8,4},{9,5},... | collective-permute-start | bytes 897032 | tf_op jit(solution)/shard_map/ppermute | solution.py:363
  17.6 0.3 collective-permute-start.2
  17.9 1.3 collective-permute-start.3
  19.3 13.0 %rest.1 = (bf16[1168,128]{1,0:T(8,128)(2,1)S(1)}, bf16[1168,128]{1,0:T(8,128)(2,1)S(1)}, bf16[1168,128]{1,0:T(8,128)(2,1)S(1)}, bf16[1168,128]{1,0:T(8,128)(2,1)...) custom-call(s32[3,2048]{1,0:T(4,128)S(1)} %copy-done.1, ...), custom_call_target="tpu_custom_call" | custom-call | flops 7247757312 | tf_op jit(solution)/shard_map/rest/pallas_call | solution.py:347
  32.2 0.0 collective-permute-done.1.refs_2_
  32.2 2.5 %collective-permute-start.5 = (bf16[1168,128]{1,0:T(8,128)(2,1)S(1)}, bf16[1168,128]{1,0:T(8,128)(2,1)S(1)}, u32[]{:S(2)}, u32[]{:S(2)}) collective-permute-start(bf16[1168,128]{1,0:T(8,128)(2,1)S(1)} %get-tuple-element.83), channel_id=1, source_target_pairs={{0,13},{1,12},{2,15},{3,14},{4,9},{5,8},{6,11},{7,10},{8,5},{9,4},... | collective-permute-start | bytes 897032 | tf_op jit(solution)/shard_map/ppermute | solution.py:363
  34.8 0.0 collective-permute-done.refs_1_
  34.8 17.3 %collective-permute-start.4 = (bf16[1168,128]{1,0:T(8,128)(2,1)S(1)}, bf16[1168,128]{1,0:T(8,128)(2,1)S(1)}, u32[]{:S(2)}, u32[]{:S(2)}) collective-permute-start(bf16[1168,128]{1,0:T(8,128)(2,1)S(1)} %get-tuple-element.79), channel_id=1, source_target_pairs={{0,5},{1,4},{2,7},{3,6},{4,1},{5,0},{6,3},{7,2},{8,13},{9,12},{10,... | collective-permute-start | bytes 897032 | tf_op jit(solution)/shard_map/ppermute | solution.py:363
  52.1 2.7 %collective-permute-done.3.refs_4_ = bf16[1168,128]{1,0:T(8,128)(2,1)S(1)} collective-permute-done((bf16[1168,128]{1,0:T(8,128)(2,1)S(1)}, bf16[1168,128]{1,0:T(8,128)(2,1)S(1)}, u32[]{:S(2)}, u32[]{:S(2)}) %collective-permute-start.3) | collective-permute-done | bytes 299040 | tf_op jit(solution)/shard_map/ppermute | solution.py:363
  54.7 2.4 %collective-permute-start.9 = (bf16[1168,128]{1,0:T(8,128)(2,1)S(1)}, bf16[1168,128]{1,0:T(8,128)(2,1)S(1)}, u32[]{:S(2)}, u32[]{:S(2)}) collective-permute-start(bf16[1168,128]{1,0:T(8,128)(2,1)S(1)} %get-tuple-element.93), channel_id=1, source_target_pairs={{0,10},{1,11},{2,8},{3,9},{4,14},{5,15},{6,12},{7,13},{8,2},{9,3},... | collective-permute-start | bytes 897032 | tf_op jit(solution)/shard_map/ppermute | solution.py:363
  57.1 0.0 collective-permute-done.2.refs_3_
  57.1 3.3 %collective-permute-start.6 = (bf16[1168,128]{1,0:T(8,128)(2,1)S(1)}, bf16[1168,128]{1,0:T(8,128)(2,1)S(1)}, u32[]{:S(2)}, u32[]{:S(2)}) collective-permute-start(bf16[1168,128]{1,0:T(8,128)(2,1)S(1)} %get-tuple-element.87), channel_id=1, source_target_pairs={{0,6},{1,7},{2,4},{3,5},{4,2},{5,3},{6,0},{7,1},{8,14},{9,15},{10,... | collective-permute-start | bytes 897032 | tf_op jit(solution)/shard_map/ppermute | solution.py:363
  60.4 1.5 %collective-permute-start.7 = (bf16[1168,128]{1,0:T(8,128)(2,1)S(1)}, bf16[1168,128]{1,0:T(8,128)(2,1)S(1)}, u32[]{:S(2)}, u32[]{:S(2)}) collective-permute-start(bf16[1168,128]{1,0:T(8,128)(2,1)S(1)} %get-tuple-element.89), channel_id=1, source_target_pairs={{0,2},{1,3},{2,0},{3,1},{4,6},{5,7},{6,4},{7,5},{8,10},{9,11},{10,... | collective-permute-start | bytes 897032 | tf_op jit(solution)/shard_map/ppermute | solution.py:363
  62.0 0.0 collective-permute-done.5.refs_6_
  62.0 0.0 collective-permute-start.8
  62.0 0.0 collective-permute-done.4.refs_5_
  62.0 8.7 %collective-permute-start.10 = (bf16[1168,128]{1,0:T(8,128)(2,1)S(1)}, bf16[1168,128]{1,0:T(8,128)(2,1)S(1)}, u32[]{:S(2)}, u32[]{:S(2)}) collective-permute-start(bf16[1168,128]{1,0:T(8,128)(2,1)S(1)} %get-tuple-element.96), channel_id=1, source_target_pairs={{0,7},{1,6},{2,5},{3,4},{4,3},{5,2},{6,1},{7,0},{8,15},{9,14},{10,... | collective-permute-start | bytes 897032 | tf_op jit(solution)/shard_map/ppermute | solution.py:363
  70.7 1.5 %gram.8 = (f32[16,1,256]{2,1,0:T(1,128)S(1)}, f32[768,256]{1,0:T(8,128)S(1)}) custom-call(bf16[1168,128]{1,0:T(8,128)(2,1)S(1)} %get-tuple-element.63.refs_0_, bf16[1168,128]{1,0:T(8,128)(2,1)S(1)} %collective-permute-done.refs_1_, bf16[1168,128]{1,0:T(8,128)(2,1)S(1)} %collective-permute-done.1.refs_2_, bf16[1168,128]{1,0:T(8,128)(2,1)S(1)} %collective-permute-done.2.refs_3_), custom_call_target="tpu_custom_call" | custom-call | flops 905969664 | bytes 1179648 | tf_op jit(solution)/shard_map/gram/pallas_call | solution.py:372
  72.2 3.7 %collective-permute-done.9.refs_10_ = bf16[1168,128]{1,0:T(8,128)(2,1)S(1)} collective-permute-done((bf16[1168,128]{1,0:T(8,128)(2,1)S(1)}, bf16[1168,128]{1,0:T(8,128)(2,1)S(1)}, u32[]{:S(2)}, u32[]{:S(2)}) %collective-permute-start.9) | collective-permute-done | bytes 299040 | tf_op jit(solution)/shard_map/ppermute | solution.py:363
  75.8 0.0 collective-permute-start.11
  75.8 0.0 collective-permute-done.6.refs_7_
  75.8 3.5 %collective-permute-start.12 = (bf16[1168,128]{1,0:T(8,128)(2,1)S(1)}, bf16[1168,128]{1,0:T(8,128)(2,1)S(1)}, u32[]{:S(2)}, u32[]{:S(2)}) collective-permute-start(bf16[1168,128]{1,0:T(8,128)(2,1)S(1)} %get-tuple-element.98), channel_id=1, source_target_pairs={{0,14},{1,15},{2,12},{3,13},{4,10},{5,11},{6,8},{7,9},{8,6},{9,7},... | collective-permute-start | bytes 897032 | tf_op jit(solution)/shard_map/ppermute | solution.py:363
  79.3 1.3 gram.9
  80.6 1.7 %gram.10 = (f32[16,1,256]{2,1,0:T(1,128)S(1)}, f32[384,256]{1,0:T(8,128)S(1)}) custom-call(bf16[1168,128]{1,0:T(8,128)(2,1)S(1)} %get-tuple-element.63.refs_0_, bf16[1168,128]{1,0:T(8,128)(2,1)S(1)} %collective-permute-done.refs_1_, bf16[1168,128]{1,0:T(8,128)(2,1)S(1)} %collective-permute-done.1.refs_2_, ...), custom_call_target="tpu_custom_call" | custom-call | flops 905969664 | bytes 2359296 | tf_op jit(solution)/shard_map/gram/pallas_call | solution.py:372
  82.4 12.7 %collective-permute-done.7.refs_8_ = bf16[1168,128]{1,0:T(8,128)(2,1)S(1)} collective-permute-done((bf16[1168,128]{1,0:T(8,128)(2,1)S(1)}, bf16[1168,128]{1,0:T(8,128)(2,1)S(1)}, u32[]{:S(2)}, u32[]{:S(2)}) %collective-permute-start.7) | collective-permute-done | bytes 299040 | tf_op jit(solution)/shard_map/ppermute | solution.py:363
  95.1 1.0 collective-permute-start.14
  96.1 10.8 %collective-permute-done.8.refs_9_ = bf16[1168,128]{1,0:T(8,128)(2,1)S(1)} collective-permute-done((bf16[1168,128]{1,0:T(8,128)(2,1)S(1)}, bf16[1168,128]{1,0:T(8,128)(2,1)S(1)}, u32[]{:S(2)}, u32[]{:S(2)}) %collective-permute-start.8) | collective-permute-done | bytes 299040 | tf_op jit(solution)/shard_map/ppermute | solution.py:363
  106.9 0.0 collective-permute-start.13
  106.9 2.1 %gram.11 = (f32[16,1,256]{2,1,0:T(1,128)S(1)}, f32[384,256]{1,0:T(8,128)S(1)}) custom-call(bf16[1168,128]{1,0:T(8,128)(2,1)S(1)} %get-tuple-element.63.refs_0_, bf16[1168,128]{1,0:T(8,128)(2,1)S(1)} %collective-permute-done.refs_1_, bf16[1168,128]{1,0:T(8,128)(2,1)S(1)} %collective-permute-done.1.refs_2_, ...), custom_call_target="tpu_custom_call" | custom-call | flops 1132462080 | bytes 2949120 | tf_op jit(solution)/shard_map/gram/pallas_call | solution.py:372
  109.0 0.0 collective-permute-done.10.refs_11_
  109.0 2.5 %gram.12 = (f32[16,1,256]{2,1,0:T(1,128)S(1)}, f32[384,256]{1,0:T(8,128)S(1)}) custom-call(bf16[1168,128]{1,0:T(8,128)(2,1)S(1)} %get-tuple-element.63.refs_0_, bf16[1168,128]{1,0:T(8,128)(2,1)S(1)} %collective-permute-done.refs_1_, bf16[1168,128]{1,0:T(8,128)(2,1)S(1)} %collective-permute-done.1.refs_2_, ...), custom_call_target="tpu_custom_call" | custom-call | flops 1358954496 | bytes 3538944 | tf_op jit(solution)/shard_map/gram/pallas_call | solution.py:372
  111.5 0.0 collective-permute-done.11.refs_12_
  111.5 0.0 collective-permute-done.12.refs_13_
  111.5 2.9 %gram.13 = (f32[16,1,256]{2,1,0:T(1,128)S(1)}, f32[384,256]{1,0:T(8,128)S(1)}) custom-call(bf16[1168,128]{1,0:T(8,128)(2,1)S(1)} %get-tuple-element.63.refs_0_, bf16[1168,128]{1,0:T(8,128)(2,1)S(1)} %collective-permute-done.refs_1_, bf16[1168,128]{1,0:T(8,128)(2,1)S(1)} %collective-permute-done.1.refs_2_, ...), custom_call_target="tpu_custom_call" | custom-call | flops 1585446912 | bytes 4128768 | tf_op jit(solution)/shard_map/gram/pallas_call | solution.py:372
  114.4 8.1 %collective-permute-done.13.refs_14_ = bf16[1168,128]{1,0:T(8,128)(2,1)S(1)} collective-permute-done((bf16[1168,128]{1,0:T(8,128)(2,1)S(1)}, bf16[1168,128]{1,0:T(8,128)(2,1)S(1)}, u32[]{:S(2)}, u32[]{:S(2)}) %collective-permute-start.13) | collective-permute-done | bytes 299040 | tf_op jit(solution)/shard_map/ppermute | solution.py:363
  122.5 0.0 copy-start.2
  122.5 1.7 %gram.14 = (f32[16,1,256]{2,1,0:T(1,128)S(1)}, f32[192,256]{1,0:T(8,128)S(1)}) custom-call(bf16[1168,128]{1,0:T(8,128)(2,1)S(1)} %get-tuple-element.63.refs_0_, bf16[1168,128]{1,0:T(8,128)(2,1)S(1)} %collective-permute-done.refs_1_, bf16[1168,128]{1,0:T(8,128)(2,1)S(1)} %collective-permute-done.1.refs_2_, ...), custom_call_target="tpu_custom_call" | custom-call | flops 849346560 | bytes 4423680 | tf_op jit(solution)/shard_map/gram/pallas_call | solution.py:372
  124.2 0.0 collective-permute-done.14.refs_15_
  124.2 1.9 %gram.15 = f32[16,1,256]{2,1,0:T(1,128)S(1)} custom-call(bf16[1168,128]{1,0:T(8,128)(2,1)S(1)} %get-tuple-element.63.refs_0_, bf16[1168,128]{1,0:T(8,128)(2,1)S(1)} %collective-permute-done.refs_1_, bf16[1168,128]{1,0:T(8,128)(2,1)S(1)} %collective-permute-done.1.refs_2_, bf16[1168,128]{1,0:T(8,128)(2,1)S(1)} %collective-permute-done.2.refs_3_, ...), custom_call_target="tpu_custom_call" | custom-call | flops 905969664 | bytes 4718592 | tf_op jit(solution)/shard_map/gram/pallas_call | solution.py:372
  126.1 10.8 %all_to_all.5.gains_ref = f32[16,1,256]{2,1,0:T(1,128)S(1)} all-to-all(f32[16,1,256]{2,1,0:T(1,128)S(1)} %gram.15), channel_id=1, replica_groups=mesh['parts'=2,'clus'=16] {'clus'}, dimensions={0} | all-to-all | bytes 32768 | tf_op jit(solution)/shard_map/all_to_all | solution.py:380
  136.9 0.0 copy-done.2
  136.9 1.3 last.1
Async XLA Ops:
  5.5 29.2 %collective-permute-start = (bf16[1168,128]{1,0:T(8,128)(2,1)}, bf16[1168,128]{1,0:T(8,128)(2,1)S(1)}, u32[]{:S(2)}, u32[]{:S(2)}) collective-permute-start(bf16[1168,128]{1,0:T(8,128)(2,1)} %get-tuple-element.65), channel_id=1, source_target_pairs={{0,8},{1,9},{2,10},{3,11},{4,12},{5,13},{6,14},{7,15},{8,0},{9,1},... | collective-permute-start | bytes 897032 | tf_op jit(solution)/shard_map/ppermute | solution.py:363
  9.6 1.9 %copy-start = (bf16[2048,768]{1,0:T(8,128)(2,1)S(1)}, bf16[2048,768]{1,0:T(8,128)(2,1)}, u32[]{:S(2)}) copy-start(bf16[2048,768]{1,0:T(8,128)(2,1)} %get-tuple-element.62.unit_ref) | copy-start | bytes 9437188
  11.5 0.8 copy-start.1
  12.3 0.8 copy-start.3
  16.2 16.0 %collective-permute-start.1 = (bf16[1168,128]{1,0:T(8,128)(2,1)S(1)}, bf16[1168,128]{1,0:T(8,128)(2,1)S(1)}, u32[]{:S(2)}, u32[]{:S(2)}) collective-permute-start(bf16[1168,128]{1,0:T(8,128)(2,1)S(1)} %get-tuple-element.68), channel_id=1, source_target_pairs={{0,12},{1,13},{2,14},{3,15},{4,8},{5,9},{6,10},{7,11},{8,4},{9,5},... | collective-permute-start | bytes 897032 | tf_op jit(solution)/shard_map/ppermute | solution.py:363
  17.6 39.5 %collective-permute-start.2 = (bf16[1168,128]{1,0:T(8,128)(2,1)S(1)}, bf16[1168,128]{1,0:T(8,128)(2,1)S(1)}, u32[]{:S(2)}, u32[]{:S(2)}) collective-permute-start(bf16[1168,128]{1,0:T(8,128)(2,1)S(1)} %get-tuple-element.71), channel_id=1, source_target_pairs={{0,4},{1,5},{2,6},{3,7},{4,0},{5,1},{6,2},{7,3},{8,12},{9,13},{10,... | collective-permute-start | bytes 897032 | tf_op jit(solution)/shard_map/ppermute | solution.py:363
  17.9 36.8 %collective-permute-start.3 = (bf16[1168,128]{1,0:T(8,128)(2,1)S(1)}, bf16[1168,128]{1,0:T(8,128)(2,1)S(1)}, u32[]{:S(2)}, u32[]{:S(2)}) collective-permute-start(bf16[1168,128]{1,0:T(8,128)(2,1)S(1)} %get-tuple-element.75), channel_id=1, source_target_pairs={{0,9},{1,8},{2,11},{3,10},{4,13},{5,12},{6,15},{7,14},{8,1},{9,0},... | collective-permute-start | bytes 897032 | tf_op jit(solution)/shard_map/ppermute | solution.py:363
  32.2 29.7 %collective-permute-start.5 = (bf16[1168,128]{1,0:T(8,128)(2,1)S(1)}, bf16[1168,128]{1,0:T(8,128)(2,1)S(1)}, u32[]{:S(2)}, u32[]{:S(2)}) collective-permute-start(bf16[1168,128]{1,0:T(8,128)(2,1)S(1)} %get-tuple-element.83), channel_id=1, source_target_pairs={{0,13},{1,12},{2,15},{3,14},{4,9},{5,8},{6,11},{7,10},{8,5},{9,4},... | collective-permute-start | bytes 897032 | tf_op jit(solution)/shard_map/ppermute | solution.py:363
  34.8 27.2 %collective-permute-start.4 = (bf16[1168,128]{1,0:T(8,128)(2,1)S(1)}, bf16[1168,128]{1,0:T(8,128)(2,1)S(1)}, u32[]{:S(2)}, u32[]{:S(2)}) collective-permute-start(bf16[1168,128]{1,0:T(8,128)(2,1)S(1)} %get-tuple-element.79), channel_id=1, source_target_pairs={{0,5},{1,4},{2,7},{3,6},{4,1},{5,0},{6,3},{7,2},{8,13},{9,12},{10,... | collective-permute-start | bytes 897032 | tf_op jit(solution)/shard_map/ppermute | solution.py:363
  54.7 21.1 %collective-permute-start.9 = (bf16[1168,128]{1,0:T(8,128)(2,1)S(1)}, bf16[1168,128]{1,0:T(8,128)(2,1)S(1)}, u32[]{:S(2)}, u32[]{:S(2)}) collective-permute-start(bf16[1168,128]{1,0:T(8,128)(2,1)S(1)} %get-tuple-element.93), channel_id=1, source_target_pairs={{0,10},{1,11},{2,8},{3,9},{4,14},{5,15},{6,12},{7,13},{8,2},{9,3},... | collective-permute-start | bytes 897032 | tf_op jit(solution)/shard_map/ppermute | solution.py:363
  57.1 18.7 %collective-permute-start.6 = (bf16[1168,128]{1,0:T(8,128)(2,1)S(1)}, bf16[1168,128]{1,0:T(8,128)(2,1)S(1)}, u32[]{:S(2)}, u32[]{:S(2)}) collective-permute-start(bf16[1168,128]{1,0:T(8,128)(2,1)S(1)} %get-tuple-element.87), channel_id=1, source_target_pairs={{0,6},{1,7},{2,4},{3,5},{4,2},{5,3},{6,0},{7,1},{8,14},{9,15},{10,... | collective-permute-start | bytes 897032 | tf_op jit(solution)/shard_map/ppermute | solution.py:363
  60.4 34.6 %collective-permute-start.7 = (bf16[1168,128]{1,0:T(8,128)(2,1)S(1)}, bf16[1168,128]{1,0:T(8,128)(2,1)S(1)}, u32[]{:S(2)}, u32[]{:S(2)}) collective-permute-start(bf16[1168,128]{1,0:T(8,128)(2,1)S(1)} %get-tuple-element.89), channel_id=1, source_target_pairs={{0,2},{1,3},{2,0},{3,1},{4,6},{5,7},{6,4},{7,5},{8,10},{9,11},{10,... | collective-permute-start | bytes 897032 | tf_op jit(solution)/shard_map/ppermute | solution.py:363
  62.0 44.9 %collective-permute-start.8 = (bf16[1168,128]{1,0:T(8,128)(2,1)S(1)}, bf16[1168,128]{1,0:T(8,128)(2,1)S(1)}, u32[]{:S(2)}, u32[]{:S(2)}) collective-permute-start(bf16[1168,128]{1,0:T(8,128)(2,1)S(1)} %get-tuple-element.90), channel_id=1, source_target_pairs={{0,3},{1,2},{2,1},{3,0},{4,7},{5,6},{6,5},{7,4},{8,11},{9,10},{10,... | collective-permute-start | bytes 897032 | tf_op jit(solution)/shard_map/ppermute | solution.py:363
  62.0 47.0 %collective-permute-start.10 = (bf16[1168,128]{1,0:T(8,128)(2,1)S(1)}, bf16[1168,128]{1,0:T(8,128)(2,1)S(1)}, u32[]{:S(2)}, u32[]{:S(2)}) collective-permute-start(bf16[1168,128]{1,0:T(8,128)(2,1)S(1)} %get-tuple-element.96), channel_id=1, source_target_pairs={{0,7},{1,6},{2,5},{3,4},{4,3},{5,2},{6,1},{7,0},{8,15},{9,14},{10,... | collective-permute-start | bytes 897032 | tf_op jit(solution)/shard_map/ppermute | solution.py:363
  75.8 35.7 %collective-permute-start.11 = (bf16[1168,128]{1,0:T(8,128)(2,1)S(1)}, bf16[1168,128]{1,0:T(8,128)(2,1)S(1)}, u32[]{:S(2)}, u32[]{:S(2)}) collective-permute-start(bf16[1168,128]{1,0:T(8,128)(2,1)S(1)} %get-tuple-element.97), channel_id=1, source_target_pairs={{0,1},{1,0},{2,3},{3,2},{4,5},{5,4},{6,7},{7,6},{8,9},{9,8},{10,11... | collective-permute-start | bytes 897032 | tf_op jit(solution)/shard_map/ppermute | solution.py:363
  75.8 35.7 %collective-permute-start.12 = (bf16[1168,128]{1,0:T(8,128)(2,1)S(1)}, bf16[1168,128]{1,0:T(8,128)(2,1)S(1)}, u32[]{:S(2)}, u32[]{:S(2)}) collective-permute-start(bf16[1168,128]{1,0:T(8,128)(2,1)S(1)} %get-tuple-element.98), channel_id=1, source_target_pairs={{0,14},{1,15},{2,12},{3,13},{4,10},{5,11},{6,8},{7,9},{8,6},{9,7},... | collective-permute-start | bytes 897032 | tf_op jit(solution)/shard_map/ppermute | solution.py:363
  95.1 29.1 %collective-permute-start.14 = (bf16[1168,128]{1,0:T(8,128)(2,1)S(1)}, bf16[1168,128]{1,0:T(8,128)(2,1)S(1)}, u32[]{:S(2)}, u32[]{:S(2)}) collective-permute-start(bf16[1168,128]{1,0:T(8,128)(2,1)S(1)} %get-tuple-element.100), channel_id=1, source_target_pairs={{0,15},{1,14},{2,13},{3,12},{4,11},{5,10},{6,9},{7,8},{8,7},{9,6},... | collective-permute-start | bytes 897032 | tf_op jit(solution)/shard_map/ppermute | solution.py:363
  106.9 15.6 %collective-permute-start.13 = (bf16[1168,128]{1,0:T(8,128)(2,1)S(1)}, bf16[1168,128]{1,0:T(8,128)(2,1)S(1)}, u32[]{:S(2)}, u32[]{:S(2)}) collective-permute-start(bf16[1168,128]{1,0:T(8,128)(2,1)S(1)} %get-tuple-element.99), channel_id=1, source_target_pairs={{0,11},{1,10},{2,9},{3,8},{4,15},{5,14},{6,13},{7,12},{8,3},{9,2},... | collective-permute-start | bytes 897032 | tf_op jit(solution)/shard_map/ppermute | solution.py:363
  122.5 14.4 %copy-start.2 = (s32[3,2048]{1,0:T(4,128)S(1)}, s32[3,2048]{1,0:T(4,128)}, u32[]{:S(2)}) copy-start(s32[3,2048]{1,0:T(4,128)} %get-tuple-element.60.where_ref) | copy-start | bytes 73732

commit v9 on v7

--- a/solution.py
+++ b/solution.py
@@ -178,11 +178,12 @@
 def gram_kernel(devices, cap, offsets, stops, which_stop):
     seg = PARTS * cap
     wide = lanes(seg)
-    per_tile = max(1, 768 // seg)
+    per_tile = max(1, 768 // cap)
     done = stops[which_stop - 1] if which_stop else 0
     new = stops[which_stop]
     xs = list(range(done, new))
-    n = len(xs) * wide
+    m = len(xs)
+    meets = ((0, 1), (0, 1, 2), (1, 2))
     final = new == devices
 
     def kernel(*refs):
@@ -193,8 +194,9 @@
         out_ref = refs[0]
         slabs = (pieces[0].shape[0] - TAIL) // seg
 
-        def rows_of(p):
-            return jnp.concatenate([pieces[p][f * seg : (f + 1) * seg, :] for f in range(slabs)], axis=1)
+        def chunk(p, c):
+            rows = [pieces[p][f * seg + c * cap : f * seg + (c + 1) * cap, :] for f in range(slabs)]
+            return jnp.concatenate(rows, axis=1)
 
         def meta_of(p):
             tail = pieces[p][slabs * seg :, :].astype(jnp.float32)
@@ -203,12 +205,16 @@
             return jnp.concatenate(parts[:half], axis=1), jnp.concatenate(parts[half:], axis=1)
 
         metas = [meta_of(p) for p in xs]
-        right = jnp.concatenate([pad_rows(rows_of(p), wide) for p in xs], axis=0)
-        right_cover = jnp.concatenate([m[0] for m in metas], axis=1)
-        right_which = jnp.concatenate([m[1] for m in metas], axis=1)
-        lane = lax.broadcasted_iota(jnp.int32, (1, wide), 1)
-        inside = jnp.concatenate([lane < seg] * len(xs), axis=1)
-        right_which = jnp.where(inside, right_which, -1.0)
+        right, right_cover, right_which, down = [], [], [], []
+        for meet in meets:
+            n = lanes(len(meet) * m * cap)
+            fill = [jnp.full((1, n - len(meet) * m * cap), -1.0, jnp.float32)]
+            fill = fill if fill[0].shape[1] else []
+            right.append(pad_rows(jnp.concatenate([chunk(p, c) for c in meet for p in xs], axis=0), n))
+            rows = [[meta[v][:, c * cap : (c + 1) * cap] for c in meet for meta in metas] for v in (0, 1)]
+            right_cover.append(jnp.concatenate(rows[0] + fill, axis=1))
+            right_which.append(jnp.concatenate(rows[1] + fill, axis=1))
+            down.append(jnp.zeros((8, n), jnp.float32))
         cover_cols, which_cols = {}, {}
         first = 0
         for g in range(which_stop):
@@ -223,31 +229,44 @@
             if not final:
                 refs[1][i * seg : (i + 1) * seg, :128] = cover_cols[p]
                 refs[1][i * seg : (i + 1) * seg, 128:] = which_cols[p]
-        down = jnp.zeros((8, n), jnp.float32)
-        total = {}
+        total, found = {}, {}
         for start in range(0, new, per_tile):
             members = range(start, min(start + per_tile, new))
-            left = jnp.concatenate([rows_of(p) for p in members], axis=0)
-            similar = dot(left, right, NT)
-            count = len(members) * seg
-            which = jnp.concatenate([which_cols[p] for p in members], axis=0)
-            cover = jnp.concatenate([cover_cols[p] for p in members], axis=0)
-            similar = jnp.where(repeat(which, n) == right_which, similar, -1e30)
-            gain = jnp.maximum(similar - repeat(cover, n), 0.0)
-            down = down + jnp.sum(gain.reshape(count // 8, 8, n), axis=0)
             old = [p for p in members if p < done]
-            if not old:
-                continue
-            other = jnp.maximum(similar[: len(old) * seg] - right_cover, 0.0)
-            part = other[:, :128]
-            for begin in range(128, n, 128):
-                part = part + other[:, begin : begin + 128]
-            for i, p in enumerate(old):
-                mine = pad_rows(part[i * seg : (i + 1) * seg], wide)
-                total[p] = jnp.sum(jnp.transpose(mine), axis=0, keepdims=True)
-        down = jnp.sum(down, axis=0, keepdims=True)
+            for c, meet in enumerate(meets):
+                n = right[c].shape[0]
+                part = slice(c * cap, (c + 1) * cap)
+                left = jnp.concatenate([chunk(p, c) for p in members], axis=0)
+                similar = dot(left, right[c], NT)
+                which = jnp.concatenate([which_cols[p][part] for p in members], axis=0)
+                cover = jnp.concatenate([cover_cols[p][part] for p in members], axis=0)
+                similar = jnp.where(repeat(which, n) == right_which[c], similar, -1e30)
+                gain = jnp.maximum(similar - repeat(cover, n), 0.0)
+                down[c] = down[c] + jnp.sum(gain.reshape(left.shape[0] // 8, 8, n), axis=0)
+                if not old:
+                    continue
+                other = jnp.maximum(similar[: len(old) * cap] - right_cover[c], 0.0)
+                folded = other[:, :128]
+                for begin in range(128, n, 128):
+                    folded = folded + other[:, begin : begin + 128]
+                for i, p in enumerate(old):
+                    found[p, c] = folded[i * cap : (i + 1) * cap]
+        for p in range(done):
+            mine = pad_rows(jnp.concatenate([found[p, c] for c in range(PARTS)], axis=0), wide)
+            total[p] = jnp.sum(jnp.transpose(mine), axis=0, keepdims=True)
+        down = [jnp.sum(d, axis=0, keepdims=True) for d in down]
         for i, p in enumerate(xs):
-            total[p] = down[:, i * wide : (i + 1) * wide]
+            values = []
+            for c in range(PARTS):
+                value = jnp.zeros((1, cap), jnp.float32)
+                for d, meet in zip(down, meets):
+                    if c in meet:
+                        begin = (meet.index(c) * m + i) * cap
+                        value = value + d[:, begin : begin + cap]
+                values.append(value)
+            if wide > seg:
+                values.append(jnp.zeros((1, wide - seg), jnp.float32))
+            total[p] = jnp.concatenate(values, axis=1)
         me = lax.axis_index("clus")
         for p in range(new):
             value = total[p]

time: 128 us -> 128 us (level)
  Pallas kernels: 38.6 us -> 34.9 us
  waiting for transfers between devices: 47.1 us -> 49.6 us
    pallas_call x8, Pallas kernels: 15.7 us -> 12 us  [body(): call(gram_kernel(devices, cap, offsets, stops, g), [gain_shape] + [S((fre...]
    ppermute x15, waiting for transfers between devices: 47.1 us -> 49.6 us  [body(): lax.ppermute(x, 'clus', [(d, d ^ offsets[1 + i]) for d in range(devices)])]
  transfers between devices with their start and end apart: 15 -> 15, of which waited for: 6 -> 6; matrix products, arithmetic and copies ran while one was open for 0% -> 0% of each run, Pallas kernels for 23% -> 21%
where the time goes in v9:
time: 128 us; the launch traced here: 127 us
  waiting for transfers between devices  49.6 us (39%)
  Pallas kernels  34.9 us (27%)
  starting transfers between devices  25.3 us (20%)
  blocking collectives  14 us (11%)
  local copies, waits for them, and re-layouts  3.41 us (3%)
    ppermute x15, waiting for transfers between devices, body(): lax.ppermute(x, 'clus', [(d, d ^ offsets[1 + i]) for d in range(devices)])  49.6 us
    ppermute x15, starting transfers between devices, body(): lax.ppermute(x, 'clus', [(d, d ^ offsets[1 + i]) for d in range(devices)])  25.3 us
    pallas_call x2, Pallas kernels, body(): call(rest_kernel(devices, cap, ks), [piece] * len(ks), (0, 0), name, in_s...  16.1 us
    all_to_all x1, blocking collectives, body(): back = lax.all_to_all(gains, 'clus', 0, 0, tiled=True)  14 us
    pallas_call x8, Pallas kernels, body(): call(gram_kernel(devices, cap, offsets, stops, g), [gain_shape] + [S((fre...  12 us
    pallas_call x1, Pallas kernels, body(): call(first_kernel(devices, cap, steps, offsets[1:1 + early]), [S((rows, w...  5.53 us
    unnamed x8, local copies, waits for them, and re-layouts  3.41 us
  transfers between devices with their start and end apart: 15, of which 6 were waited for; matrix products, arithmetic and copies ran while one was open for 0% of the time, Pallas kernels for 21%

profile of v9, /device:TPU:0, one launch (start us, length us, event | category | flops | bytes accessed | tf_op | source)
XLA Modules:
  0.0 127.3 jit_solution(4579269000199344310)
XLA Ops:
  0.0 5.5 %first.1 = (bf16[2048,768]{1,0:T(8,128)(2,1)}, s32[3,2048]{1,0:T(4,128)}, f32[16,1,512]{2,1,0:T(1,128)}, bf16[1168,128]{1,0:T(8,128)(2,1)}) custom-call(s32[1,2048]{1,0:T(1,128)} %bitcast.3, bf16[16,128]{1,0:T(8,128)(2,1)} %bitcast.4, f32[2048,768]{1,0:T(8,128)} %emb_ref.1), custom_call_target="tpu_custom_call" | custom-call | flops 603979776 | bytes 6291456 | tf_op jit(solution)/shard_map/first/pallas_call | solution.py:350
  5.5 4.1 %collective-permute-start = (bf16[1168,128]{1,0:T(8,128)(2,1)}, bf16[1168,128]{1,0:T(8,128)(2,1)S(1)}, u32[]{:S(2)}, u32[]{:S(2)}) collective-permute-start(bf16[1168,128]{1,0:T(8,128)(2,1)} %get-tuple-element.65), channel_id=1, source_target_pairs={{0,8},{1,9},{2,10},{3,11},{4,12},{5,13},{6,14},{7,15},{8,0},{9,1},... | collective-permute-start | bytes 897032 | tf_op jit(solution)/shard_map/ppermute | solution.py:381
  9.6 0.0 copy-start
  9.6 1.9 %copy-done = bf16[2048,768]{1,0:T(8,128)(2,1)S(1)} copy-done((bf16[2048,768]{1,0:T(8,128)(2,1)S(1)}, bf16[2048,768]{1,0:T(8,128)(2,1)}, u32[]{:S(2)}) %copy-start) | copy-done | bytes 3145752
  11.5 0.0 copy-start.1
  11.5 0.8 copy-done.1
  12.3 0.0 copy-start.3
  12.3 0.8 copy-done.3
  13.0 3.2 %second.1 = (bf16[1168,128]{1,0:T(8,128)(2,1)S(1)}, bf16[1168,128]{1,0:T(8,128)(2,1)S(1)}, bf16[1168,128]{1,0:T(8,128)(2,1)S(1)}) custom-call(s32[3,2048]{1,0:T(4,128)S(1)} %copy-done.1, f32[16,1,512]{2,1,0:T(1,128)S(1)} %copy-done.3, bf16[2048,768]{1,0:T(8,128)(2,1)S(1)} %copy-done), custom_call_target="tpu_custom_call" | custom-call | tf_op jit(solution)/shard_map/second/pallas_call | solution.py:366
  16.2 1.6 %collective-permute-start.2 = (bf16[1168,128]{1,0:T(8,128)(2,1)S(1)}, bf16[1168,128]{1,0:T(8,128)(2,1)S(1)}, u32[]{:S(2)}, u32[]{:S(2)}) collective-permute-start(bf16[1168,128]{1,0:T(8,128)(2,1)S(1)} %get-tuple-element.71), channel_id=1, source_target_pairs={{0,4},{1,5},{2,6},{3,7},{4,0},{5,1},{6,2},{7,3},{8,12},{9,13},{10,... | collective-permute-start | bytes 897032 | tf_op jit(solution)/shard_map/ppermute | solution.py:381
  17.9 0.0 collective-permute-start.1
  17.9 0.5 collective-permute-start.3
  18.4 13.0 %rest.1 = (bf16[1168,128]{1,0:T(8,128)(2,1)S(1)}, bf16[1168,128]{1,0:T(8,128)(2,1)S(1)}, bf16[1168,128]{1,0:T(8,128)(2,1)S(1)}, bf16[1168,128]{1,0:T(8,128)(2,1)...) custom-call(s32[3,2048]{1,0:T(4,128)S(1)} %copy-done.1, ...), custom_call_target="tpu_custom_call" | custom-call | tf_op jit(solution)/shard_map/rest/pallas_call | solution.py:366
  31.3 0.0 collective-permute-done.refs_1_
  31.4 3.7 %collective-permute-start.4 = (bf16[1168,128]{1,0:T(8,128)(2,1)S(1)}, bf16[1168,128]{1,0:T(8,128)(2,1)S(1)}, u32[]{:S(2)}, u32[]{:S(2)}) collective-permute-start(bf16[1168,128]{1,0:T(8,128)(2,1)S(1)} %get-tuple-element.77), channel_id=1, source_target_pairs={{0,5},{1,4},{2,7},{3,6},{4,1},{5,0},{6,3},{7,2},{8,13},{9,12},{10,... | collective-permute-start | bytes 897032 | tf_op jit(solution)/shard_map/ppermute | solution.py:381
  35.0 1.2 collective-permute-done.2.refs_3_
  36.2 0.6 collective-permute-start.6
  36.7 0.0 collective-permute-done.1.refs_2_
  36.7 1.2 collective-permute-start.5
  37.9 10.4 %collective-permute-done.3.refs_4_ = bf16[1168,128]{1,0:T(8,128)(2,1)S(1)} collective-permute-done((bf16[1168,128]{1,0:T(8,128)(2,1)S(1)}, bf16[1168,128]{1,0:T(8,128)(2,1)S(1)}, u32[]{:S(2)}, u32[]{:S(2)}) %collective-permute-start.3) | collective-permute-done | bytes 299040 | tf_op jit(solution)/shard_map/ppermute | solution.py:381
  48.3 3.4 %collective-permute-start.7 = (bf16[1168,128]{1,0:T(8,128)(2,1)S(1)}, bf16[1168,128]{1,0:T(8,128)(2,1)S(1)}, u32[]{:S(2)}, u32[]{:S(2)}) collective-permute-start(bf16[1168,128]{1,0:T(8,128)(2,1)S(1)} %get-tuple-element.86), channel_id=1, source_target_pairs={{0,10},{1,11},{2,8},{3,9},{4,14},{5,15},{6,12},{7,13},{8,2},{9,3},... | collective-permute-start | bytes 897032 | tf_op jit(solution)/shard_map/ppermute | solution.py:381
  51.7 0.0 collective-permute-done.4.refs_5_
  51.7 2.2 %collective-permute-start.8 = (bf16[1168,128]{1,0:T(8,128)(2,1)S(1)}, bf16[1168,128]{1,0:T(8,128)(2,1)S(1)}, u32[]{:S(2)}, u32[]{:S(2)}) collective-permute-start(bf16[1168,128]{1,0:T(8,128)(2,1)S(1)} %get-tuple-element.89), channel_id=1, source_target_pairs={{0,7},{1,6},{2,5},{3,4},{4,3},{5,2},{6,1},{7,0},{8,15},{9,14},{10,... | collective-permute-start | bytes 897032 | tf_op jit(solution)/shard_map/ppermute | solution.py:381
  53.9 8.8 %collective-permute-done.6.refs_7_ = bf16[1168,128]{1,0:T(8,128)(2,1)S(1)} collective-permute-done((bf16[1168,128]{1,0:T(8,128)(2,1)S(1)}, bf16[1168,128]{1,0:T(8,128)(2,1)S(1)}, u32[]{:S(2)}, u32[]{:S(2)}) %collective-permute-start.6) | collective-permute-done | bytes 299040 | tf_op jit(solution)/shard_map/ppermute | solution.py:381
  62.7 0.4 collective-permute-start.10
  63.1 0.0 collective-permute-done.5.refs_6_
  63.1 4.8 %collective-permute-start.9 = (bf16[1168,128]{1,0:T(8,128)(2,1)S(1)}, bf16[1168,128]{1,0:T(8,128)(2,1)S(1)}, u32[]{:S(2)}, u32[]{:S(2)}) collective-permute-start(bf16[1168,128]{1,0:T(8,128)(2,1)S(1)} %get-tuple-element.92), channel_id=1, source_target_pairs={{0,14},{1,15},{2,12},{3,13},{4,10},{5,11},{6,8},{7,9},{8,6},{9,7},... | collective-permute-start | bytes 897032 | tf_op jit(solution)/shard_map/ppermute | solution.py:381
  67.9 1.1 gram.8
  69.0 14.3 %collective-permute-done.7.refs_8_ = bf16[1168,128]{1,0:T(8,128)(2,1)S(1)} collective-permute-done((bf16[1168,128]{1,0:T(8,128)(2,1)S(1)}, bf16[1168,128]{1,0:T(8,128)(2,1)S(1)}, u32[]{:S(2)}, u32[]{:S(2)}) %collective-permute-start.7) | collective-permute-done | bytes 299040 | tf_op jit(solution)/shard_map/ppermute | solution.py:381
  83.2 0.0 collective-permute-start.11
  83.2 1.0 gram.9
  84.3 0.0 collective-permute-done.8.refs_9_
  84.3 0.1 collective-permute-start.12
  84.3 1.3 %gram.10 = (f32[16,1,256]{2,1,0:T(1,128)S(1)}, f32[384,256]{1,0:T(8,128)S(1)}) custom-call(bf16[1168,128]{1,0:T(8,128)(2,1)S(1)} %get-tuple-element.63.refs_0_, bf16[1168,128]{1,0:T(8,128)(2,1)S(1)} %collective-permute-done.refs_1_, bf16[1168,128]{1,0:T(8,128)(2,1)S(1)} %collective-permute-done.1.refs_2_, ...), custom_call_target="tpu_custom_call" | custom-call | flops 905969664 | bytes 2359296 | tf_op jit(solution)/shard_map/gram/pallas_call | solution.py:389
  85.6 2.9 %collective-permute-done.10.refs_11_ = bf16[1168,128]{1,0:T(8,128)(2,1)S(1)} collective-permute-done((bf16[1168,128]{1,0:T(8,128)(2,1)S(1)}, bf16[1168,128]{1,0:T(8,128)(2,1)S(1)}, u32[]{:S(2)}, u32[]{:S(2)}) %collective-permute-start.10) | collective-permute-done | bytes 299040 | tf_op jit(solution)/shard_map/ppermute | solution.py:381
  88.5 2.2 %collective-permute-start.14 = (bf16[1168,128]{1,0:T(8,128)(2,1)S(1)}, bf16[1168,128]{1,0:T(8,128)(2,1)S(1)}, u32[]{:S(2)}, u32[]{:S(2)}) collective-permute-start(bf16[1168,128]{1,0:T(8,128)(2,1)S(1)} %get-tuple-element.100), channel_id=1, source_target_pairs={{0,15},{1,14},{2,13},{3,12},{4,11},{5,10},{6,9},{7,8},{8,7},{9,6},... | collective-permute-start | bytes 897032 | tf_op jit(solution)/shard_map/ppermute | solution.py:381
  90.7 0.0 collective-permute-done.9.refs_10_
  90.7 0.6 collective-permute-start.13
  91.3 1.5 %gram.11 = (f32[16,1,256]{2,1,0:T(1,128)S(1)}, f32[384,256]{1,0:T(8,128)S(1)}) custom-call(bf16[1168,128]{1,0:T(8,128)(2,1)S(1)} %get-tuple-element.63.refs_0_, bf16[1168,128]{1,0:T(8,128)(2,1)S(1)} %collective-permute-done.refs_1_, bf16[1168,128]{1,0:T(8,128)(2,1)S(1)} %collective-permute-done.1.refs_2_, ...), custom_call_target="tpu_custom_call" | custom-call | flops 1132462080 | bytes 2949120 | tf_op jit(solution)/shard_map/gram/pallas_call | solution.py:389
  92.8 1.8 %gram.12 = (f32[16,1,256]{2,1,0:T(1,128)S(1)}, f32[384,256]{1,0:T(8,128)S(1)}) custom-call(bf16[1168,128]{1,0:T(8,128)(2,1)S(1)} %get-tuple-element.63.refs_0_, bf16[1168,128]{1,0:T(8,128)(2,1)S(1)} %collective-permute-done.refs_1_, bf16[1168,128]{1,0:T(8,128)(2,1)S(1)} %collective-permute-done.1.refs_2_, ...), custom_call_target="tpu_custom_call" | custom-call | flops 1358954496 | bytes 3538944 | tf_op jit(solution)/shard_map/gram/pallas_call | solution.py:389
  94.6 12.0 %collective-permute-done.11.refs_12_ = bf16[1168,128]{1,0:T(8,128)(2,1)S(1)} collective-permute-done((bf16[1168,128]{1,0:T(8,128)(2,1)S(1)}, bf16[1168,128]{1,0:T(8,128)(2,1)S(1)}, u32[]{:S(2)}, u32[]{:S(2)}) %collective-permute-start.11) | collective-permute-done | bytes 299040 | tf_op jit(solution)/shard_map/ppermute | solution.py:381
  106.7 0.0 collective-permute-done.12.refs_13_
  106.7 2.1 %gram.13 = (f32[16,1,256]{2,1,0:T(1,128)S(1)}, f32[384,256]{1,0:T(8,128)S(1)}) custom-call(bf16[1168,128]{1,0:T(8,128)(2,1)S(1)} %get-tuple-element.63.refs_0_, bf16[1168,128]{1,0:T(8,128)(2,1)S(1)} %collective-permute-done.refs_1_, bf16[1168,128]{1,0:T(8,128)(2,1)S(1)} %collective-permute-done.1.refs_2_, ...), custom_call_target="tpu_custom_call" | custom-call | flops 1585446912 | bytes 4128768 | tf_op jit(solution)/shard_map/gram/pallas_call | solution.py:389
  108.7 0.0 collective-permute-done.13.refs_14_
  108.7 0.0 copy-start.2
  108.7 1.6 %gram.14 = (f32[16,1,256]{2,1,0:T(1,128)S(1)}, f32[192,256]{1,0:T(8,128)S(1)}) custom-call(bf16[1168,128]{1,0:T(8,128)(2,1)S(1)} %get-tuple-element.63.refs_0_, bf16[1168,128]{1,0:T(8,128)(2,1)S(1)} %collective-permute-done.refs_1_, bf16[1168,128]{1,0:T(8,128)(2,1)S(1)} %collective-permute-done.1.refs_2_, ...), custom_call_target="tpu_custom_call" | custom-call | flops 849346560 | bytes 4423680 | tf_op jit(solution)/shard_map/gram/pallas_call | solution.py:389
  110.3 0.0 collective-permute-done.14.refs_15_
  110.3 1.7 %gram.15 = f32[16,1,256]{2,1,0:T(1,128)S(1)} custom-call(bf16[1168,128]{1,0:T(8,128)(2,1)S(1)} %get-tuple-element.63.refs_0_, bf16[1168,128]{1,0:T(8,128)(2,1)S(1)} %collective-permute-done.refs_1_, bf16[1168,128]{1,0:T(8,128)(2,1)S(1)} %collective-permute-done.1.refs_2_, bf16[1168,128]{1,0:T(8,128)(2,1)S(1)} %collective-permute-done.2.refs_3_, ...), custom_call_target="tpu_custom_call" | custom-call | flops 905969664 | bytes 4718592 | tf_op jit(solution)/shard_map/gram/pallas_call | solution.py:389
  112.0 14.0 %all_to_all.5.gains_ref = f32[16,1,256]{2,1,0:T(1,128)S(1)} all-to-all(f32[16,1,256]{2,1,0:T(1,128)S(1)} %gram.15), channel_id=1, replica_groups=mesh['parts'=2,'clus'=16] {'clus'}, dimensions={0} | all-to-all | bytes 32768 | tf_op jit(solution)/shard_map/all_to_all | solution.py:397
  126.0 0.0 copy-done.2
  126.0 1.3 last.1
Async XLA Ops:
  5.5 25.8 %collective-permute-start = (bf16[1168,128]{1,0:T(8,128)(2,1)}, bf16[1168,128]{1,0:T(8,128)(2,1)S(1)}, u32[]{:S(2)}, u32[]{:S(2)}) collective-permute-start(bf16[1168,128]{1,0:T(8,128)(2,1)} %get-tuple-element.65), channel_id=1, source_target_pairs={{0,8},{1,9},{2,10},{3,11},{4,12},{5,13},{6,14},{7,15},{8,0},{9,1},... | collective-permute-start | bytes 897032 | tf_op jit(solution)/shard_map/ppermute | solution.py:381
  9.6 1.9 %copy-start = (bf16[2048,768]{1,0:T(8,128)(2,1)S(1)}, bf16[2048,768]{1,0:T(8,128)(2,1)}, u32[]{:S(2)}) copy-start(bf16[2048,768]{1,0:T(8,128)(2,1)} %get-tuple-element.62.unit_ref) | copy-start | bytes 9437188
  11.5 0.8 copy-start.1
  12.3 0.8 copy-start.3
  16.2 20.0 %collective-permute-start.2 = (bf16[1168,128]{1,0:T(8,128)(2,1)S(1)}, bf16[1168,128]{1,0:T(8,128)(2,1)S(1)}, u32[]{:S(2)}, u32[]{:S(2)}) collective-permute-start(bf16[1168,128]{1,0:T(8,128)(2,1)S(1)} %get-tuple-element.71), channel_id=1, source_target_pairs={{0,4},{1,5},{2,6},{3,7},{4,0},{5,1},{6,2},{7,3},{8,12},{9,13},{10,... | collective-permute-start | bytes 897032 | tf_op jit(solution)/shard_map/ppermute | solution.py:381
  17.9 18.9 %collective-permute-start.1 = (bf16[1168,128]{1,0:T(8,128)(2,1)S(1)}, bf16[1168,128]{1,0:T(8,128)(2,1)S(1)}, u32[]{:S(2)}, u32[]{:S(2)}) collective-permute-start(bf16[1168,128]{1,0:T(8,128)(2,1)S(1)} %get-tuple-element.68), channel_id=1, source_target_pairs={{0,12},{1,13},{2,14},{3,15},{4,8},{5,9},{6,10},{7,11},{8,4},{9,5},... | collective-permute-start | bytes 897032 | tf_op jit(solution)/shard_map/ppermute | solution.py:381
  17.9 30.4 %collective-permute-start.3 = (bf16[1168,128]{1,0:T(8,128)(2,1)S(1)}, bf16[1168,128]{1,0:T(8,128)(2,1)S(1)}, u32[]{:S(2)}, u32[]{:S(2)}) collective-permute-start(bf16[1168,128]{1,0:T(8,128)(2,1)S(1)} %get-tuple-element.74), channel_id=1, source_target_pairs={{0,9},{1,8},{2,11},{3,10},{4,13},{5,12},{6,15},{7,14},{8,1},{9,0},... | collective-permute-start | bytes 897032 | tf_op jit(solution)/shard_map/ppermute | solution.py:381
  31.4 20.3 %collective-permute-start.4 = (bf16[1168,128]{1,0:T(8,128)(2,1)S(1)}, bf16[1168,128]{1,0:T(8,128)(2,1)S(1)}, u32[]{:S(2)}, u32[]{:S(2)}) collective-permute-start(bf16[1168,128]{1,0:T(8,128)(2,1)S(1)} %get-tuple-element.77), channel_id=1, source_target_pairs={{0,5},{1,4},{2,7},{3,6},{4,1},{5,0},{6,3},{7,2},{8,13},{9,12},{10,... | collective-permute-start | bytes 897032 | tf_op jit(solution)/shard_map/ppermute | solution.py:381
  36.2 26.5 %collective-permute-start.6 = (bf16[1168,128]{1,0:T(8,128)(2,1)S(1)}, bf16[1168,128]{1,0:T(8,128)(2,1)S(1)}, u32[]{:S(2)}, u32[]{:S(2)}) collective-permute-start(bf16[1168,128]{1,0:T(8,128)(2,1)S(1)} %get-tuple-element.83), channel_id=1, source_target_pairs={{0,6},{1,7},{2,4},{3,5},{4,2},{5,3},{6,0},{7,1},{8,14},{9,15},{10,... | collective-permute-start | bytes 897032 | tf_op jit(solution)/shard_map/ppermute | solution.py:381
  36.7 26.4 %collective-permute-start.5 = (bf16[1168,128]{1,0:T(8,128)(2,1)S(1)}, bf16[1168,128]{1,0:T(8,128)(2,1)S(1)}, u32[]{:S(2)}, u32[]{:S(2)}) collective-permute-start(bf16[1168,128]{1,0:T(8,128)(2,1)S(1)} %get-tuple-element.80), channel_id=1, source_target_pairs={{0,13},{1,12},{2,15},{3,14},{4,9},{5,8},{6,11},{7,10},{8,5},{9,4},... | collective-permute-start | bytes 897032 | tf_op jit(solution)/shard_map/ppermute | solution.py:381
  48.3 34.9 %collective-permute-start.7 = (bf16[1168,128]{1,0:T(8,128)(2,1)S(1)}, bf16[1168,128]{1,0:T(8,128)(2,1)S(1)}, u32[]{:S(2)}, u32[]{:S(2)}) collective-permute-start(bf16[1168,128]{1,0:T(8,128)(2,1)S(1)} %get-tuple-element.86), channel_id=1, source_target_pairs={{0,10},{1,11},{2,8},{3,9},{4,14},{5,15},{6,12},{7,13},{8,2},{9,3},... | collective-permute-start | bytes 897032 | tf_op jit(solution)/shard_map/ppermute | solution.py:381
  51.7 32.6 %collective-permute-start.8 = (bf16[1168,128]{1,0:T(8,128)(2,1)S(1)}, bf16[1168,128]{1,0:T(8,128)(2,1)S(1)}, u32[]{:S(2)}, u32[]{:S(2)}) collective-permute-start(bf16[1168,128]{1,0:T(8,128)(2,1)S(1)} %get-tuple-element.89), channel_id=1, source_target_pairs={{0,7},{1,6},{2,5},{3,4},{4,3},{5,2},{6,1},{7,0},{8,15},{9,14},{10,... | collective-permute-start | bytes 897032 | tf_op jit(solution)/shard_map/ppermute | solution.py:381
  62.7 25.8 %collective-permute-start.10 = (bf16[1168,128]{1,0:T(8,128)(2,1)S(1)}, bf16[1168,128]{1,0:T(8,128)(2,1)S(1)}, u32[]{:S(2)}, u32[]{:S(2)}) collective-permute-start(bf16[1168,128]{1,0:T(8,128)(2,1)S(1)} %get-tuple-element.95), channel_id=1, source_target_pairs={{0,2},{1,3},{2,0},{3,1},{4,6},{5,7},{6,4},{7,5},{8,10},{9,11},{10,... | collective-permute-start | bytes 897032 | tf_op jit(solution)/shard_map/ppermute | solution.py:381
  63.1 27.6 %collective-permute-start.9 = (bf16[1168,128]{1,0:T(8,128)(2,1)S(1)}, bf16[1168,128]{1,0:T(8,128)(2,1)S(1)}, u32[]{:S(2)}, u32[]{:S(2)}) collective-permute-start(bf16[1168,128]{1,0:T(8,128)(2,1)S(1)} %get-tuple-element.92), channel_id=1, source_target_pairs={{0,14},{1,15},{2,12},{3,13},{4,10},{5,11},{6,8},{7,9},{8,6},{9,7},... | collective-permute-start | bytes 897032 | tf_op jit(solution)/shard_map/ppermute | solution.py:381
  83.2 23.4 %collective-permute-start.11 = (bf16[1168,128]{1,0:T(8,128)(2,1)S(1)}, bf16[1168,128]{1,0:T(8,128)(2,1)S(1)}, u32[]{:S(2)}, u32[]{:S(2)}) collective-permute-start(bf16[1168,128]{1,0:T(8,128)(2,1)S(1)} %get-tuple-element.97), channel_id=1, source_target_pairs={{0,11},{1,10},{2,9},{3,8},{4,15},{5,14},{6,13},{7,12},{8,3},{9,2},... | collective-permute-start | bytes 897032 | tf_op jit(solution)/shard_map/ppermute | solution.py:381
  84.3 22.4 %collective-permute-start.12 = (bf16[1168,128]{1,0:T(8,128)(2,1)S(1)}, bf16[1168,128]{1,0:T(8,128)(2,1)S(1)}, u32[]{:S(2)}, u32[]{:S(2)}) collective-permute-start(bf16[1168,128]{1,0:T(8,128)(2,1)S(1)} %get-tuple-element.98), channel_id=1, source_target_pairs={{0,3},{1,2},{2,1},{3,0},{4,7},{5,6},{6,5},{7,4},{8,11},{9,10},{10,... | collective-permute-start | bytes 897032 | tf_op jit(solution)/shard_map/ppermute | solution.py:381
  88.5 21.8 %collective-permute-start.14 = (bf16[1168,128]{1,0:T(8,128)(2,1)S(1)}, bf16[1168,128]{1,0:T(8,128)(2,1)S(1)}, u32[]{:S(2)}, u32[]{:S(2)}) collective-permute-start(bf16[1168,128]{1,0:T(8,128)(2,1)S(1)} %get-tuple-element.100), channel_id=1, source_target_pairs={{0,15},{1,14},{2,13},{3,12},{4,11},{5,10},{6,9},{7,8},{8,7},{9,6},... | collective-permute-start | bytes 897032 | tf_op jit(solution)/shard_map/ppermute | solution.py:381
  90.7 18.0 %collective-permute-start.13 = (bf16[1168,128]{1,0:T(8,128)(2,1)S(1)}, bf16[1168,128]{1,0:T(8,128)(2,1)S(1)}, u32[]{:S(2)}, u32[]{:S(2)}) collective-permute-start(bf16[1168,128]{1,0:T(8,128)(2,1)S(1)} %get-tuple-element.99), channel_id=1, source_target_pairs={{0,1},{1,0},{2,3},{3,2},{4,5},{5,4},{6,7},{7,6},{8,9},{9,8},{10,11... | collective-permute-start | bytes 897032 | tf_op jit(solution)/shard_map/ppermute | solution.py:381
  108.7 17.3 %copy-start.2 = (s32[3,2048]{1,0:T(4,128)S(1)}, s32[3,2048]{1,0:T(4,128)}, u32[]{:S(2)}) copy-start(s32[3,2048]{1,0:T(4,128)} %get-tuple-element.60.where_ref) | copy-start | bytes 73732

commit v10 on v9

--- a/solution.py
+++ b/solution.py
@@ -106,10 +106,14 @@
         cover = cover_ref[...].astype(jnp.float32)
         cover = jnp.concatenate([cover[i : i + 1] for i in range(cover.shape[0])], axis=1)
         which = (ids - owner * CL_DEV).astype(jnp.float32)
-        meta_ref[:, 0, :wide] = dot(own * cover.astype(jnp.bfloat16), there, NT)
-        meta_ref[:, 0, wide:] = dot(own * which.astype(jnp.bfloat16), there, NT)
+        both = [own * cover.astype(jnp.bfloat16), own * which.astype(jnp.bfloat16)]
+        both = dot(jnp.concatenate(both, axis=0), there, NT)
+        meta_ref[:, 0, :wide] = both[:devices]
+        meta_ref[:, 0, wide:] = both[devices:]
         small[2].start()
         small[3].start()
+        picks = [hot(code, seg, (me ^ k) * seg) for k in offsets]
+        found = [jnp.zeros((seg, rows_ref.shape[1]), jnp.float32) for _ in offsets]
         for i in range(steps):
             load(i).wait()
             if i == steps - 1:
@@ -119,8 +123,10 @@
             sums = jnp.sum(raw * raw, axis=-1, keepdims=True)
             unit = (raw * lax.rsqrt(sums + 1e-06)).astype(jnp.bfloat16)
             rows_ref[i * block : (i + 1) * block, :] = unit
+            for j, pick in enumerate(picks):
+                found[j] = found[j] + dot(pick[:, i * block : (i + 1) * block], unit, NN)
         store(steps - 1).start()
-        send_pieces(code, rows_ref, meta_ref, seg, me, offsets, outs, piece_ref, out_sems)
+        send_pieces(found, meta_ref, seg, me, offsets, outs, piece_ref, out_sems)
         small[2].wait()
         small[3].wait()
         for i in range(steps):
@@ -129,15 +135,15 @@
     return kernel
 
 
-def send_pieces(code, unit_ref, meta_ref, seg, me, offsets, outs, piece_ref, sems):
+def send_pieces(found, meta_ref, seg, me, offsets, outs, piece_ref, sems):
     copies = []
-    slabs = unit_ref.shape[1] // 128
+    slabs = (piece_ref.shape[1] - TAIL) // seg
     index = lax.broadcasted_iota(jnp.int32, (TAIL, 128), 0)
     for i, (k, out_ref) in enumerate(zip(offsets, outs)):
-        pick = hot(code, seg, (me ^ k) * seg)
-        found = dot(pick, unit_ref[...], NN).astype(jnp.bfloat16)
+        rows = found[i] if isinstance(found, list) else found(k)
+        rows = rows.astype(jnp.bfloat16)
         for f in range(slabs):
-            piece_ref[i, f * seg : (f + 1) * seg, :] = found[:, f * 128 : (f + 1) * 128]
+            piece_ref[i, f * seg : (f + 1) * seg, :] = rows[:, f * 128 : (f + 1) * 128]
         row = meta_ref[me ^ k]
         tail = jnp.zeros((TAIL, 128), jnp.float32)
         for j in range(row.shape[1] // 128):
@@ -155,7 +161,11 @@
     def kernel(where_ref, meta_ref, unit_ref, *rest):
         outs, (piece_ref, sems) = rest[: len(offsets)], rest[len(offsets) :]
         me = lax.axis_index("clus")
-        send_pieces(where_ref[0:1, :], unit_ref, meta_ref, seg, me, offsets, outs, piece_ref, sems)
+
+        def found(k):
+            return dot(hot(where_ref[0:1, :], seg, (me ^ k) * seg), unit_ref[...], NN)
+
+        send_pieces(found, meta_ref, seg, me, offsets, outs, piece_ref, sems)
 
     return kernel
 
@@ -288,7 +298,9 @@
         mid = rest.astype(jnp.bfloat16)
         low = (rest - mid.astype(jnp.float32)).astype(jnp.bfloat16)
         there = hot(where_ref[2:3, :], gains.shape[1])
-        found = dot(high, there, NN) + dot(mid, there, NN) + dot(low, there, NN)
+        parts = dot(jnp.concatenate([high, mid, low], axis=0), there, NN)
+        count = gains.shape[0]
+        found = parts[:count] + parts[count : 2 * count] + parts[2 * count :]
         index = lax.broadcasted_iota(jnp.int32, found.shape, 0)
         mine = jnp.where(index == where_ref[1:2, :], found, 0.0)
         out_ref[...] = jnp.sum(mine, axis=0, keepdims=True)

time: 128 us -> 128 us (level)
  no operation moved by 1% of the time
where the time goes in v10:
time: 128 us
  waiting for transfers between devices  49.8 us (39%)
  Pallas kernels  35 us (27%)
  starting transfers between devices  25.1 us (20%)
  blocking collectives  14 us (11%)
  local copies, waits for them, and re-layouts  3.41 us (3%)
    ppermute x15, waiting for transfers between devices, body(): lax.ppermute(x, 'clus', [(d, d ^ offsets[1 + i]) for d in range(devices)])  49.8 us
    ppermute x15, starting transfers between devices, body(): lax.ppermute(x, 'clus', [(d, d ^ offsets[1 + i]) for d in range(devices)])  25.1 us
    pallas_call x2, Pallas kernels, body(): call(rest_kernel(devices, cap, ks), [piece] * len(ks), (0, 0), name, in_s...  16 us
    all_to_all x1, blocking collectives, body(): back = lax.all_to_all(gains, 'clus', 0, 0, tiled=True)  14 us
    pallas_call x8, Pallas kernels, body(): call(gram_kernel(devices, cap, offsets, stops, g), [gain_shape] + [S((fre...  12 us
    pallas_call x1, Pallas kernels, body(): call(first_kernel(devices, cap, steps, offsets[1:1 + early]), [S((rows, w...  6.02 us
    unnamed x8, local copies, waits for them, and re-layouts  3.41 us
  transfers between devices with their start and end apart: 15, of which 6 were waited for; matrix products, arithmetic and copies ran while one was open for 0% of the time, Pallas kernels for 21%

profile of v10, /device:TPU:0, one launch (start us, length us, event | category | flops | bytes accessed | tf_op | source)
XLA Modules:
  0.0 127.5 jit_solution(10308114862005270254)
XLA Ops:
  0.0 6.0 %first.1 = (bf16[2048,768]{1,0:T(8,128)(2,1)}, s32[3,2048]{1,0:T(4,128)}, f32[16,1,512]{2,1,0:T(1,128)}, bf16[1168,128]{1,0:T(8,128)(2,1)}) custom-call(s32[1,2048]{1,0:T(1,128)} %bitcast.3, bf16[16,128]{1,0:T(8,128)(2,1)} %bitcast.4, f32[2048,768]{1,0:T(8,128)} %emb_ref.1), custom_call_target="tpu_custom_call" | custom-call | flops 603979776 | bytes 6291456 | tf_op jit(solution)/shard_map/first/pallas_call | solution.py:362
  6.0 4.1 %collective-permute-start = (bf16[1168,128]{1,0:T(8,128)(2,1)}, bf16[1168,128]{1,0:T(8,128)(2,1)S(1)}, u32[]{:S(2)}, u32[]{:S(2)}) collective-permute-start(bf16[1168,128]{1,0:T(8,128)(2,1)} %get-tuple-element.65), channel_id=1, source_target_pairs={{0,8},{1,9},{2,10},{3,11},{4,12},{5,13},{6,14},{7,15},{8,0},{9,1},... | collective-permute-start | bytes 897032 | tf_op jit(solution)/shard_map/ppermute | solution.py:393
  10.1 0.0 copy-start
  10.1 1.9 %copy-done = bf16[2048,768]{1,0:T(8,128)(2,1)S(1)} copy-done((bf16[2048,768]{1,0:T(8,128)(2,1)S(1)}, bf16[2048,768]{1,0:T(8,128)(2,1)}, u32[]{:S(2)}) %copy-start) | copy-done | bytes 3145752
  12.0 0.0 copy-start.1
  12.0 0.8 copy-done.1
  12.8 0.0 copy-start.3
  12.8 0.8 copy-done.3
  13.5 3.1 %second.1 = (bf16[1168,128]{1,0:T(8,128)(2,1)S(1)}, bf16[1168,128]{1,0:T(8,128)(2,1)S(1)}, bf16[1168,128]{1,0:T(8,128)(2,1)S(1)}) custom-call(s32[3,2048]{1,0:T(4,128)S(1)} %copy-done.1, f32[16,1,512]{2,1,0:T(1,128)S(1)} %copy-done.3, bf16[2048,768]{1,0:T(8,128)(2,1)S(1)} %copy-done), custom_call_target="tpu_custom_call" | custom-call | tf_op jit(solution)/shard_map/second/pallas_call | solution.py:378
  16.7 1.6 %collective-permute-start.2 = (bf16[1168,128]{1,0:T(8,128)(2,1)S(1)}, bf16[1168,128]{1,0:T(8,128)(2,1)S(1)}, u32[]{:S(2)}, u32[]{:S(2)}) collective-permute-start(bf16[1168,128]{1,0:T(8,128)(2,1)S(1)} %get-tuple-element.71), channel_id=1, source_target_pairs={{0,4},{1,5},{2,6},{3,7},{4,0},{5,1},{6,2},{7,3},{8,12},{9,13},{10,... | collective-permute-start | bytes 897032 | tf_op jit(solution)/shard_map/ppermute | solution.py:393
  18.3 0.0 collective-permute-start.1
  18.3 0.5 collective-permute-start.3
  18.9 12.9 %rest.1 = (bf16[1168,128]{1,0:T(8,128)(2,1)S(1)}, bf16[1168,128]{1,0:T(8,128)(2,1)S(1)}, bf16[1168,128]{1,0:T(8,128)(2,1)S(1)}, bf16[1168,128]{1,0:T(8,128)(2,1)...) custom-call(s32[3,2048]{1,0:T(4,128)S(1)} %copy-done.1, ...), custom_call_target="tpu_custom_call" | custom-call | tf_op jit(solution)/shard_map/rest/pallas_call | solution.py:378
  31.7 0.0 collective-permute-done.refs_1_
  31.7 3.7 %collective-permute-start.4 = (bf16[1168,128]{1,0:T(8,128)(2,1)S(1)}, bf16[1168,128]{1,0:T(8,128)(2,1)S(1)}, u32[]{:S(2)}, u32[]{:S(2)}) collective-permute-start(bf16[1168,128]{1,0:T(8,128)(2,1)S(1)} %get-tuple-element.77), channel_id=1, source_target_pairs={{0,5},{1,4},{2,7},{3,6},{4,1},{5,0},{6,3},{7,2},{8,13},{9,12},{10,... | collective-permute-start | bytes 897032 | tf_op jit(solution)/shard_map/ppermute | solution.py:393
  35.4 1.3 collective-permute-done.2.refs_3_
  36.7 0.5 collective-permute-start.6
  37.2 0.0 collective-permute-done.1.refs_2_
  37.2 1.1 collective-permute-start.5
  38.3 10.4 %collective-permute-done.3.refs_4_ = bf16[1168,128]{1,0:T(8,128)(2,1)S(1)} collective-permute-done((bf16[1168,128]{1,0:T(8,128)(2,1)S(1)}, bf16[1168,128]{1,0:T(8,128)(2,1)S(1)}, u32[]{:S(2)}, u32[]{:S(2)}) %collective-permute-start.3) | collective-permute-done | bytes 299040 | tf_op jit(solution)/shard_map/ppermute | solution.py:393
  48.8 3.4 %collective-permute-start.7 = (bf16[1168,128]{1,0:T(8,128)(2,1)S(1)}, bf16[1168,128]{1,0:T(8,128)(2,1)S(1)}, u32[]{:S(2)}, u32[]{:S(2)}) collective-permute-start(bf16[1168,128]{1,0:T(8,128)(2,1)S(1)} %get-tuple-element.86), channel_id=1, source_target_pairs={{0,10},{1,11},{2,8},{3,9},{4,14},{5,15},{6,12},{7,13},{8,2},{9,3},... | collective-permute-start | bytes 897032 | tf_op jit(solution)/shard_map/ppermute | solution.py:393
  52.2 0.0 collective-permute-done.4.refs_5_
  52.2 2.2 %collective-permute-start.8 = (bf16[1168,128]{1,0:T(8,128)(2,1)S(1)}, bf16[1168,128]{1,0:T(8,128)(2,1)S(1)}, u32[]{:S(2)}, u32[]{:S(2)}) collective-permute-start(bf16[1168,128]{1,0:T(8,128)(2,1)S(1)} %get-tuple-element.89), channel_id=1, source_target_pairs={{0,7},{1,6},{2,5},{3,4},{4,3},{5,2},{6,1},{7,0},{8,15},{9,14},{10,... | collective-permute-start | bytes 897032 | tf_op jit(solution)/shard_map/ppermute | solution.py:393
  54.4 8.9 %collective-permute-done.6.refs_7_ = bf16[1168,128]{1,0:T(8,128)(2,1)S(1)} collective-permute-done((bf16[1168,128]{1,0:T(8,128)(2,1)S(1)}, bf16[1168,128]{1,0:T(8,128)(2,1)S(1)}, u32[]{:S(2)}, u32[]{:S(2)}) %collective-permute-start.6) | collective-permute-done | bytes 299040 | tf_op jit(solution)/shard_map/ppermute | solution.py:393
  63.3 0.4 collective-permute-start.10
  63.7 0.0 collective-permute-done.5.refs_6_
  63.7 4.7 %collective-permute-start.9 = (bf16[1168,128]{1,0:T(8,128)(2,1)S(1)}, bf16[1168,128]{1,0:T(8,128)(2,1)S(1)}, u32[]{:S(2)}, u32[]{:S(2)}) collective-permute-start(bf16[1168,128]{1,0:T(8,128)(2,1)S(1)} %get-tuple-element.92), channel_id=1, source_target_pairs={{0,14},{1,15},{2,12},{3,13},{4,10},{5,11},{6,8},{7,9},{8,6},{9,7},... | collective-permute-start | bytes 897032 | tf_op jit(solution)/shard_map/ppermute | solution.py:393
  68.4 1.1 gram.8
  69.5 14.3 %collective-permute-done.7.refs_8_ = bf16[1168,128]{1,0:T(8,128)(2,1)S(1)} collective-permute-done((bf16[1168,128]{1,0:T(8,128)(2,1)S(1)}, bf16[1168,128]{1,0:T(8,128)(2,1)S(1)}, u32[]{:S(2)}, u32[]{:S(2)}) %collective-permute-start.7) | collective-permute-done | bytes 299040 | tf_op jit(solution)/shard_map/ppermute | solution.py:393
  83.7 0.0 collective-permute-start.11
  83.7 1.0 gram.9
  84.7 0.0 collective-permute-done.8.refs_9_
  84.7 0.1 collective-permute-start.12
  84.8 1.3 %gram.10 = (f32[16,1,256]{2,1,0:T(1,128)S(1)}, f32[384,256]{1,0:T(8,128)S(1)}) custom-call(bf16[1168,128]{1,0:T(8,128)(2,1)S(1)} %get-tuple-element.63.refs_0_, bf16[1168,128]{1,0:T(8,128)(2,1)S(1)} %collective-permute-done.refs_1_, bf16[1168,128]{1,0:T(8,128)(2,1)S(1)} %collective-permute-done.1.refs_2_, ...), custom_call_target="tpu_custom_call" | custom-call | flops 905969664 | bytes 2359296 | tf_op jit(solution)/shard_map/gram/pallas_call | solution.py:401
  86.1 2.9 %collective-permute-done.10.refs_11_ = bf16[1168,128]{1,0:T(8,128)(2,1)S(1)} collective-permute-done((bf16[1168,128]{1,0:T(8,128)(2,1)S(1)}, bf16[1168,128]{1,0:T(8,128)(2,1)S(1)}, u32[]{:S(2)}, u32[]{:S(2)}) %collective-permute-start.10) | collective-permute-done | bytes 299040 | tf_op jit(solution)/shard_map/ppermute | solution.py:393
  89.0 2.2 %collective-permute-start.14 = (bf16[1168,128]{1,0:T(8,128)(2,1)S(1)}, bf16[1168,128]{1,0:T(8,128)(2,1)S(1)}, u32[]{:S(2)}, u32[]{:S(2)}) collective-permute-start(bf16[1168,128]{1,0:T(8,128)(2,1)S(1)} %get-tuple-element.100), channel_id=1, source_target_pairs={{0,15},{1,14},{2,13},{3,12},{4,11},{5,10},{6,9},{7,8},{8,7},{9,6},... | collective-permute-start | bytes 897032 | tf_op jit(solution)/shard_map/ppermute | solution.py:393
  91.2 0.0 collective-permute-done.9.refs_10_
  91.2 0.6 collective-permute-start.13
  91.8 1.5 %gram.11 = (f32[16,1,256]{2,1,0:T(1,128)S(1)}, f32[384,256]{1,0:T(8,128)S(1)}) custom-call(bf16[1168,128]{1,0:T(8,128)(2,1)S(1)} %get-tuple-element.63.refs_0_, bf16[1168,128]{1,0:T(8,128)(2,1)S(1)} %collective-permute-done.refs_1_, bf16[1168,128]{1,0:T(8,128)(2,1)S(1)} %collective-permute-done.1.refs_2_, ...), custom_call_target="tpu_custom_call" | custom-call | flops 1132462080 | bytes 2949120 | tf_op jit(solution)/shard_map/gram/pallas_call | solution.py:401
  93.3 1.8 %gram.12 = (f32[16,1,256]{2,1,0:T(1,128)S(1)}, f32[384,256]{1,0:T(8,128)S(1)}) custom-call(bf16[1168,128]{1,0:T(8,128)(2,1)S(1)} %get-tuple-element.63.refs_0_, bf16[1168,128]{1,0:T(8,128)(2,1)S(1)} %collective-permute-done.refs_1_, bf16[1168,128]{1,0:T(8,128)(2,1)S(1)} %collective-permute-done.1.refs_2_, ...), custom_call_target="tpu_custom_call" | custom-call | flops 1358954496 | bytes 3538944 | tf_op jit(solution)/shard_map/gram/pallas_call | solution.py:401
  95.1 12.0 %collective-permute-done.11.refs_12_ = bf16[1168,128]{1,0:T(8,128)(2,1)S(1)} collective-permute-done((bf16[1168,128]{1,0:T(8,128)(2,1)S(1)}, bf16[1168,128]{1,0:T(8,128)(2,1)S(1)}, u32[]{:S(2)}, u32[]{:S(2)}) %collective-permute-start.11) | collective-permute-done | bytes 299040 | tf_op jit(solution)/shard_map/ppermute | solution.py:393
  107.1 0.0 collective-permute-done.12.refs_13_
  107.2 2.1 %gram.13 = (f32[16,1,256]{2,1,0:T(1,128)S(1)}, f32[384,256]{1,0:T(8,128)S(1)}) custom-call(bf16[1168,128]{1,0:T(8,128)(2,1)S(1)} %get-tuple-element.63.refs_0_, bf16[1168,128]{1,0:T(8,128)(2,1)S(1)} %collective-permute-done.refs_1_, bf16[1168,128]{1,0:T(8,128)(2,1)S(1)} %collective-permute-done.1.refs_2_, ...), custom_call_target="tpu_custom_call" | custom-call | flops 1585446912 | bytes 4128768 | tf_op jit(solution)/shard_map/gram/pallas_call | solution.py:401
  109.2 0.0 collective-permute-done.13.refs_14_
  109.2 0.0 copy-start.2
  109.2 1.6 %gram.14 = (f32[16,1,256]{2,1,0:T(1,128)S(1)}, f32[192,256]{1,0:T(8,128)S(1)}) custom-call(bf16[1168,128]{1,0:T(8,128)(2,1)S(1)} %get-tuple-element.63.refs_0_, bf16[1168,128]{1,0:T(8,128)(2,1)S(1)} %collective-permute-done.refs_1_, bf16[1168,128]{1,0:T(8,128)(2,1)S(1)} %collective-permute-done.1.refs_2_, ...), custom_call_target="tpu_custom_call" | custom-call | flops 849346560 | bytes 4423680 | tf_op jit(solution)/shard_map/gram/pallas_call | solution.py:401
  110.8 0.0 collective-permute-done.14.refs_15_
  110.8 1.7 %gram.15 = f32[16,1,256]{2,1,0:T(1,128)S(1)} custom-call(bf16[1168,128]{1,0:T(8,128)(2,1)S(1)} %get-tuple-element.63.refs_0_, bf16[1168,128]{1,0:T(8,128)(2,1)S(1)} %collective-permute-done.refs_1_, bf16[1168,128]{1,0:T(8,128)(2,1)S(1)} %collective-permute-done.1.refs_2_, bf16[1168,128]{1,0:T(8,128)(2,1)S(1)} %collective-permute-done.2.refs_3_, ...), custom_call_target="tpu_custom_call" | custom-call | flops 905969664 | bytes 4718592 | tf_op jit(solution)/shard_map/gram/pallas_call | solution.py:401
  112.5 14.0 %all_to_all.5.gains_ref = f32[16,1,256]{2,1,0:T(1,128)S(1)} all-to-all(f32[16,1,256]{2,1,0:T(1,128)S(1)} %gram.15), channel_id=1, replica_groups=mesh['parts'=2,'clus'=16] {'clus'}, dimensions={0} | all-to-all | bytes 32768 | tf_op jit(solution)/shard_map/all_to_all | solution.py:409
  126.5 0.0 copy-done.2
  126.5 1.0 last.1
Async XLA Ops:
  6.0 25.7 %collective-permute-start = (bf16[1168,128]{1,0:T(8,128)(2,1)}, bf16[1168,128]{1,0:T(8,128)(2,1)S(1)}, u32[]{:S(2)}, u32[]{:S(2)}) collective-permute-start(bf16[1168,128]{1,0:T(8,128)(2,1)} %get-tuple-element.65), channel_id=1, source_target_pairs={{0,8},{1,9},{2,10},{3,11},{4,12},{5,13},{6,14},{7,15},{8,0},{9,1},... | collective-permute-start | bytes 897032 | tf_op jit(solution)/shard_map/ppermute | solution.py:393
  10.1 1.9 %copy-start = (bf16[2048,768]{1,0:T(8,128)(2,1)S(1)}, bf16[2048,768]{1,0:T(8,128)(2,1)}, u32[]{:S(2)}) copy-start(bf16[2048,768]{1,0:T(8,128)(2,1)} %get-tuple-element.62.unit_ref) | copy-start | bytes 9437188
  12.0 0.8 copy-start.1
  12.8 0.8 copy-start.3
  16.7 20.0 %collective-permute-start.2 = (bf16[1168,128]{1,0:T(8,128)(2,1)S(1)}, bf16[1168,128]{1,0:T(8,128)(2,1)S(1)}, u32[]{:S(2)}, u32[]{:S(2)}) collective-permute-start(bf16[1168,128]{1,0:T(8,128)(2,1)S(1)} %get-tuple-element.71), channel_id=1, source_target_pairs={{0,4},{1,5},{2,6},{3,7},{4,0},{5,1},{6,2},{7,3},{8,12},{9,13},{10,... | collective-permute-start | bytes 897032 | tf_op jit(solution)/shard_map/ppermute | solution.py:393
  18.3 18.9 %collective-permute-start.1 = (bf16[1168,128]{1,0:T(8,128)(2,1)S(1)}, bf16[1168,128]{1,0:T(8,128)(2,1)S(1)}, u32[]{:S(2)}, u32[]{:S(2)}) collective-permute-start(bf16[1168,128]{1,0:T(8,128)(2,1)S(1)} %get-tuple-element.68), channel_id=1, source_target_pairs={{0,12},{1,13},{2,14},{3,15},{4,8},{5,9},{6,10},{7,11},{8,4},{9,5},... | collective-permute-start | bytes 897032 | tf_op jit(solution)/shard_map/ppermute | solution.py:393
  18.3 30.4 %collective-permute-start.3 = (bf16[1168,128]{1,0:T(8,128)(2,1)S(1)}, bf16[1168,128]{1,0:T(8,128)(2,1)S(1)}, u32[]{:S(2)}, u32[]{:S(2)}) collective-permute-start(bf16[1168,128]{1,0:T(8,128)(2,1)S(1)} %get-tuple-element.74), channel_id=1, source_target_pairs={{0,9},{1,8},{2,11},{3,10},{4,13},{5,12},{6,15},{7,14},{8,1},{9,0},... | collective-permute-start | bytes 897032 | tf_op jit(solution)/shard_map/ppermute | solution.py:393
  31.7 20.5 %collective-permute-start.4 = (bf16[1168,128]{1,0:T(8,128)(2,1)S(1)}, bf16[1168,128]{1,0:T(8,128)(2,1)S(1)}, u32[]{:S(2)}, u32[]{:S(2)}) collective-permute-start(bf16[1168,128]{1,0:T(8,128)(2,1)S(1)} %get-tuple-element.77), channel_id=1, source_target_pairs={{0,5},{1,4},{2,7},{3,6},{4,1},{5,0},{6,3},{7,2},{8,13},{9,12},{10,... | collective-permute-start | bytes 897032 | tf_op jit(solution)/shard_map/ppermute | solution.py:393
  36.7 26.6 %collective-permute-start.6 = (bf16[1168,128]{1,0:T(8,128)(2,1)S(1)}, bf16[1168,128]{1,0:T(8,128)(2,1)S(1)}, u32[]{:S(2)}, u32[]{:S(2)}) collective-permute-start(bf16[1168,128]{1,0:T(8,128)(2,1)S(1)} %get-tuple-element.83), channel_id=1, source_target_pairs={{0,6},{1,7},{2,4},{3,5},{4,2},{5,3},{6,0},{7,1},{8,14},{9,15},{10,... | collective-permute-start | bytes 897032 | tf_op jit(solution)/shard_map/ppermute | solution.py:393
  37.2 26.5 %collective-permute-start.5 = (bf16[1168,128]{1,0:T(8,128)(2,1)S(1)}, bf16[1168,128]{1,0:T(8,128)(2,1)S(1)}, u32[]{:S(2)}, u32[]{:S(2)}) collective-permute-start(bf16[1168,128]{1,0:T(8,128)(2,1)S(1)} %get-tuple-element.80), channel_id=1, source_target_pairs={{0,13},{1,12},{2,15},{3,14},{4,9},{5,8},{6,11},{7,10},{8,5},{9,4},... | collective-permute-start | bytes 897032 | tf_op jit(solution)/shard_map/ppermute | solution.py:393
  48.8 34.9 %collective-permute-start.7 = (bf16[1168,128]{1,0:T(8,128)(2,1)S(1)}, bf16[1168,128]{1,0:T(8,128)(2,1)S(1)}, u32[]{:S(2)}, u32[]{:S(2)}) collective-permute-start(bf16[1168,128]{1,0:T(8,128)(2,1)S(1)} %get-tuple-element.86), channel_id=1, source_target_pairs={{0,10},{1,11},{2,8},{3,9},{4,14},{5,15},{6,12},{7,13},{8,2},{9,3},... | collective-permute-start | bytes 897032 | tf_op jit(solution)/shard_map/ppermute | solution.py:393
  52.2 32.5 %collective-permute-start.8 = (bf16[1168,128]{1,0:T(8,128)(2,1)S(1)}, bf16[1168,128]{1,0:T(8,128)(2,1)S(1)}, u32[]{:S(2)}, u32[]{:S(2)}) collective-permute-start(bf16[1168,128]{1,0:T(8,128)(2,1)S(1)} %get-tuple-element.89), channel_id=1, source_target_pairs={{0,7},{1,6},{2,5},{3,4},{4,3},{5,2},{6,1},{7,0},{8,15},{9,14},{10,... | collective-permute-start | bytes 897032 | tf_op jit(solution)/shard_map/ppermute | solution.py:393
  63.3 25.7 %collective-permute-start.10 = (bf16[1168,128]{1,0:T(8,128)(2,1)S(1)}, bf16[1168,128]{1,0:T(8,128)(2,1)S(1)}, u32[]{:S(2)}, u32[]{:S(2)}) collective-permute-start(bf16[1168,128]{1,0:T(8,128)(2,1)S(1)} %get-tuple-element.95), channel_id=1, source_target_pairs={{0,2},{1,3},{2,0},{3,1},{4,6},{5,7},{6,4},{7,5},{8,10},{9,11},{10,... | collective-permute-start | bytes 897032 | tf_op jit(solution)/shard_map/ppermute | solution.py:393
  63.7 27.5 %collective-permute-start.9 = (bf16[1168,128]{1,0:T(8,128)(2,1)S(1)}, bf16[1168,128]{1,0:T(8,128)(2,1)S(1)}, u32[]{:S(2)}, u32[]{:S(2)}) collective-permute-start(bf16[1168,128]{1,0:T(8,128)(2,1)S(1)} %get-tuple-element.92), channel_id=1, source_target_pairs={{0,14},{1,15},{2,12},{3,13},{4,10},{5,11},{6,8},{7,9},{8,6},{9,7},... | collective-permute-start | bytes 897032 | tf_op jit(solution)/shard_map/ppermute | solution.py:393
  83.7 23.4 %collective-permute-start.11 = (bf16[1168,128]{1,0:T(8,128)(2,1)S(1)}, bf16[1168,128]{1,0:T(8,128)(2,1)S(1)}, u32[]{:S(2)}, u32[]{:S(2)}) collective-permute-start(bf16[1168,128]{1,0:T(8,128)(2,1)S(1)} %get-tuple-element.97), channel_id=1, source_target_pairs={{0,11},{1,10},{2,9},{3,8},{4,15},{5,14},{6,13},{7,12},{8,3},{9,2},... | collective-permute-start | bytes 897032 | tf_op jit(solution)/shard_map/ppermute | solution.py:393
  84.7 22.4 %collective-permute-start.12 = (bf16[1168,128]{1,0:T(8,128)(2,1)S(1)}, bf16[1168,128]{1,0:T(8,128)(2,1)S(1)}, u32[]{:S(2)}, u32[]{:S(2)}) collective-permute-start(bf16[1168,128]{1,0:T(8,128)(2,1)S(1)} %get-tuple-element.98), channel_id=1, source_target_pairs={{0,3},{1,2},{2,1},{3,0},{4,7},{5,6},{6,5},{7,4},{8,11},{9,10},{10,... | collective-permute-start | bytes 897032 | tf_op jit(solution)/shard_map/ppermute | solution.py:393
  89.0 21.8 %collective-permute-start.14 = (bf16[1168,128]{1,0:T(8,128)(2,1)S(1)}, bf16[1168,128]{1,0:T(8,128)(2,1)S(1)}, u32[]{:S(2)}, u32[]{:S(2)}) collective-permute-start(bf16[1168,128]{1,0:T(8,128)(2,1)S(1)} %get-tuple-element.100), channel_id=1, source_target_pairs={{0,15},{1,14},{2,13},{3,12},{4,11},{5,10},{6,9},{7,8},{8,7},{9,6},... | collective-permute-start | bytes 897032 | tf_op jit(solution)/shard_map/ppermute | solution.py:393
  91.2 18.1 %collective-permute-start.13 = (bf16[1168,128]{1,0:T(8,128)(2,1)S(1)}, bf16[1168,128]{1,0:T(8,128)(2,1)S(1)}, u32[]{:S(2)}, u32[]{:S(2)}) collective-permute-start(bf16[1168,128]{1,0:T(8,128)(2,1)S(1)} %get-tuple-element.99), channel_id=1, source_target_pairs={{0,1},{1,0},{2,3},{3,2},{4,5},{5,4},{6,7},{7,6},{8,9},{9,8},{10,11... | collective-permute-start | bytes 897032 | tf_op jit(solution)/shard_map/ppermute | solution.py:393
  109.2 17.3 %copy-start.2 = (s32[3,2048]{1,0:T(4,128)S(1)}, s32[3,2048]{1,0:T(4,128)}, u32[]{:S(2)}) copy-start(s32[3,2048]{1,0:T(4,128)} %get-tuple-element.60.where_ref) | copy-start | bytes 73732

commit v11 on v10

--- a/solution.py
+++ b/solution.py
@@ -112,8 +112,6 @@
         meta_ref[:, 0, wide:] = both[devices:]
         small[2].start()
         small[3].start()
-        picks = [hot(code, seg, (me ^ k) * seg) for k in offsets]
-        found = [jnp.zeros((seg, rows_ref.shape[1]), jnp.float32) for _ in offsets]
         for i in range(steps):
             load(i).wait()
             if i == steps - 1:
@@ -123,9 +121,11 @@
             sums = jnp.sum(raw * raw, axis=-1, keepdims=True)
             unit = (raw * lax.rsqrt(sums + 1e-06)).astype(jnp.bfloat16)
             rows_ref[i * block : (i + 1) * block, :] = unit
-            for j, pick in enumerate(picks):
-                found[j] = found[j] + dot(pick[:, i * block : (i + 1) * block], unit, NN)
         store(steps - 1).start()
+
+        def found(k):
+            return dot(hot(code, seg, (me ^ k) * seg), rows_ref[...], NN)
+
         send_pieces(found, meta_ref, seg, me, offsets, outs, piece_ref, out_sems)
         small[2].wait()
         small[3].wait()
@@ -140,8 +140,7 @@
     slabs = (piece_ref.shape[1] - TAIL) // seg
     index = lax.broadcasted_iota(jnp.int32, (TAIL, 128), 0)
     for i, (k, out_ref) in enumerate(zip(offsets, outs)):
-        rows = found[i] if isinstance(found, list) else found(k)
-        rows = rows.astype(jnp.bfloat16)
+        rows = found(k).astype(jnp.bfloat16)
         for f in range(slabs):
             piece_ref[i, f * seg : (f + 1) * seg, :] = rows[:, f * 128 : (f + 1) * 128]
         row = meta_ref[me ^ k]

time: 128 us -> 127 us (level)
  no operation moved by 1% of the time
where the time goes in v11:
time: 127 us
  waiting for transfers between devices  49.8 us (39%)
  Pallas kernels  34.2 us (27%)
  starting transfers between devices  25.2 us (20%)
  blocking collectives  14.1 us (11%)
  local copies, waits for them, and re-layouts  3.41 us (3%)
    ppermute x15, waiting for transfers between devices, body(): lax.ppermute(x, 'clus', [(d, d ^ offsets[1 + i]) for d in range(devices)])  49.8 us
    ppermute x15, starting transfers between devices, body(): lax.ppermute(x, 'clus', [(d, d ^ offsets[1 + i]) for d in range(devices)])  25.2 us
    pallas_call x2, Pallas kernels, body(): call(rest_kernel(devices, cap, ks), [piece] * len(ks), (0, 0), name, in_s...  16 us
    all_to_all x1, blocking collectives, body(): back = lax.all_to_all(gains, 'clus', 0, 0, tiled=True)  14.1 us
    pallas_call x8, Pallas kernels, body(): call(gram_kernel(devices, cap, offsets, stops, g), [gain_shape] + [S((fre...  12 us
    pallas_call x1, Pallas kernels, body(): call(first_kernel(devices, cap, steps, offsets[1:1 + early]), [S((rows, w...  5.25 us
    unnamed x8, local copies, waits for them, and re-layouts  3.41 us
  transfers between devices with their start and end apart: 15, of which 6 were waited for; matrix products, arithmetic and copies ran while one was open for 0% of the time, Pallas kernels for 21%

profile of v11, /device:TPU:0, one launch (start us, length us, event | category | flops | bytes accessed | tf_op | source)
XLA Modules:
  0.0 126.7 jit_solution(3754338047340506315)
XLA Ops:
  0.0 5.2 %first.1 = (bf16[2048,768]{1,0:T(8,128)(2,1)}, s32[3,2048]{1,0:T(4,128)}, f32[16,1,512]{2,1,0:T(1,128)}, bf16[1168,128]{1,0:T(8,128)(2,1)}) custom-call(s32[1,2048]{1,0:T(1,128)} %bitcast.3, bf16[16,128]{1,0:T(8,128)(2,1)} %bitcast.4, f32[2048,768]{1,0:T(8,128)} %emb_ref.1), custom_call_target="tpu_custom_call" | custom-call | flops 603979776 | bytes 6291456 | tf_op jit(solution)/shard_map/first/pallas_call | solution.py:361
  5.3 4.1 %collective-permute-start = (bf16[1168,128]{1,0:T(8,128)(2,1)}, bf16[1168,128]{1,0:T(8,128)(2,1)S(1)}, u32[]{:S(2)}, u32[]{:S(2)}) collective-permute-start(bf16[1168,128]{1,0:T(8,128)(2,1)} %get-tuple-element.65), channel_id=1, source_target_pairs={{0,8},{1,9},{2,10},{3,11},{4,12},{5,13},{6,14},{7,15},{8,0},{9,1},... | collective-permute-start | bytes 897032 | tf_op jit(solution)/shard_map/ppermute | solution.py:392
  9.4 0.0 copy-start
  9.4 1.9 %copy-done = bf16[2048,768]{1,0:T(8,128)(2,1)S(1)} copy-done((bf16[2048,768]{1,0:T(8,128)(2,1)S(1)}, bf16[2048,768]{1,0:T(8,128)(2,1)}, u32[]{:S(2)}) %copy-start) | copy-done | bytes 3145752
  11.3 0.0 copy-start.1
  11.3 0.8 copy-done.1
  12.0 0.0 copy-start.3
  12.0 0.8 copy-done.3
  12.8 3.2 %second.1 = (bf16[1168,128]{1,0:T(8,128)(2,1)S(1)}, bf16[1168,128]{1,0:T(8,128)(2,1)S(1)}, bf16[1168,128]{1,0:T(8,128)(2,1)S(1)}) custom-call(s32[3,2048]{1,0:T(4,128)S(1)} %copy-done.1, f32[16,1,512]{2,1,0:T(1,128)S(1)} %copy-done.3, bf16[2048,768]{1,0:T(8,128)(2,1)S(1)} %copy-done), custom_call_target="tpu_custom_call" | custom-call | tf_op jit(solution)/shard_map/second/pallas_call | solution.py:377
  15.9 1.6 %collective-permute-start.2 = (bf16[1168,128]{1,0:T(8,128)(2,1)S(1)}, bf16[1168,128]{1,0:T(8,128)(2,1)S(1)}, u32[]{:S(2)}, u32[]{:S(2)}) collective-permute-start(bf16[1168,128]{1,0:T(8,128)(2,1)S(1)} %get-tuple-element.71), channel_id=1, source_target_pairs={{0,4},{1,5},{2,6},{3,7},{4,0},{5,1},{6,2},{7,3},{8,12},{9,13},{10,... | collective-permute-start | bytes 897032 | tf_op jit(solution)/shard_map/ppermute | solution.py:392
  17.6 0.0 collective-permute-start.1
  17.6 0.5 collective-permute-start.3
  18.1 12.9 %rest.1 = (bf16[1168,128]{1,0:T(8,128)(2,1)S(1)}, bf16[1168,128]{1,0:T(8,128)(2,1)S(1)}, bf16[1168,128]{1,0:T(8,128)(2,1)S(1)}, bf16[1168,128]{1,0:T(8,128)(2,1)...) custom-call(s32[3,2048]{1,0:T(4,128)S(1)} %copy-done.1, ...), custom_call_target="tpu_custom_call" | custom-call | tf_op jit(solution)/shard_map/rest/pallas_call | solution.py:377
  30.9 0.0 collective-permute-done.refs_1_
  31.0 3.7 %collective-permute-start.4 = (bf16[1168,128]{1,0:T(8,128)(2,1)S(1)}, bf16[1168,128]{1,0:T(8,128)(2,1)S(1)}, u32[]{:S(2)}, u32[]{:S(2)}) collective-permute-start(bf16[1168,128]{1,0:T(8,128)(2,1)S(1)} %get-tuple-element.77), channel_id=1, source_target_pairs={{0,5},{1,4},{2,7},{3,6},{4,1},{5,0},{6,3},{7,2},{8,13},{9,12},{10,... | collective-permute-start | bytes 897032 | tf_op jit(solution)/shard_map/ppermute | solution.py:392
  34.6 1.3 %collective-permute-done.2.refs_3_ = bf16[1168,128]{1,0:T(8,128)(2,1)S(1)} collective-permute-done((bf16[1168,128]{1,0:T(8,128)(2,1)S(1)}, bf16[1168,128]{1,0:T(8,128)(2,1)S(1)}, u32[]{:S(2)}, u32[]{:S(2)}) %collective-permute-start.2) | collective-permute-done | bytes 299040 | tf_op jit(solution)/shard_map/ppermute | solution.py:392
  35.9 0.5 collective-permute-start.6
  36.4 0.0 collective-permute-done.1.refs_2_
  36.4 1.1 collective-permute-start.5
  37.6 10.4 %collective-permute-done.3.refs_4_ = bf16[1168,128]{1,0:T(8,128)(2,1)S(1)} collective-permute-done((bf16[1168,128]{1,0:T(8,128)(2,1)S(1)}, bf16[1168,128]{1,0:T(8,128)(2,1)S(1)}, u32[]{:S(2)}, u32[]{:S(2)}) %collective-permute-start.3) | collective-permute-done | bytes 299040 | tf_op jit(solution)/shard_map/ppermute | solution.py:392
  48.0 3.4 %collective-permute-start.7 = (bf16[1168,128]{1,0:T(8,128)(2,1)S(1)}, bf16[1168,128]{1,0:T(8,128)(2,1)S(1)}, u32[]{:S(2)}, u32[]{:S(2)}) collective-permute-start(bf16[1168,128]{1,0:T(8,128)(2,1)S(1)} %get-tuple-element.86), channel_id=1, source_target_pairs={{0,10},{1,11},{2,8},{3,9},{4,14},{5,15},{6,12},{7,13},{8,2},{9,3},... | collective-permute-start | bytes 897032 | tf_op jit(solution)/shard_map/ppermute | solution.py:392
  51.4 0.0 collective-permute-done.4.refs_5_
  51.4 2.2 %collective-permute-start.8 = (bf16[1168,128]{1,0:T(8,128)(2,1)S(1)}, bf16[1168,128]{1,0:T(8,128)(2,1)S(1)}, u32[]{:S(2)}, u32[]{:S(2)}) collective-permute-start(bf16[1168,128]{1,0:T(8,128)(2,1)S(1)} %get-tuple-element.89), channel_id=1, source_target_pairs={{0,7},{1,6},{2,5},{3,4},{4,3},{5,2},{6,1},{7,0},{8,15},{9,14},{10,... | collective-permute-start | bytes 897032 | tf_op jit(solution)/shard_map/ppermute | solution.py:392
  53.6 8.9 %collective-permute-done.6.refs_7_ = bf16[1168,128]{1,0:T(8,128)(2,1)S(1)} collective-permute-done((bf16[1168,128]{1,0:T(8,128)(2,1)S(1)}, bf16[1168,128]{1,0:T(8,128)(2,1)S(1)}, u32[]{:S(2)}, u32[]{:S(2)}) %collective-permute-start.6) | collective-permute-done | bytes 299040 | tf_op jit(solution)/shard_map/ppermute | solution.py:392
  62.5 0.4 collective-permute-start.10
  62.9 0.0 collective-permute-done.5.refs_6_
  62.9 4.7 %collective-permute-start.9 = (bf16[1168,128]{1,0:T(8,128)(2,1)S(1)}, bf16[1168,128]{1,0:T(8,128)(2,1)S(1)}, u32[]{:S(2)}, u32[]{:S(2)}) collective-permute-start(bf16[1168,128]{1,0:T(8,128)(2,1)S(1)} %get-tuple-element.92), channel_id=1, source_target_pairs={{0,14},{1,15},{2,12},{3,13},{4,10},{5,11},{6,8},{7,9},{8,6},{9,7},... | collective-permute-start | bytes 897032 | tf_op jit(solution)/shard_map/ppermute | solution.py:392
  67.6 1.1 gram.8
  68.7 14.3 %collective-permute-done.7.refs_8_ = bf16[1168,128]{1,0:T(8,128)(2,1)S(1)} collective-permute-done((bf16[1168,128]{1,0:T(8,128)(2,1)S(1)}, bf16[1168,128]{1,0:T(8,128)(2,1)S(1)}, u32[]{:S(2)}, u32[]{:S(2)}) %collective-permute-start.7) | collective-permute-done | bytes 299040 | tf_op jit(solution)/shard_map/ppermute | solution.py:392
  83.0 0.0 collective-permute-start.11
  83.0 1.0 gram.9
  84.0 0.0 collective-permute-done.8.refs_9_
  84.0 0.1 collective-permute-start.12
  84.0 1.3 %gram.10 = (f32[16,1,256]{2,1,0:T(1,128)S(1)}, f32[384,256]{1,0:T(8,128)S(1)}) custom-call(bf16[1168,128]{1,0:T(8,128)(2,1)S(1)} %get-tuple-element.63.refs_0_, bf16[1168,128]{1,0:T(8,128)(2,1)S(1)} %collective-permute-done.refs_1_, bf16[1168,128]{1,0:T(8,128)(2,1)S(1)} %collective-permute-done.1.refs_2_, ...), custom_call_target="tpu_custom_call" | custom-call | flops 905969664 | bytes 2359296 | tf_op jit(solution)/shard_map/gram/pallas_call | solution.py:400
  85.3 2.9 %collective-permute-done.10.refs_11_ = bf16[1168,128]{1,0:T(8,128)(2,1)S(1)} collective-permute-done((bf16[1168,128]{1,0:T(8,128)(2,1)S(1)}, bf16[1168,128]{1,0:T(8,128)(2,1)S(1)}, u32[]{:S(2)}, u32[]{:S(2)}) %collective-permute-start.10) | collective-permute-done | bytes 299040 | tf_op jit(solution)/shard_map/ppermute | solution.py:392
  88.2 2.2 %collective-permute-start.14 = (bf16[1168,128]{1,0:T(8,128)(2,1)S(1)}, bf16[1168,128]{1,0:T(8,128)(2,1)S(1)}, u32[]{:S(2)}, u32[]{:S(2)}) collective-permute-start(bf16[1168,128]{1,0:T(8,128)(2,1)S(1)} %get-tuple-element.100), channel_id=1, source_target_pairs={{0,15},{1,14},{2,13},{3,12},{4,11},{5,10},{6,9},{7,8},{8,7},{9,6},... | collective-permute-start | bytes 897032 | tf_op jit(solution)/shard_map/ppermute | solution.py:392
  90.4 0.0 collective-permute-done.9.refs_10_
  90.4 0.6 collective-permute-start.13
  91.0 1.5 %gram.11 = (f32[16,1,256]{2,1,0:T(1,128)S(1)}, f32[384,256]{1,0:T(8,128)S(1)}) custom-call(bf16[1168,128]{1,0:T(8,128)(2,1)S(1)} %get-tuple-element.63.refs_0_, bf16[1168,128]{1,0:T(8,128)(2,1)S(1)} %collective-permute-done.refs_1_, bf16[1168,128]{1,0:T(8,128)(2,1)S(1)} %collective-permute-done.1.refs_2_, ...), custom_call_target="tpu_custom_call" | custom-call | flops 1132462080 | bytes 2949120 | tf_op jit(solution)/shard_map/gram/pallas_call | solution.py:400
  92.5 1.8 %gram.12 = (f32[16,1,256]{2,1,0:T(1,128)S(1)}, f32[384,256]{1,0:T(8,128)S(1)}) custom-call(bf16[1168,128]{1,0:T(8,128)(2,1)S(1)} %get-tuple-element.63.refs_0_, bf16[1168,128]{1,0:T(8,128)(2,1)S(1)} %collective-permute-done.refs_1_, bf16[1168,128]{1,0:T(8,128)(2,1)S(1)} %collective-permute-done.1.refs_2_, ...), custom_call_target="tpu_custom_call" | custom-call | flops 1358954496 | bytes 3538944 | tf_op jit(solution)/shard_map/gram/pallas_call | solution.py:400
  94.4 12.0 %collective-permute-done.11.refs_12_ = bf16[1168,128]{1,0:T(8,128)(2,1)S(1)} collective-permute-done((bf16[1168,128]{1,0:T(8,128)(2,1)S(1)}, bf16[1168,128]{1,0:T(8,128)(2,1)S(1)}, u32[]{:S(2)}, u32[]{:S(2)}) %collective-permute-start.11) | collective-permute-done | bytes 299040 | tf_op jit(solution)/shard_map/ppermute | solution.py:392
  106.4 0.0 collective-permute-done.12.refs_13_
  106.4 2.1 %gram.13 = (f32[16,1,256]{2,1,0:T(1,128)S(1)}, f32[384,256]{1,0:T(8,128)S(1)}) custom-call(bf16[1168,128]{1,0:T(8,128)(2,1)S(1)} %get-tuple-element.63.refs_0_, bf16[1168,128]{1,0:T(8,128)(2,1)S(1)} %collective-permute-done.refs_1_, bf16[1168,128]{1,0:T(8,128)(2,1)S(1)} %collective-permute-done.1.refs_2_, ...), custom_call_target="tpu_custom_call" | custom-call | flops 1585446912 | bytes 4128768 | tf_op jit(solution)/shard_map/gram/pallas_call | solution.py:400
  108.5 0.0 collective-permute-done.13.refs_14_
  108.5 0.0 copy-start.2
  108.5 1.5 %gram.14 = (f32[16,1,256]{2,1,0:T(1,128)S(1)}, f32[192,256]{1,0:T(8,128)S(1)}) custom-call(bf16[1168,128]{1,0:T(8,128)(2,1)S(1)} %get-tuple-element.63.refs_0_, bf16[1168,128]{1,0:T(8,128)(2,1)S(1)} %collective-permute-done.refs_1_, bf16[1168,128]{1,0:T(8,128)(2,1)S(1)} %collective-permute-done.1.refs_2_, ...), custom_call_target="tpu_custom_call" | custom-call | flops 849346560 | bytes 4423680 | tf_op jit(solution)/shard_map/gram/pallas_call | solution.py:400
  110.0 0.0 collective-permute-done.14.refs_15_
  110.0 1.7 %gram.15 = f32[16,1,256]{2,1,0:T(1,128)S(1)} custom-call(bf16[1168,128]{1,0:T(8,128)(2,1)S(1)} %get-tuple-element.63.refs_0_, bf16[1168,128]{1,0:T(8,128)(2,1)S(1)} %collective-permute-done.refs_1_, bf16[1168,128]{1,0:T(8,128)(2,1)S(1)} %collective-permute-done.1.refs_2_, bf16[1168,128]{1,0:T(8,128)(2,1)S(1)} %collective-permute-done.2.refs_3_, ...), custom_call_target="tpu_custom_call" | custom-call | flops 905969664 | bytes 4718592 | tf_op jit(solution)/shard_map/gram/pallas_call | solution.py:400
  111.7 14.1 %all_to_all.5.gains_ref = f32[16,1,256]{2,1,0:T(1,128)S(1)} all-to-all(f32[16,1,256]{2,1,0:T(1,128)S(1)} %gram.15), channel_id=1, replica_groups=mesh['parts'=2,'clus'=16] {'clus'}, dimensions={0} | all-to-all | bytes 32768 | tf_op jit(solution)/shard_map/all_to_all | solution.py:408
  125.8 0.0 copy-done.2
  125.8 1.0 last.1
Async XLA Ops:
  5.3 25.7 %collective-permute-start = (bf16[1168,128]{1,0:T(8,128)(2,1)}, bf16[1168,128]{1,0:T(8,128)(2,1)S(1)}, u32[]{:S(2)}, u32[]{:S(2)}) collective-permute-start(bf16[1168,128]{1,0:T(8,128)(2,1)} %get-tuple-element.65), channel_id=1, source_target_pairs={{0,8},{1,9},{2,10},{3,11},{4,12},{5,13},{6,14},{7,15},{8,0},{9,1},... | collective-permute-start | bytes 897032 | tf_op jit(solution)/shard_map/ppermute | solution.py:392
  9.4 1.9 %copy-start = (bf16[2048,768]{1,0:T(8,128)(2,1)S(1)}, bf16[2048,768]{1,0:T(8,128)(2,1)}, u32[]{:S(2)}) copy-start(bf16[2048,768]{1,0:T(8,128)(2,1)} %get-tuple-element.62.unit_ref) | copy-start | bytes 9437188
  11.3 0.8 copy-start.1
  12.0 0.8 copy-start.3
  15.9 20.0 %collective-permute-start.2 = (bf16[1168,128]{1,0:T(8,128)(2,1)S(1)}, bf16[1168,128]{1,0:T(8,128)(2,1)S(1)}, u32[]{:S(2)}, u32[]{:S(2)}) collective-permute-start(bf16[1168,128]{1,0:T(8,128)(2,1)S(1)} %get-tuple-element.71), channel_id=1, source_target_pairs={{0,4},{1,5},{2,6},{3,7},{4,0},{5,1},{6,2},{7,3},{8,12},{9,13},{10,... | collective-permute-start | bytes 897032 | tf_op jit(solution)/shard_map/ppermute | solution.py:392
  17.6 18.9 %collective-permute-start.1 = (bf16[1168,128]{1,0:T(8,128)(2,1)S(1)}, bf16[1168,128]{1,0:T(8,128)(2,1)S(1)}, u32[]{:S(2)}, u32[]{:S(2)}) collective-permute-start(bf16[1168,128]{1,0:T(8,128)(2,1)S(1)} %get-tuple-element.68), channel_id=1, source_target_pairs={{0,12},{1,13},{2,14},{3,15},{4,8},{5,9},{6,10},{7,11},{8,4},{9,5},... | collective-permute-start | bytes 897032 | tf_op jit(solution)/shard_map/ppermute | solution.py:392
  17.6 30.4 %collective-permute-start.3 = (bf16[1168,128]{1,0:T(8,128)(2,1)S(1)}, bf16[1168,128]{1,0:T(8,128)(2,1)S(1)}, u32[]{:S(2)}, u32[]{:S(2)}) collective-permute-start(bf16[1168,128]{1,0:T(8,128)(2,1)S(1)} %get-tuple-element.74), channel_id=1, source_target_pairs={{0,9},{1,8},{2,11},{3,10},{4,13},{5,12},{6,15},{7,14},{8,1},{9,0},... | collective-permute-start | bytes 897032 | tf_op jit(solution)/shard_map/ppermute | solution.py:392
  31.0 20.5 %collective-permute-start.4 = (bf16[1168,128]{1,0:T(8,128)(2,1)S(1)}, bf16[1168,128]{1,0:T(8,128)(2,1)S(1)}, u32[]{:S(2)}, u32[]{:S(2)}) collective-permute-start(bf16[1168,128]{1,0:T(8,128)(2,1)S(1)} %get-tuple-element.77), channel_id=1, source_target_pairs={{0,5},{1,4},{2,7},{3,6},{4,1},{5,0},{6,3},{7,2},{8,13},{9,12},{10,... | collective-permute-start | bytes 897032 | tf_op jit(solution)/shard_map/ppermute | solution.py:392
  35.9 26.6 %collective-permute-start.6 = (bf16[1168,128]{1,0:T(8,128)(2,1)S(1)}, bf16[1168,128]{1,0:T(8,128)(2,1)S(1)}, u32[]{:S(2)}, u32[]{:S(2)}) collective-permute-start(bf16[1168,128]{1,0:T(8,128)(2,1)S(1)} %get-tuple-element.83), channel_id=1, source_target_pairs={{0,6},{1,7},{2,4},{3,5},{4,2},{5,3},{6,0},{7,1},{8,14},{9,15},{10,... | collective-permute-start | bytes 897032 | tf_op jit(solution)/shard_map/ppermute | solution.py:392
  36.4 26.5 %collective-permute-start.5 = (bf16[1168,128]{1,0:T(8,128)(2,1)S(1)}, bf16[1168,128]{1,0:T(8,128)(2,1)S(1)}, u32[]{:S(2)}, u32[]{:S(2)}) collective-permute-start(bf16[1168,128]{1,0:T(8,128)(2,1)S(1)} %get-tuple-element.80), channel_id=1, source_target_pairs={{0,13},{1,12},{2,15},{3,14},{4,9},{5,8},{6,11},{7,10},{8,5},{9,4},... | collective-permute-start | bytes 897032 | tf_op jit(solution)/shard_map/ppermute | solution.py:392
  48.0 34.9 %collective-permute-start.7 = (bf16[1168,128]{1,0:T(8,128)(2,1)S(1)}, bf16[1168,128]{1,0:T(8,128)(2,1)S(1)}, u32[]{:S(2)}, u32[]{:S(2)}) collective-permute-start(bf16[1168,128]{1,0:T(8,128)(2,1)S(1)} %get-tuple-element.86), channel_id=1, source_target_pairs={{0,10},{1,11},{2,8},{3,9},{4,14},{5,15},{6,12},{7,13},{8,2},{9,3},... | collective-permute-start | bytes 897032 | tf_op jit(solution)/shard_map/ppermute | solution.py:392
  51.4 32.6 %collective-permute-start.8 = (bf16[1168,128]{1,0:T(8,128)(2,1)S(1)}, bf16[1168,128]{1,0:T(8,128)(2,1)S(1)}, u32[]{:S(2)}, u32[]{:S(2)}) collective-permute-start(bf16[1168,128]{1,0:T(8,128)(2,1)S(1)} %get-tuple-element.89), channel_id=1, source_target_pairs={{0,7},{1,6},{2,5},{3,4},{4,3},{5,2},{6,1},{7,0},{8,15},{9,14},{10,... | collective-permute-start | bytes 897032 | tf_op jit(solution)/shard_map/ppermute | solution.py:392
  62.5 25.7 %collective-permute-start.10 = (bf16[1168,128]{1,0:T(8,128)(2,1)S(1)}, bf16[1168,128]{1,0:T(8,128)(2,1)S(1)}, u32[]{:S(2)}, u32[]{:S(2)}) collective-permute-start(bf16[1168,128]{1,0:T(8,128)(2,1)S(1)} %get-tuple-element.95), channel_id=1, source_target_pairs={{0,2},{1,3},{2,0},{3,1},{4,6},{5,7},{6,4},{7,5},{8,10},{9,11},{10,... | collective-permute-start | bytes 897032 | tf_op jit(solution)/shard_map/ppermute | solution.py:392
  62.9 27.5 %collective-permute-start.9 = (bf16[1168,128]{1,0:T(8,128)(2,1)S(1)}, bf16[1168,128]{1,0:T(8,128)(2,1)S(1)}, u32[]{:S(2)}, u32[]{:S(2)}) collective-permute-start(bf16[1168,128]{1,0:T(8,128)(2,1)S(1)} %get-tuple-element.92), channel_id=1, source_target_pairs={{0,14},{1,15},{2,12},{3,13},{4,10},{5,11},{6,8},{7,9},{8,6},{9,7},... | collective-permute-start | bytes 897032 | tf_op jit(solution)/shard_map/ppermute | solution.py:392
  83.0 23.4 %collective-permute-start.11 = (bf16[1168,128]{1,0:T(8,128)(2,1)S(1)}, bf16[1168,128]{1,0:T(8,128)(2,1)S(1)}, u32[]{:S(2)}, u32[]{:S(2)}) collective-permute-start(bf16[1168,128]{1,0:T(8,128)(2,1)S(1)} %get-tuple-element.97), channel_id=1, source_target_pairs={{0,11},{1,10},{2,9},{3,8},{4,15},{5,14},{6,13},{7,12},{8,3},{9,2},... | collective-permute-start | bytes 897032 | tf_op jit(solution)/shard_map/ppermute | solution.py:392
  84.0 22.4 %collective-permute-start.12 = (bf16[1168,128]{1,0:T(8,128)(2,1)S(1)}, bf16[1168,128]{1,0:T(8,128)(2,1)S(1)}, u32[]{:S(2)}, u32[]{:S(2)}) collective-permute-start(bf16[1168,128]{1,0:T(8,128)(2,1)S(1)} %get-tuple-element.98), channel_id=1, source_target_pairs={{0,3},{1,2},{2,1},{3,0},{4,7},{5,6},{6,5},{7,4},{8,11},{9,10},{10,... | collective-permute-start | bytes 897032 | tf_op jit(solution)/shard_map/ppermute | solution.py:392
  88.2 21.8 %collective-permute-start.14 = (bf16[1168,128]{1,0:T(8,128)(2,1)S(1)}, bf16[1168,128]{1,0:T(8,128)(2,1)S(1)}, u32[]{:S(2)}, u32[]{:S(2)}) collective-permute-start(bf16[1168,128]{1,0:T(8,128)(2,1)S(1)} %get-tuple-element.100), channel_id=1, source_target_pairs={{0,15},{1,14},{2,13},{3,12},{4,11},{5,10},{6,9},{7,8},{8,7},{9,6},... | collective-permute-start | bytes 897032 | tf_op jit(solution)/shard_map/ppermute | solution.py:392
  90.4 18.1 %collective-permute-start.13 = (bf16[1168,128]{1,0:T(8,128)(2,1)S(1)}, bf16[1168,128]{1,0:T(8,128)(2,1)S(1)}, u32[]{:S(2)}, u32[]{:S(2)}) collective-permute-start(bf16[1168,128]{1,0:T(8,128)(2,1)S(1)} %get-tuple-element.99), channel_id=1, source_target_pairs={{0,1},{1,0},{2,3},{3,2},{4,5},{5,4},{6,7},{7,6},{8,9},{9,8},{10,11... | collective-permute-start | bytes 897032 | tf_op jit(solution)/shard_map/ppermute | solution.py:392
  108.5 17.3 %copy-start.2 = (s32[3,2048]{1,0:T(4,128)S(1)}, s32[3,2048]{1,0:T(4,128)}, u32[]{:S(2)}) copy-start(s32[3,2048]{1,0:T(4,128)} %get-tuple-element.60.where_ref) | copy-start | bytes 73732
